TPU v7x, 32 devices: a whole 2x2x4 slice. The times are simulated.
32 devices in a mesh: ctx: 8 (over z, x), head: 4 (over y, core).
Axes of the slice: x: 2, y: 2, z: 4, core: 2. Of those that a mesh axis runs over, the one named last changes fastest.
Arguments:
- queries: bfloat16 [1536, 1024], P(('ctx', 'head')), may hold values from -1.5 to 1.5, as said below
- key_inputs: bfloat16 [1536, 1024], P(('ctx', 'head')), may hold values from -1.5 to 1.5, as said below
- value_inputs: bfloat16 [1536, 1024], P(('ctx', 'head')), may hold values from -6 to 6
- out_grad: bfloat16 [1536, 1024], P(('ctx', 'head')), may hold values from -6 to 6
- attn_output: bfloat16 [1536, 1024], P(('ctx', 'head')), may hold values from -6 to 6
- gate_logits: bfloat16 [1536, 8], P(('ctx', 'head')), may hold values from 0 to 16
- lse: float32 [1536, 8], P(('ctx', 'head')), as said below
Outputs:
- query_grad: bfloat16 [1536, 1024], P(('ctx', 'head'))
- key_grad: bfloat16 [1536, 1024], P(('ctx', 'head'))
- value_grad: bfloat16 [1536, 1024], P(('ctx', 'head'))
- gate_grad: bfloat16 [1536, 8], P(('ctx', 'head'))
Inputs may be any that keep to these rules, and one draw needn't show every extreme that they name: `queries`: queries of every token. `key_inputs`: keys of every token. `lse`: the forward pass's log-sum-exp of each query's scores.
All inputs are finite; a program needn't handle non-finite values.
Results may differ from a plain program's by a relative error of at most 0.0052.
Values may be sent and summed in bfloat16 or wider, within the bound.
No kernel may reach another device: no remote copies, remote signals or barrier semaphores. Data moves between devices by JAX's collectives and lax.ppermute only.
A program may use at most 128 MiB of HBM per device.

v0:
```python
import math

import jax
import jax.numpy as jnp
from jax import lax
from jax.sharding import PartitionSpec as P


def prefix(value, axis, combine, identity, reverse):
    devices, here = (lax.axis_size(axis), lax.axis_index(axis))
    everything = lax.all_gather(value, axis)
    start = jnp.broadcast_to(jnp.asarray(identity, value.dtype), value.shape)

    def step(k, before):
        at = devices - 1 - k if reverse else k
        reached = at > here if reverse else at < here
        new = combine(before, everything[at])
        return jnp.where(reached, new, before)

    return lax.fori_loop(0, devices, step, start)


def block_scores(query_blk, key_blk, query_curve, key_curve, query_pos, key_pos, score_scale):
    product = jnp.einsum("qhd,khd->hqk", query_blk, key_blk, preferred_element_type=jnp.float32)
    scores = score_scale * product + query_curve.T[:, :, None] - key_curve.T[:, None, :]
    causal = key_pos[None, :] <= query_pos[:, None]
    return (scores, causal)


def attention_terms(
    query_blk,
    grad_blk,
    query_curve,
    query_lse,
    query_delta,
    query_pos,
    key_blk,
    value_blk,
    key_curve,
    key_pos,
    score_scale,
):
    scores, causal = block_scores(
        query_blk, key_blk, query_curve, key_curve, query_pos, key_pos, score_scale
    )
    probs = jnp.where(causal[None], jnp.exp(scores - query_lse[:, :, None]), 0.0)
    grad_probs = jnp.einsum("qhd,khd->hqk", grad_blk, value_blk, preferred_element_type=jnp.float32)
    score_grad = probs * (grad_probs - query_delta[:, :, None])
    return (probs, score_grad)


def fold_blocks(block_step, carry_in, pieces, useful):
    piece_len = pieces[0].shape[0]
    block_len = math.gcd(piece_len, 512)

    def one_turn(turn_index, carry_now):
        offset = turn_index * block_len
        sliced = tuple(
            (lax.dynamic_slice_in_dim(member, offset, block_len, 0) for member in pieces)
        )
        return lax.cond(
            useful(offset, block_len),
            lambda carry_arg: block_step(carry_arg, sliced, offset),
            lambda carry_arg: carry_arg,
            carry_now,
        )

    return lax.fori_loop(0, piece_len // block_len, one_turn, carry_in)


def per_device(queries, key_inputs, value_inputs, out_grad, attn_output, gate_logits, lse):
    my_query, my_keys, my_values, my_grad, my_output = (
        lax.all_to_all(queries, "head", split_axis=1, concat_axis=0, tiled=True),
        lax.all_to_all(key_inputs, "head", split_axis=1, concat_axis=0, tiled=True),
        lax.all_to_all(value_inputs, "head", split_axis=1, concat_axis=0, tiled=True),
        lax.all_to_all(out_grad, "head", split_axis=1, concat_axis=0, tiled=True),
        lax.all_to_all(attn_output, "head", split_axis=1, concat_axis=0, tiled=True),
    )
    gate_float, my_lse = (
        lax.all_to_all(
            gate_logits.astype(jnp.float32), "head", split_axis=1, concat_axis=0, tiled=True
        ),
        lax.all_to_all(lse, "head", split_axis=1, concat_axis=0, tiled=True),
    )
    row_count = my_query.shape[0]
    head_count = gate_float.shape[1]
    head_width = my_query.shape[1] // head_count
    score_scale = head_width ** (-0.5)
    dev_index = lax.axis_index("ctx")
    my_start = dev_index * row_count
    my_last = my_start + row_count - 1
    query_pos = my_start + jnp.arange(row_count, dtype=jnp.int32)
    query_three = my_query.reshape(row_count, head_count, head_width)
    key_three = my_keys.reshape(row_count, head_count, head_width)
    value_three = my_values.reshape(row_count, head_count, head_width)
    grad_three = my_grad.reshape(row_count, head_count, head_width)
    output_three = my_output.reshape(row_count, head_count, head_width)
    local_curve = jnp.cumsum(jax.nn.log_sigmoid(gate_float), axis=0)
    before = prefix(local_curve[-1], "ctx", jnp.add, jnp.zeros((head_count,), jnp.float32), False)
    source = local_curve + before[None, :]
    gathered = lax.all_gather(source, "ctx", axis=0, tiled=True)
    my_curve = lax.dynamic_slice_in_dim(gathered, my_start, row_count, 0)

    def keys_useful(start_row, block_len):
        return start_row <= my_last

    def queries_useful(start_row, block_len):
        return start_row + block_len - 1 >= my_start

    zero_stat = jnp.zeros((head_count, row_count), jnp.float32)
    zero_rows = jnp.zeros((row_count, head_count, head_width), jnp.float32)
    log_total = my_lse.T
    row_delta = jnp.sum(grad_three.astype(jnp.float32) * output_three.astype(jnp.float32), axis=2).T

    def add_query_side(carry_now, sliced, start_row):
        query_acc, row_acc = carry_now
        key_blk = sliced[0].reshape(-1, head_count, head_width)
        value_blk = sliced[1].reshape(-1, head_count, head_width)
        block_len = key_blk.shape[0]
        key_curve = lax.dynamic_slice_in_dim(gathered, start_row, block_len, 0)
        key_pos = start_row + jnp.arange(block_len, dtype=jnp.int32)
        probs, score_grad = attention_terms(
            query_three,
            grad_three,
            my_curve,
            log_total,
            row_delta,
            query_pos,
            key_blk,
            value_blk,
            key_curve,
            key_pos,
            score_scale,
        )
        query_acc = query_acc + jnp.einsum(
            "hqk,khd->qhd",
            score_grad.astype(jnp.bfloat16),
            key_blk,
            preferred_element_type=jnp.float32,
        )
        return (query_acc, row_acc + jnp.sum(score_grad, axis=2))

    query_acc, row_acc = fold_blocks(
        add_query_side,
        (zero_rows, zero_stat),
        (
            lax.all_gather(my_keys, "ctx", axis=0, tiled=True),
            lax.all_gather(my_values, "ctx", axis=0, tiled=True),
        ),
        keys_useful,
    )
    all_lse, all_delta = (
        lax.all_gather(my_lse, "ctx", axis=0, tiled=True),
        lax.all_gather(row_delta.T, "ctx", axis=0, tiled=True),
    )

    def add_key_side(carry_now, sliced, start_row):
        key_acc, value_acc, column_acc = carry_now
        query_blk = sliced[0].reshape(-1, head_count, head_width)
        grad_blk = sliced[1].reshape(-1, head_count, head_width)
        block_len = query_blk.shape[0]
        query_curve = lax.dynamic_slice_in_dim(gathered, start_row, block_len, 0)
        query_lse = lax.dynamic_slice_in_dim(all_lse, start_row, block_len, 0).T
        query_delta = lax.dynamic_slice_in_dim(all_delta, start_row, block_len, 0).T
        other_pos = start_row + jnp.arange(block_len, dtype=jnp.int32)
        probs, score_grad = attention_terms(
            query_blk,
            grad_blk,
            query_curve,
            query_lse,
            query_delta,
            other_pos,
            key_three,
            value_three,
            my_curve,
            query_pos,
            score_scale,
        )
        value_acc = value_acc + jnp.einsum(
            "hqk,qhd->khd", probs.astype(jnp.bfloat16), grad_blk, preferred_element_type=jnp.float32
        )
        key_acc = key_acc + jnp.einsum(
            "hqk,qhd->khd",
            score_grad.astype(jnp.bfloat16),
            query_blk,
            preferred_element_type=jnp.float32,
        )
        return (key_acc, value_acc, column_acc + jnp.sum(score_grad, axis=1))

    key_acc, value_acc, column_acc = fold_blocks(
        add_key_side,
        (zero_rows, zero_rows, zero_stat),
        (
            lax.all_gather(my_query, "ctx", axis=0, tiled=True),
            lax.all_gather(my_grad, "ctx", axis=0, tiled=True),
        ),
        queries_useful,
    )
    curve_grad = row_acc - column_acc
    local_rev = jnp.flip(jnp.cumsum(jnp.flip(curve_grad, 1), axis=1), 1)
    shard_total = jnp.sum(curve_grad, axis=1)
    after = prefix(shard_total, "ctx", jnp.add, jnp.zeros((head_count,), jnp.float32), True)
    gate_sum = local_rev + after[:, None]
    gate_grad = (gate_sum.T * jax.nn.sigmoid(-gate_float)).astype(jnp.bfloat16)
    query_grad = (
        (score_scale * query_acc).reshape(row_count, head_count * head_width).astype(jnp.bfloat16)
    )
    key_grad = (
        (score_scale * key_acc).reshape(row_count, head_count * head_width).astype(jnp.bfloat16)
    )
    value_grad = value_acc.reshape(row_count, head_count * head_width).astype(jnp.bfloat16)
    return (
        lax.all_to_all(query_grad, "head", split_axis=0, concat_axis=1, tiled=True),
        lax.all_to_all(key_grad, "head", split_axis=0, concat_axis=1, tiled=True),
        lax.all_to_all(value_grad, "head", split_axis=0, concat_axis=1, tiled=True),
        lax.all_to_all(gate_grad, "head", split_axis=0, concat_axis=1, tiled=True),
    )


def solution(mesh):
    placed = (
        P(("ctx", "head"), None),
        P(("ctx", "head"), None),
        P(("ctx", "head"), None),
        P(("ctx", "head"), None),
        P(("ctx", "head"), None),
        P(("ctx", "head"), None),
        P(("ctx", "head"), None),
    )
    return jax.shard_map(
        per_device,
        mesh=mesh,
        in_specs=placed,
        out_specs=(
            P(("ctx", "head"), None),
            P(("ctx", "head"), None),
            P(("ctx", "head"), None),
            P(("ctx", "head"), None),
        ),
        check_vma=False,
    )
```

profile of v0, /device:TPU:0, one launch (start us, length us, event | category | flops | bytes accessed | tf_op | source)
XLA Modules:
  0.0 330.8 jit_solution(912031704471712153)
XLA Ops:
  0.6 1.3 convert.3
  1.9 4.2 %all-to-all-start.2 = ((f32[48,4,2]{0,2,1:T(2,128)}), f32[48,4,2]{0,2,1:T(2,128)S(1)}, u32[]{:S(2)}, u32[]{:S(2)}) async-start(f32[48,4,2]{0,2,1:T(2,128)} %convert.3), calls=%async_computation.2 | async-start | bytes 8192 | tf_op jit(solution)/shard_map/all_to_all | solution.py:80
  6.1 1.6 copy.256
  7.7 0.6 copy.255
  8.4 0.3 copy-done.1
  8.6 0.6 copy.259
  9.6 0.6 copy.257
  10.2 0.3 copy-done.3
  10.5 0.6 copy.258
  11.2 0.7 copy-done.4
  11.8 0.6 dynamic-slice
  13.1 3.3 all-to-all-start.3
  16.6 0.6 reduce-window.14
  17.8 21.1 %all-gather.1 = f32[8,1,2]{2,1,0:T(1,128)S(1)} all-gather(f32[1,1,2]{2,1,0:T(1,128)S(1)} %bitcast.198), channel_id=1, replica_groups=mesh['ctx'=8,'head'=4] {'ctx'}, dimensions={0}, use_global_device_ids=true | all-gather | bytes 72 | tf_op jit(solution)/shard_map/all_gather | solution.py:11
  39.0 0.3 while.70
  39.3 3.3 %all-to-all-start.5 = ((bf16[48,4,256]{2,0,1:T(8,128)(2,1)}), bf16[48,4,256]{2,0,1:T(8,128)(2,1)S(1)}, u32[]{:S(2)}, u32[]{:S(2)}) async-start(bf16[48,4,256]{2,0,1:T(8,128)(2,1)} %bitcast.143), calls=%async_computation.5 | async-start | bytes 196608 | tf_op jit(solution)/shard_map/all_to_all | solution.py:76
  42.8 26.0 %all-gather.2 = f32[8,192,2]{1,2,0:T(2,128)S(1)} all-gather(f32[1,192,2]{1,2,0:T(2,128)S(1)} %fusion.26), channel_id=1, replica_groups=mesh['ctx'=8,'head'=4] {'ctx'}, dimensions={0}, use_global_device_ids=true | all-gather | bytes 13824 | tf_op jit(solution)/shard_map/all_gather | solution.py:101
  68.9 26.0 %all-gather.3 = f32[8,192,2]{1,2,0:T(2,128)S(1)} all-gather(f32[1,192,2]{1,2,0:T(2,128)S(1)} %reshape.213), channel_id=1, replica_groups=mesh['ctx'=8,'head'=4] {'ctx'}, dimensions={0}, use_global_device_ids=true | all-gather | bytes 13824 | tf_op jit(solution)/shard_map/all_gather | solution.py:153
  95.1 3.3 %all-to-all-start = ((bf16[48,4,256]{2,0,1:T(8,128)(2,1)}), bf16[48,4,256]{2,0,1:T(8,128)(2,1)S(1)}, u32[]{:S(2)}, u32[]{:S(2)}) async-start(bf16[48,4,256]{2,0,1:T(8,128)(2,1)} %bitcast.146), calls=%async_computation | async-start | bytes 196608 | tf_op jit(solution)/shard_map/all_to_all | solution.py:74
  98.5 4.2 %all-to-all-done = bf16[48,4,256]{2,0,1:T(8,128)(2,1)S(1)} async-done(((bf16[48,4,256]{2,0,1:T(8,128)(2,1)}), bf16[48,4,256]{2,0,1:T(8,128)(2,1)S(1)}, u32[]{:S(2)}, u32[]{:S(2)}) %all-to-all-start) | async-done | bytes 98336 | tf_op jit(solution)/shard_map/all_to_all | solution.py:74
  102.7 3.3 all-to-all-start.6
  106.0 32.2 %all_gather.30 = bf16[1536,256]{1,0:T(8,128)(2,1)S(1)} all-gather(bf16[192,256]{1,0:T(8,128)(2,1)S(1)} %bitcast.166), channel_id=1, replica_groups=mesh['ctx'=8,'head'=4] {'ctx'}, dimensions={0}, use_global_device_ids=true | all-gather | bytes 884736 | tf_op jit(solution)/shard_map/all_gather | solution.py:147
  138.2 3.3 all-to-all-start.4
  141.7 4.1 %all-to-all-done.4 = bf16[48,4,256]{2,0,1:T(8,128)(2,1)S(1)} async-done(((bf16[48,4,256]{2,0,1:T(8,128)(2,1)}), bf16[48,4,256]{2,0,1:T(8,128)(2,1)S(1)}, u32[]{:S(2)}, u32[]{:S(2)}) %all-to-all-start.4) | async-done | bytes 98336 | tf_op jit(solution)/shard_map/all_to_all | solution.py:75
  145.7 3.3 all-to-all-start.1
  149.1 32.2 %all_gather.33 = bf16[1536,256]{1,0:T(8,128)(2,1)S(1)} all-gather(bf16[192,256]{1,0:T(8,128)(2,1)S(1)} %bitcast.168), channel_id=1, replica_groups=mesh['ctx'=8,'head'=4] {'ctx'}, dimensions={0}, use_global_device_ids=true | all-gather | bytes 884736 | tf_op jit(solution)/shard_map/all_gather | solution.py:148
  181.2 0.3 multiply_reduce_fusion
  181.6 0.3 copy.209
  182.3 1.4 while.69
  182.3 1.3 conditional.7
  182.5 0.4 fusion.11
  182.9 0.4 fusion.29
  183.8 26.0 %all-gather.4 = f32[8,192,2]{1,2,0:T(2,128)S(1)} all-gather(f32[1,192,2]{1,2,0:T(2,128)S(1)} %copy.218), channel_id=1, replica_groups=mesh['ctx'=8,'head'=4] {'ctx'}, dimensions={0}, use_global_device_ids=true | all-gather | bytes 13824 | tf_op jit(solution)/shard_map/all_gather | solution.py:154
  209.9 32.3 %all_gather.34 = bf16[1536,256]{1,0:T(8,128)(2,1)S(1)} all-gather(bf16[192,256]{1,0:T(8,128)(2,1)S(1)} %bitcast.171), channel_id=1, replica_groups=mesh['ctx'=8,'head'=4] {'ctx'}, dimensions={0}, use_global_device_ids=true | all-gather | bytes 884736 | tf_op jit(solution)/shard_map/all_gather | solution.py:194
  242.5 32.0 %all_gather.36 = bf16[1536,256]{1,0:T(8,128)(2,1)S(1)} all-gather(bf16[192,256]{1,0:T(8,128)(2,1)S(1)} %bitcast.165), channel_id=1, replica_groups=mesh['ctx'=8,'head'=4] {'ctx'}, dimensions={0}, use_global_device_ids=true | all-gather | bytes 884736 | tf_op jit(solution)/shard_map/all_gather | solution.py:195
  274.9 4.9 %while.72 = (s32[]{:T(128)}, f32[192,2,128]{2,0,1:T(8,128)S(1)}, f32[192,2,128]{2,0,1:T(8,128)S(1)}, f32[2,192]{1,0:T(2,128)S(1)}, s32[]{:T(128)}, /*index=5*/bf...) while((s32[]{:T(128)}, f32[192,2,128]{2,0,1:T(8,128)S(1)}, ...), condition=%wide.region_14.15_spmd.clone.clone, body=%wide.region_10.14_spmd.clone.clone.sunk | while | flops 203489984 | bytes 6474649 | solution.py:68
  275.0 1.6 conditional.8
  275.2 0.4 fusion.19
  275.9 0.4 fusion.30
  276.6 1.6 conditional.8
  276.9 0.4 fusion.19
  277.5 0.4 fusion.30
  278.2 1.6 conditional.8
  278.5 0.4 fusion.19
  279.1 0.4 fusion.30
  280.2 0.6 reduce-window.16
  281.6 17.1 %all-reduce.2 = f32[16]{0:T(128)S(1)} all-reduce(f32[16]{0:T(128)S(1)} %dynamic-update-slice), channel_id=2, replica_groups=mesh['ctx'=8,'head'=4] {'ctx'}, use_global_device_ids=true, to_apply=%add.2 | all-reduce | flops 16 | bytes 128
  298.8 0.3 while.71
  299.4 0.6 copy.229
  299.9 3.2 all-to-all-start.10
  303.3 0.7 convert_element_type.80
  304.0 2.8 all-to-all-done.10
  306.8 3.3 all-to-all-start.7
  310.3 0.7 convert_element_type.82
  311.0 3.4 %all-to-all-done.7 = bf16[4,48,256]{2,1,0:T(8,128)(2,1)S(1)} async-done(((bf16[4,48,256]{2,1,0:T(8,128)(2,1)}), bf16[4,48,256]{2,1,0:T(8,128)(2,1)S(1)}, u32[]{:S(2)}, u32[]{:S(2)}) %all-to-all-start.7) | async-done | bytes 98336 | tf_op jit(solution)/shard_map/all_to_all | solution.py:213
  314.4 3.3 all-to-all-start.8
  317.8 0.7 convert_element_type.84
  318.5 3.4 %all-to-all-done.8 = bf16[4,48,256]{2,1,0:T(8,128)(2,1)S(1)} async-done(((bf16[4,48,256]{2,1,0:T(8,128)(2,1)}), bf16[4,48,256]{2,1,0:T(8,128)(2,1)S(1)}, u32[]{:S(2)}, u32[]{:S(2)}) %all-to-all-start.8) | async-done | bytes 98336 | tf_op jit(solution)/shard_map/all_to_all | solution.py:214
  322.0 3.3 all-to-all-start.9
  325.3 0.6 copy.243
  325.9 0.6 copy.244
  326.6 3.0 all-to-all-done.9
  329.5 0.6 copy.245
  330.2 0.6 copy.313
  (137 shorter events, 7.9 us)
Async XLA Ops:
  1.9 11.2 %all-to-all-start.2 = ((f32[48,4,2]{0,2,1:T(2,128)}), f32[48,4,2]{0,2,1:T(2,128)S(1)}, u32[]{:S(2)}, u32[]{:S(2)}) async-start(f32[48,4,2]{0,2,1:T(2,128)} %convert.3), calls=%async_computation.2 | async-start | bytes 8192 | tf_op jit(solution)/shard_map/all_to_all | solution.py:80
  6.1 1.6 copy-start
  7.7 0.9 copy-start.1
  8.6 0.9 copy-start.2
  9.6 0.9 copy-start.3
  11.2 0.7 copy-start.4
  13.1 26.1 %all-to-all-start.3 = ((f32[48,4,2]{0,2,1:T(2,128)}), f32[48,4,2]{0,2,1:T(2,128)S(1)}, u32[]{:S(2)}, u32[]{:S(2)}) async-start(f32[48,4,2]{0,2,1:T(2,128)} %bitcast.24), calls=%async_computation.3 | async-start | bytes 8192 | tf_op jit(solution)/shard_map/all_to_all | solution.py:83
  39.3 55.8 %all-to-all-start.5 = ((bf16[48,4,256]{2,0,1:T(8,128)(2,1)}), bf16[48,4,256]{2,0,1:T(8,128)(2,1)S(1)}, u32[]{:S(2)}, u32[]{:S(2)}) async-start(bf16[48,4,256]{2,0,1:T(8,128)(2,1)} %bitcast.143), calls=%async_computation.5 | async-start | bytes 196608 | tf_op jit(solution)/shard_map/all_to_all | solution.py:76
  95.1 7.6 %all-to-all-start = ((bf16[48,4,256]{2,0,1:T(8,128)(2,1)}), bf16[48,4,256]{2,0,1:T(8,128)(2,1)S(1)}, u32[]{:S(2)}, u32[]{:S(2)}) async-start(bf16[48,4,256]{2,0,1:T(8,128)(2,1)} %bitcast.146), calls=%async_computation | async-start | bytes 196608 | tf_op jit(solution)/shard_map/all_to_all | solution.py:74
  102.7 35.5 %all-to-all-start.6 = ((bf16[48,4,256]{2,0,1:T(8,128)(2,1)}), bf16[48,4,256]{2,0,1:T(8,128)(2,1)S(1)}, u32[]{:S(2)}, u32[]{:S(2)}) async-start(bf16[48,4,256]{2,0,1:T(8,128)(2,1)} %bitcast.142), calls=%async_computation.6 | async-start | bytes 196608 | tf_op jit(solution)/shard_map/all_to_all | solution.py:77
  138.2 7.6 %all-to-all-start.4 = ((bf16[48,4,256]{2,0,1:T(8,128)(2,1)}), bf16[48,4,256]{2,0,1:T(8,128)(2,1)S(1)}, u32[]{:S(2)}, u32[]{:S(2)}) async-start(bf16[48,4,256]{2,0,1:T(8,128)(2,1)} %bitcast.144), calls=%async_computation.4 | async-start | bytes 196608 | tf_op jit(solution)/shard_map/all_to_all | solution.py:75
  145.7 36.4 %all-to-all-start.1 = ((bf16[48,4,256]{2,0,1:T(8,128)(2,1)}), bf16[48,4,256]{2,0,1:T(8,128)(2,1)S(1)}, u32[]{:S(2)}, u32[]{:S(2)}) async-start(bf16[48,4,256]{2,0,1:T(8,128)(2,1)} %bitcast.145), calls=%async_computation.1 | async-start | bytes 196608 | tf_op jit(solution)/shard_map/all_to_all | solution.py:73
  299.9 6.9 %all-to-all-start.10 = ((bf16[4,48,2]{1,2,0:T(2,128)(2,1)}), bf16[4,48,2]{1,2,0:T(2,128)(2,1)S(1)}, u32[]{:S(2)}, u32[]{:S(2)}) async-start(bf16[4,48,2]{1,2,0:T(2,128)(2,1)} %copy.229), calls=%async_computation.10 | async-start | bytes 4096 | tf_op jit(solution)/shard_map/all_to_all | solution.py:216
  306.8 7.6 %all-to-all-start.7 = ((bf16[4,48,256]{2,1,0:T(8,128)(2,1)}), bf16[4,48,256]{2,1,0:T(8,128)(2,1)S(1)}, u32[]{:S(2)}, u32[]{:S(2)}) async-start(bf16[4,48,256]{2,1,0:T(8,128)(2,1)} %convert_element_type.80), calls=%async_computation.7 | async-start | bytes 196608 | tf_op jit(solution)/shard_map/all_to_all | solution.py:213
  314.4 7.6 %all-to-all-start.8 = ((bf16[4,48,256]{2,1,0:T(8,128)(2,1)}), bf16[4,48,256]{2,1,0:T(8,128)(2,1)S(1)}, u32[]{:S(2)}, u32[]{:S(2)}) async-start(bf16[4,48,256]{2,1,0:T(8,128)(2,1)} %convert_element_type.82), calls=%async_computation.8 | async-start | bytes 196608 | tf_op jit(solution)/shard_map/all_to_all | solution.py:214
  322.0 7.6 %all-to-all-start.9 = ((bf16[4,48,256]{2,1,0:T(8,128)(2,1)}), bf16[4,48,256]{2,1,0:T(8,128)(2,1)S(1)}, u32[]{:S(2)}, u32[]{:S(2)}) async-start(bf16[4,48,256]{2,1,0:T(8,128)(2,1)} %convert_element_type.84), calls=%async_computation.9 | async-start | bytes 196608 | tf_op jit(solution)/shard_map/all_to_all | solution.py:215
where the time goes:
time: 332 us; the launch traced here: 331 us
  blocking collectives  245 us (74%)
  starting transfers between devices  37.2 us (11%)
  waiting for transfers between devices  20.8 us (6%)
  local copies, waits for them, and re-layouts  15.8 us (5%)
  matrix products  4.86 us (1%)
  other arithmetic  4.5 us (1%)
    all_gather x1, blocking collectives, per_device(): lax.all_gather(my_query, 'ctx', axis=0, tiled=True)  32.3 us
    all_gather x1, blocking collectives, per_device(): lax.all_gather(my_values, 'ctx', axis=0, tiled=True)  32.2 us
    all_gather x1, blocking collectives, per_device(): lax.all_gather(my_keys, 'ctx', axis=0, tiled=True)  32.2 us
    all_gather x1, blocking collectives, per_device(): lax.all_gather(my_grad, 'ctx', axis=0, tiled=True)  32 us
    all_gather x1, blocking collectives, per_device(): lax.all_gather(row_delta.T, 'ctx', axis=0, tiled=True)  26 us
    all_gather x1, blocking collectives, per_device(): gathered = lax.all_gather(source, 'ctx', axis=0, tiled=True)  26 us
    all_gather x1, blocking collectives, per_device(): lax.all_gather(my_lse, 'ctx', axis=0, tiled=True)  26 us
    all_gather x1, blocking collectives, prefix(): everything = lax.all_gather(value, axis)  21.1 us
  transfers between devices with their start and end apart: 11, of which 6 were waited for; matrix products, arithmetic and copies ran while one was open for 4% of the time, Pallas kernels for 0%

commit v1 on v0

v1 whole, which is shorter than its diff:
```python
import functools
import math

import jax
import jax.numpy as jnp
from jax import lax
from jax.experimental import pallas as pl
from jax.experimental.pallas import tpu as pltpu
from jax.sharding import PartitionSpec as P

BF16 = jnp.bfloat16
F32 = jnp.float32
LANES = 128
STAT = 16
EXACT = lax.Precision.HIGHEST
VMEM = pl.BlockSpec(memory_space=pltpu.VMEM)
SMEM = pl.BlockSpec(memory_space=pltpu.SMEM)
HBM = pl.BlockSpec(memory_space=pltpu.HBM)


def iota(shape, dim):
    return lax.broadcasted_iota(jnp.int32, shape, dim)


def dot_exact(a, b):
    return jnp.dot(a, b, precision=EXACT, preferred_element_type=F32)


def split3(x):
    hi = x.astype(BF16).astype(F32)
    rest = x - hi
    mid = rest.astype(BF16).astype(F32)
    low = (rest - mid).astype(BF16).astype(F32)
    return hi, mid, low


def stack_rows(rows):
    at = iota((STAT, LANES), 0)
    block = jnp.zeros((STAT, LANES), F32)
    for j, row in enumerate(rows):
        block = jnp.where(at == j, jnp.broadcast_to(row, (STAT, LANES)), block)
    return block


def pad_rows(x):
    missing = LANES - x.shape[0]
    if missing:
        x = jnp.concatenate([x, jnp.zeros((missing, x.shape[1]), x.dtype)], axis=0)
    return x


def wrap(x, n):
    x = jnp.where(x < 0, x + n, x)
    return jnp.where(x >= n, x - n, x)


def block_positions(ids, shape, dim, heads, stride, first, sources):
    index = iota(shape, dim)
    pos = jnp.full(shape, -1, jnp.int32)
    for at, src in enumerate(sources):
        begin = first + at * heads
        here = (index >= begin) & (index < begin + heads)
        place = wrap(ids[0] - (index - begin), heads)
        pos = jnp.where(here, ids[1 + src] + place * stride, pos)
    return pos


def pack_kernel(ids, *refs):
    sources, refs = (refs[:7], refs[7:])
    heads, rows = sources[5].shape
    query_out, key_out = (refs[:heads], refs[heads : 2 * heads])
    *held, gate_wide, lse_wide, sems = refs[2 * heads :]
    copies = [pltpu.make_async_copy(src, dst, sems.at[i]) for i, (src, dst) in enumerate(zip(sources, held))]
    for i in (5, 6, 3, 4, 0, 1, 2):
        copies[i].start()
    q_ref, k_ref, v_ref, g_ref, o_ref, gate_ref, lse_ref = held
    copies[5].wait()
    copies[6].wait()
    gate_wide[...] = jnp.zeros_like(gate_wide)
    lse_wide[...] = jnp.zeros_like(lse_wide)
    gate_wide[:, 0:rows] = gate_ref[...].astype(F32)
    lse_wide[:, 0:rows] = lse_ref[...]
    copies[3].wait()
    copies[4].wait()

    columns = [pl.ds(pl.multiple_of(wrap(ids[0] + k, heads) * LANES, LANES), LANES) for k in range(heads)]
    lane = iota((rows, LANES), 1)
    delta = jnp.zeros((rows, LANES), F32)
    for k in range(heads):
        grad = g_ref[:, columns[k]]
        row_sum = jnp.sum(grad.astype(F32) * o_ref[:, columns[k]].astype(F32), axis=1, keepdims=True)
        delta = jnp.where(lane == k, row_sum, delta)
        query_out[k][rows : 2 * rows, :] = grad
    delta = split3(pad_rows(delta).T)
    for k in range(heads):
        at = pl.ds(wrap(ids[0] + k, heads), 1)
        parts = [gate_wide[at, :], *split3(lse_wide[at, :]), *[part[k : k + 1] for part in delta]]
        query_out[k][2 * rows :, :] = stack_rows(parts).astype(BF16)
    copies[0].wait()
    for k in range(heads):
        query_out[k][0:rows, :] = q_ref[:, columns[k]]
    copies[1].wait()
    copies[2].wait()
    for k in range(heads):
        key_out[k][0:rows, :] = k_ref[:, columns[k]]
        key_out[k][rows:, :] = v_ref[:, columns[k]]


def join_kernel(*refs):
    outs = [ref for ref in refs if len(ref.shape) == 3]
    chunks = [ref for ref in refs if len(ref.shape) == 2]
    for k, chunk in enumerate(chunks):
        begin = 0
        for out in outs:
            out[k] = chunk[begin : begin + out.shape[1], :]
            begin += out.shape[1]


def stat_kernel(plan, ids, *refs):
    rows, heads, across, down, stride, scale = plan
    count = across * down
    stat_refs = refs[:count]
    score_ref, delta_ref, keep_ref = refs[count:]

    def row_of(src, j):
        block = stat_refs[src][...].astype(F32)
        return jnp.concatenate([block[k, j : j + 1, :] for k in range(heads)], axis=0)

    gates = [row_of(src, 0) for src in range(count)]
    valid = iota((heads, LANES), 1) < rows
    logs = [
        jnp.where(valid, jnp.minimum(x, 0.0) - jnp.log1p(jnp.exp(-jnp.abs(x))), 0.0) for x in gates
    ]
    logs = jnp.concatenate(logs, axis=0)
    blocks = count * heads
    square = (LANES, LANES)
    upto = (iota(square, 0) <= iota(square, 1)).astype(F32)
    order = range(count)
    earlier = block_positions(ids, (blocks, blocks), 1, heads, stride, 0, order) < block_positions(
        ids, (blocks, blocks), 0, heads, stride, 0, order
    )
    before = jnp.sum(dot_exact(earlier.astype(F32), logs), axis=1, keepdims=True)
    curve = dot_exact(logs, upto) + before

    def curve_of(src):
        return curve[src * heads : (src + 1) * heads]

    zero = jnp.zeros((heads, LANES), F32)
    for m in range(score_ref.shape[0]):
        q_rows, d_rows, k_rows = [], [], []
        for s in (2 * m, 2 * m + 1):
            if s < down:
                src = s * across
                lse = row_of(src, 1) + row_of(src, 2) + row_of(src, 3)
                q_rows += [*split3((curve_of(src) - lse) / scale), zero]
                d_rows += [-row_of(src, 4), -row_of(src, 5), -row_of(src, 6), zero]
            else:
                q_rows += [zero] * 4
                d_rows += [zero] * 4
            k_rows += [*split3(-curve_of(s) / scale), zero] if s < across else [zero] * 4
        score_ref[m] = jnp.concatenate(q_rows + k_rows, axis=0).T[:rows]
        delta_ref[m] = pad_rows(jnp.concatenate(d_rows, axis=0)).T[:rows]
    keep_ref[...] = 1.0 / (1.0 + jnp.exp(gates[0]))


def attention_kernel(plan, ids, *refs):
    rows, heads, across, down, stride, scale, static_order = plan
    q_src, refs = (refs[:down], refs[down:])
    k_src, refs = (refs[:across], refs[across:])
    score_ref, delta_ref, refs = (refs[0], refs[1], refs[2:])
    dq_own, dk_own, dv_own, sums_ref, refs = (*refs[:4], refs[4:])
    to_down, refs = (refs[: down - 1], refs[down - 1 :])
    to_across, refs = (refs[: across - 1], refs[across - 1 :])
    qe, ge, ke, ve, dq_acc, dk_acc, dv_acc = refs

    lane = iota((rows, LANES), 1)
    half = 8 * heads
    upper = (lane >= half).astype(F32)
    lower = (lane < half).astype(F32)
    ones = jnp.ones((rows, LANES), BF16)

    def slot(s, k, start):
        inner = lane - start - (s % 2) * 4 * heads
        return (inner >= 0) & (inner < 4 * heads) & (lane % heads == k)

    def rows_at(k, s, sources):
        begin = (wrap(ids[0] - k, heads) * sources + s) * rows
        return pl.ds(pl.multiple_of(begin, math.gcd(rows, 128)), rows)

    for k in range(heads):
        for s in range(down):
            at = rows_at(k, s, down)
            mine = slot(s, k, 0)
            qe[at, 0:LANES] = q_src[s][k, 0:rows, :]
            qe[at, LANES:] = jnp.where(mine, score_ref[s // 2], upper).astype(BF16)
            ge[at, 0:LANES] = q_src[s][k, rows : 2 * rows, :]
            ge[at, LANES:] = jnp.where(mine, delta_ref[s // 2], 0.0).astype(BF16)
        for s in range(across):
            at = rows_at(k, s, across)
            mine = slot(s, k, half)
            ke[at, 0:LANES] = k_src[s][k, 0:rows, :]
            ke[at, LANES:] = jnp.where(mine, score_ref[s // 2], lower).astype(BF16)
            ve[at, 0:LANES] = k_src[s][k, rows : 2 * rows, :]
            ve[at, LANES:] = ones

    pair = 2
    wide, tall = (pair * down * rows, pair * across * rows)
    step = pair * stride * rows

    def token_pos(shape, dim, sources):
        index = iota(shape, dim)
        pos = jnp.zeros(shape, jnp.int32)
        for c in range(pair):
            for s, src in enumerate(sources):
                first = (c * len(sources) + s) * rows
                here = (index >= first) & (index < first + rows)
                pos = jnp.where(here, (ids[1 + src] + c * stride) * rows + index - first, pos)
        return pos

    ahead = token_pos((1, wide), 1, range(0, down * across, across)) - token_pos(
        (tall, 1), 0, range(across)
    )
    factor = scale * math.log2(math.e)
    nt = (((1,), (1,)), ((), ()))
    tn = (((0,), (0,)), ((), ()))

    def tile(col_at, row_at, allowed):
        q_part, g_part = (qe[row_at, :], ge[row_at, :])
        k_part, v_part = (ke[col_at, :], ve[col_at, :])
        scores = lax.dot_general(k_part, q_part, nt, preferred_element_type=F32)
        shifted = lax.dot_general(v_part, g_part, nt, preferred_element_type=F32)
        probs = jnp.exp2(scores * factor)
        if allowed is not None:
            probs = jnp.where(allowed, probs, 0.0)
        grads = (probs * shifted).astype(BF16)
        probs = probs.astype(BF16)
        dv = jnp.dot(probs, g_part[:, 0:LANES], preferred_element_type=F32)
        dk = jnp.dot(grads, q_part, preferred_element_type=F32)
        dq = lax.dot_general(grads, k_part, tn, preferred_element_type=F32)
        return dq, dk, dv

    groups = heads // pair
    if static_order:
        for kc in range(groups):
            col_at = pl.ds(kc * tall, tall)
            diag_at = pl.ds(kc * wide, wide)
            dq, dk, dv = tile(col_at, diag_at, ahead >= 0)
            dq_acc[diag_at, :] = dq if kc == 0 else dq_acc[diag_at, :] + dq
            if kc + 1 < groups:
                rest_at = pl.ds((kc + 1) * wide, (groups - 1 - kc) * wide)
                dq, dk2, dv2 = tile(col_at, rest_at, None)
                dq_acc[rest_at, :] = dq if kc == 0 else dq_acc[rest_at, :] + dq
                dk, dv = (dk + dk2, dv + dv2)
            dk_acc[col_at, :] = dk
            dv_acc[col_at, :] = dv
    else:
        dq_acc[...] = jnp.zeros_like(dq_acc)
        dk_acc[...] = jnp.zeros_like(dk_acc)
        dv_acc[...] = jnp.zeros_like(dv_acc)

        @pl.loop(0, groups)
        def _(kc):
            @pl.loop(0, groups)
            def _(kr):
                col_at = pl.ds(pl.multiple_of(kc * tall, tall), tall)
                row_at = pl.ds(pl.multiple_of(kr * wide, wide), wide)
                dq, dk, dv = tile(col_at, row_at, ahead >= (kc - kr) * step)
                dq_acc[row_at, :] += dq
                dk_acc[col_at, :] += dk
                dv_acc[col_at, :] += dv

    sums = jnp.zeros((rows, LANES), F32)
    for k in range(heads):
        for s in range(down):
            at = rows_at(k, s, down)
            dq = dq_acc[at, 0:LANES]
            sums = jnp.where(lane == s * heads + k, dq_acc[at, LANES:], sums)
            if s == 0:
                dq_own[k] = dq
            else:
                to_down[s - 1][k] = dq.astype(BF16)
        for s in range(across):
            at = rows_at(k, s, across)
            dk, dv = (dk_acc[at, 0:LANES], dv_acc[at, :])
            sums = jnp.where(lane == half + s * heads + k, -dk_acc[at, LANES:], sums)
            if s == 0:
                dk_own[k] = dk
                dv_own[k] = dv
            else:
                to_across[s - 1][k, 0:rows, :] = dk.astype(BF16)
                to_across[s - 1][k, rows:, :] = dv.astype(BF16)
    sums_ref[...] = sums


def suffix_kernel(plan, ids, sums_ref, own_ref, *others):
    rows, heads, across, down, stride = plan
    count = across * down
    blocks = count * heads
    square = (LANES, LANES)
    turned = pad_rows(sums_ref[...]).T
    onward = (iota(square, 0) >= iota(square, 1)).astype(F32)
    shape = (blocks, LANES)
    slot_pos = jnp.maximum(
        block_positions(ids, shape, 1, heads, stride, 0, range(0, count, across)),
        block_positions(ids, shape, 1, heads, stride, 8 * heads, range(across)),
    )
    target_pos = block_positions(ids, shape, 0, heads, stride, 0, range(count))
    later = dot_exact((slot_pos > target_pos).astype(F32), turned)
    inner = dot_exact((slot_pos == target_pos).astype(F32), turned)
    suffix = jnp.sum(later, axis=1, keepdims=True) + dot_exact(inner, onward)
    own_ref[...] = suffix[0:heads]
    for src in range(1, count):
        parts = split3(suffix[src * heads : (src + 1) * heads])
        for k in range(heads):
            others[src - 1][k] = stack_rows([part[k : k + 1] for part in parts]).astype(BF16)


def combine_keys_kernel(scale, dk_ref, dv_ref, *refs):
    heads, rows, _ = dk_ref.shape
    outs, received = (refs[-heads:], refs[:-heads])
    for k in range(heads):
        dk, dv = (dk_ref[k], dv_ref[k])
        for ref in received:
            dk += ref[k, 0:rows, :].astype(F32)
            dv += ref[k, rows:, :].astype(F32)
        outs[k][0:rows, :] = (scale * dk).astype(BF16)
        outs[k][rows:, :] = dv.astype(BF16)


def combine_queries_kernel(scale, down, dq_ref, gate_ref, keep_ref, *refs):
    heads, rows, _ = dq_ref.shape
    outs, received = (refs[-heads:], refs[:-heads])
    for k in range(heads):
        dq = dq_ref[k]
        for ref in received[: down - 1]:
            dq += ref[k].astype(F32)
        total = gate_ref[k : k + 1, :]
        extra = jnp.zeros((STAT, LANES), F32)
        for ref in received[down - 1 :]:
            extra += ref[k].astype(F32)
        gate = (total + jnp.sum(extra, axis=0, keepdims=True)) * keep_ref[k : k + 1, :]
        outs[k][0:rows, :] = (scale * dq).astype(BF16)
        outs[k][rows:, :] = jnp.broadcast_to(gate, (STAT, LANES)).astype(BF16)


def unpack_kernel(ids, *refs):
    heads = (len(refs) - 4) // 2
    queries, keys = (refs[:heads], refs[heads : 2 * heads])
    dq_ref, dk_ref, dv_ref, gate_ref = refs[2 * heads :]
    rows = dq_ref.shape[0]
    at = iota((heads, LANES), 0)
    gates = jnp.zeros((heads, LANES), F32)
    for k in range(heads):
        head = wrap(ids[0] + k, heads)
        cols = pl.ds(pl.multiple_of(head * LANES, LANES), LANES)
        dq_ref[:, cols] = queries[k][0:rows, :]
        dk_ref[:, cols] = keys[k][0:rows, :]
        dv_ref[:, cols] = keys[k][rows:, :]
        row = queries[k][rows:, :].astype(F32)[0:1]
        gates = jnp.where(at == head, jnp.broadcast_to(row, (heads, LANES)), gates)
    gate_ref[...] = gates[:, 0:rows].astype(BF16)


def struct(shape, dtype=BF16):
    return jax.ShapeDtypeStruct(shape, dtype)


def call(kernel, out_shape, inputs, scratch=(), smem=0, space=VMEM):
    return pl.pallas_call(
        kernel,
        out_shape=out_shape,
        in_specs=[SMEM] * smem + [space] * (len(inputs) - smem),
        out_specs=jax.tree.map(lambda _: VMEM, out_shape),
        scratch_shapes=list(scratch),
        compiler_params=pltpu.CompilerParams(vmem_limit_bytes=40 * 1024 * 1024),
    )(*inputs)


def per_device(queries, key_inputs, value_inputs, out_grad, attn_output, gate_logits, lse):
    ctx, group = (lax.axis_size("ctx"), lax.axis_size("head"))
    rows, heads = gate_logits.shape
    width = queries.shape[1]
    scale = (width // heads) ** -0.5
    sub = ctx // heads
    count = sub * group
    across = max(d for d in range(1, count + 1) if count % d == 0 and d * d <= count)
    down = count // across
    both = ("ctx", "head")

    def device_of(head, p):
        return ((p // group) * heads + head) * group + p % group

    def shift(array, sb, sa):
        pairs = []
        for head in range(heads):
            for b in range(down):
                for a in range(across):
                    source = ((b + sb) % down) * across + (a + sa) % across
                    pairs.append((device_of(head, source), device_of(head, b * across + a)))
        return lax.ppermute(array, both, pairs)

    def turn(chunks, sign):
        moved = [chunks[0]]
        for k in range(1, heads):
            pairs = [
                (device_of(head, p), device_of((head + sign * k) % heads, p))
                for head in range(heads)
                for p in range(count)
            ]
            moved.append(lax.ppermute(chunks[k], both, pairs))
        return moved

    here = lax.axis_index("ctx")
    member = (here // heads) * group + lax.axis_index("head")
    my_b, my_a = (member // across, member % across)
    ids = [here % heads]
    for sb in range(down):
        for sa in range(across):
            p = ((my_b + sb) % down) * across + (my_a + sa) % across
            ids.append((p // group) * heads * group + p % group)
    ids = jnp.stack(ids).astype(jnp.int32)
    members = [(sb, sa) for sb in range(down) for sa in range(across)]

    chunks = call(
        pack_kernel,
        [struct((2 * rows + STAT, LANES))] * heads + [struct((2 * rows, LANES))] * heads,
        (ids, queries, key_inputs, value_inputs, out_grad, attn_output, gate_logits.T, lse.T),
        scratch=[pltpu.VMEM((rows, width), BF16)] * 5
        + [pltpu.VMEM((heads, rows), BF16), pltpu.VMEM((heads, rows), F32)]
        + [pltpu.VMEM((heads, LANES), F32)] * 2
        + [pltpu.SemaphoreType.DMA((7,))],
        smem=1,
        space=HBM,
    )
    query_chunks = turn(chunks[:heads], 1)
    key_chunks = turn(chunks[heads:], 1)
    pieces = struct((heads, 2 * rows, LANES))
    query_own, stat_own = call(join_kernel, [pieces, struct((heads, STAT, LANES))], query_chunks)
    stat_all = [stat_own if m == (0, 0) else shift(stat_own, *m) for m in members]
    query_all = [query_own] + [shift(query_own, sb, 0) for sb in range(1, down)]
    (key_own,) = call(join_kernel, [pieces], key_chunks)
    key_all = [key_own] + [shift(key_own, 0, sa) for sa in range(1, across)]

    chunk_count = -(-max(across, down) // 2)
    extras = struct((chunk_count, rows, LANES), F32)
    score_cols, delta_cols, keep = call(
        functools.partial(stat_kernel, (rows, heads, across, down, group, scale)),
        [extras, extras, struct((heads, LANES), F32)],
        (ids, *stat_all),
        smem=1,
    )
    wide, tall = (heads * down * rows, heads * across * rows)
    piece = (heads, rows, LANES)
    dq_own, dk_own, dv_own, sums, *partial = call(
        functools.partial(attention_kernel, (rows, heads, across, down, group, scale, sub == 1)),
        [struct(piece, F32)] * 3
        + [struct((rows, LANES), F32)]
        + [struct(piece)] * (down - 1)
        + [pieces] * (across - 1),
        (ids, *query_all, *key_all, score_cols, delta_cols),
        scratch=[
            pltpu.VMEM((wide, 2 * LANES), BF16),
            pltpu.VMEM((wide, 2 * LANES), BF16),
            pltpu.VMEM((tall, 2 * LANES), BF16),
            pltpu.VMEM((tall, 2 * LANES), BF16),
            pltpu.VMEM((wide, 2 * LANES), F32),
            pltpu.VMEM((tall, 2 * LANES), F32),
            pltpu.VMEM((tall, LANES), F32),
        ],
        smem=1,
    )
    key_back = [shift(partial[down - 2 + sa], 0, across - sa) for sa in range(1, across)]
    query_back = [shift(partial[sb - 1], down - sb, 0) for sb in range(1, down)]
    gate_own, *gate_parts = call(
        functools.partial(suffix_kernel, (rows, heads, across, down, group)),
        [struct((heads, LANES), F32)] + [struct((heads, STAT, LANES))] * (count - 1),
        (ids, sums),
        smem=1,
    )
    gate_back = [
        shift(part, (down - sb) % down, (across - sa) % across)
        for part, (sb, sa) in zip(gate_parts, members[1:])
    ]
    key_grads = call(
        functools.partial(combine_keys_kernel, scale),
        [struct((2 * rows, LANES))] * heads,
        (dk_own, dv_own, *key_back),
    )
    key_grads = turn(key_grads, -1)
    query_grads = call(
        functools.partial(combine_queries_kernel, scale, down),
        [struct((rows + STAT, LANES))] * heads,
        (dq_own, gate_own, keep, *query_back, *gate_back),
    )
    query_grads = turn(query_grads, -1)
    full = struct(queries.shape)
    dq, dk, dv, gate_grad = call(
        unpack_kernel,
        [full, full, full, struct((heads, rows))],
        (ids, *query_grads, *key_grads),
        smem=1,
    )
    return dq, dk, dv, gate_grad.T


def solution(mesh):
    split = P(("ctx", "head"), None)
    return jax.shard_map(
        per_device,
        mesh=mesh,
        in_specs=(split,) * 7,
        out_specs=(split,) * 4,
        check_vma=False,
    )
```

time: 332 us -> 81.5 us (0.25)
  blocking collectives: 245 us -> 0 us
  starting transfers between devices: 37.2 us -> 51.8 us
  local copies, waits for them, and re-layouts: 15.8 us -> 2.6 us
  Pallas kernels: 0 us -> 8.15 us
  matrix products: 4.86 us -> 0 us
  other arithmetic: 4.5 us -> 0 us
    all_gather x8 -> x0, blocking collectives: 228 us -> none  [the longest x1 32.3 us: per_device(): lax.all_gather(my_query, 'ctx', axis=0, tiled=True)]
    ppermute x0 -> x38, starting transfers between devices: none -> 51.8 us  [the longest x28 44.8 us: turn(): moved.append(lax.ppermute(chunks[k], both, pairs))]
    all_to_all x11 -> x0, starting transfers between devices: 37.2 us -> none  [the longest x1 4.24 us: per_device(): lax.all_to_all(gate_logits.astype(jnp.float32), 'head', split_axis=1, con...]
    all_to_all x11 -> x0, waiting for transfers between devices: 20.8 us -> none  [the longest x1 4.18 us: per_device(): lax.all_to_all(key_inputs, 'head', split_axis=1, concat_axis=0, tiled=True)]
    ppermute x0 -> x38, waiting for transfers between devices: none -> 17.8 us  [the longest x28 11.5 us: turn(): moved.append(lax.ppermute(chunks[k], both, pairs))]
    unnamed x1 -> x0, blocking collectives: 17.1 us -> none
    pallas_call x0 -> x9, Pallas kernels: none -> 8.15 us  [call(): pl.pallas_call(kernel, out_shape=out_shape, in_specs=[SMEM] * smem + [spa...]
    all_to_all x12 -> x0, local copies, waits for them, and re-layouts: 6.85 us -> none  [the longest x1 1.56 us: per_device(): lax.all_to_all(out_grad, 'head', split_axis=1, concat_axis=0, tiled=True)]
  transfers between devices with their start and end apart: 11 -> 38, of which waited for: 6 -> 12; matrix products, arithmetic and copies ran while one was open for 4% -> 0% of each run, Pallas kernels for 0% -> 2%
where the time goes in v1:
time: 81.5 us; the launch traced here: 81.3 us
  starting transfers between devices  51.8 us (64%)
  waiting for transfers between devices  17.8 us (22%)
  Pallas kernels  8.15 us (10%)
  local copies, waits for them, and re-layouts  2.6 us (3%)
  between operations  1.02 us (1%)
    ppermute x28, starting transfers between devices, turn(): moved.append(lax.ppermute(chunks[k], both, pairs))  44.8 us
    ppermute x28, waiting for transfers between devices, turn(): moved.append(lax.ppermute(chunks[k], both, pairs))  11.5 us
    pallas_call x9, Pallas kernels, call(): pl.pallas_call(kernel, out_shape=out_shape, in_specs=[SMEM] * smem + [spa...  8.15 us
    ppermute x10, starting transfers between devices, shift(): return lax.ppermute(array, both, pairs)  7.03 us
    ppermute x10, waiting for transfers between devices, shift(): return lax.ppermute(array, both, pairs)  6.28 us
    unnamed x14, local copies, waits for them, and re-layouts  2.51 us
  transfers between devices with their start and end apart: 38, of which 12 were waited for; matrix products, arithmetic and copies ran while one was open for 0% of the time, Pallas kernels for 2%

profile of v1, /device:TPU:0, one launch (start us, length us, event | category | flops | bytes accessed | tf_op | source)
XLA Modules:
  0.0 81.3 jit_solution(9128735416793262615)
XLA Ops:
  0.9 0.1 stack.23.ids
  1.0 0.4 copy-done.5
  1.4 0.0 copy-done.6
  1.4 0.2 copy-done.2
  1.6 0.1 copy-done
  1.7 0.0 copy-done.1
  1.7 0.9 %copy-done.3 = bf16[48,1024]{1,0:T(8,128)(2,1)S(1)} copy-done((bf16[48,1024]{1,0:T(8,128)(2,1)S(1)}, bf16[48,1024]{1,0:T(8,128)(2,1)}, u32[]{:S(2)}) %copy-start.3) | copy-done | bytes 98328
  2.6 0.9 %copy-done.4 = bf16[48,1024]{1,0:T(8,128)(2,1)S(1)} copy-done((bf16[48,1024]{1,0:T(8,128)(2,1)S(1)}, bf16[48,1024]{1,0:T(8,128)(2,1)}, u32[]{:S(2)}) %copy-start.4) | copy-done | bytes 98328
  3.5 1.7 %shard_map.102 = (bf16[112,128]{1,0:T(8,128)(2,1)S(1)}, bf16[112,128]{1,0:T(8,128)(2,1)S(1)}, bf16[112,128]{1,0:T(8,128)(2,1)S(1)}, bf16[112,128]{1,0:T(8,128)(2...) custom-call(s32[5]{0:T(128)S(1)} %stack.23.ids, ...), custom_call_target="tpu_custom_call" | custom-call | tf_op jit(solution)/shard_map/pallas_call | solution.py:369
  5.2 3.0 %collective-permute-start.8 = (bf16[96,128]{1,0:T(8,128)(2,1)S(1)}, bf16[96,128]{1,0:T(8,128)(2,1)S(1)}, u32[]{:S(2)}, u32[]{:S(2)}) collective-permute-start(bf16[96,128]{1,0:T(8,128)(2,1)S(1)} %get-tuple-element.65), channel_id=1, source_target_pairs={{0,4},{1,5},{2,6},{3,7},{4,8},{5,9},{6,10},{7,11},{8,12},{9,13},{1... | collective-permute-start | bytes 73736 | tf_op jit(solution)/shard_map/ppermute | solution.py:410
  8.2 1.6 %collective-permute-start.9 = (bf16[96,128]{1,0:T(8,128)(2,1)S(1)}, bf16[96,128]{1,0:T(8,128)(2,1)S(1)}, u32[]{:S(2)}, u32[]{:S(2)}) collective-permute-start(bf16[96,128]{1,0:T(8,128)(2,1)S(1)} %get-tuple-element.66), channel_id=1, source_target_pairs={{0,8},{1,9},{2,10},{3,11},{4,12},{5,13},{6,14},{7,15},{8,16},{9,17... | collective-permute-start | bytes 73736 | tf_op jit(solution)/shard_map/ppermute | solution.py:410
  9.8 2.6 %collective-permute-start.10 = (bf16[96,128]{1,0:T(8,128)(2,1)S(1)}, bf16[96,128]{1,0:T(8,128)(2,1)S(1)}, u32[]{:S(2)}, u32[]{:S(2)}) collective-permute-start(bf16[96,128]{1,0:T(8,128)(2,1)S(1)} %get-tuple-element.67), channel_id=1, source_target_pairs={{0,12},{1,13},{2,14},{3,15},{4,16},{5,17},{6,18},{7,19},{8,20},{9,... | collective-permute-start | bytes 73736 | tf_op jit(solution)/shard_map/ppermute | solution.py:410
  12.3 1.2 %collective-permute-start.11 = (bf16[96,128]{1,0:T(8,128)(2,1)S(1)}, bf16[96,128]{1,0:T(8,128)(2,1)S(1)}, u32[]{:S(2)}, u32[]{:S(2)}) collective-permute-start(bf16[96,128]{1,0:T(8,128)(2,1)S(1)} %get-tuple-element.68), channel_id=1, source_target_pairs={{0,16},{1,17},{2,18},{3,19},{4,20},{5,21},{6,22},{7,23},{8,24},{9,... | collective-permute-start | bytes 73736 | tf_op jit(solution)/shard_map/ppermute | solution.py:410
  13.6 0.6 collective-permute-start
  14.2 1.6 %collective-permute-start.1 = (bf16[112,128]{1,0:T(8,128)(2,1)S(1)}, bf16[112,128]{1,0:T(8,128)(2,1)S(1)}, u32[]{:S(2)}, u32[]{:S(2)}) collective-permute-start(bf16[112,128]{1,0:T(8,128)(2,1)S(1)} %get-tuple-element.57), channel_id=1, source_target_pairs={{0,8},{1,9},{2,10},{3,11},{4,12},{5,13},{6,14},{7,15},{8,16},{9,17... | collective-permute-start | bytes 86024 | tf_op jit(solution)/shard_map/ppermute | solution.py:410
  15.7 0.0 collective-permute-done.9.refs_2_
  15.7 3.1 %collective-permute-start.12 = (bf16[96,128]{1,0:T(8,128)(2,1)S(1)}, bf16[96,128]{1,0:T(8,128)(2,1)S(1)}, u32[]{:S(2)}, u32[]{:S(2)}) collective-permute-start(bf16[96,128]{1,0:T(8,128)(2,1)S(1)} %get-tuple-element.69), channel_id=1, source_target_pairs={{0,20},{1,21},{2,22},{3,23},{4,24},{5,25},{6,26},{7,27},{8,28},{9,... | collective-permute-start | bytes 73736 | tf_op jit(solution)/shard_map/ppermute | solution.py:410
  18.9 0.0 collective-permute-done.10.refs_3_
  18.9 0.3 collective-permute-start.13
  19.2 2.0 %collective-permute-start.14 = (bf16[96,128]{1,0:T(8,128)(2,1)S(1)}, bf16[96,128]{1,0:T(8,128)(2,1)S(1)}, u32[]{:S(2)}, u32[]{:S(2)}) collective-permute-start(bf16[96,128]{1,0:T(8,128)(2,1)S(1)} %get-tuple-element.71), channel_id=1, source_target_pairs={{0,28},{1,29},{2,30},{3,31},{4,0},{5,1},{6,2},{7,3},{8,4},{9,5},{1... | collective-permute-start | bytes 73736 | tf_op jit(solution)/shard_map/ppermute | solution.py:410
  21.1 0.0 collective-permute-done.12.refs_5_
  21.1 1.4 %collective-permute-start.2 = (bf16[112,128]{1,0:T(8,128)(2,1)S(1)}, bf16[112,128]{1,0:T(8,128)(2,1)S(1)}, u32[]{:S(2)}, u32[]{:S(2)}) collective-permute-start(bf16[112,128]{1,0:T(8,128)(2,1)S(1)} %get-tuple-element.58), channel_id=1, source_target_pairs={{0,12},{1,13},{2,14},{3,15},{4,16},{5,17},{6,18},{7,19},{8,20},{9,... | collective-permute-start | bytes 86024 | tf_op jit(solution)/shard_map/ppermute | solution.py:410
  22.5 0.1 collective-permute-done.13.refs_6_
  22.7 3.8 %collective-permute-start.3 = (bf16[112,128]{1,0:T(8,128)(2,1)S(1)}, bf16[112,128]{1,0:T(8,128)(2,1)S(1)}, u32[]{:S(2)}, u32[]{:S(2)}) collective-permute-start(bf16[112,128]{1,0:T(8,128)(2,1)S(1)} %get-tuple-element.59), channel_id=1, source_target_pairs={{0,16},{1,17},{2,18},{3,19},{4,20},{5,21},{6,22},{7,23},{8,24},{9,... | collective-permute-start | bytes 86024 | tf_op jit(solution)/shard_map/ppermute | solution.py:410
  26.5 2.4 %collective-permute-start.5 = (bf16[112,128]{1,0:T(8,128)(2,1)S(1)}, bf16[112,128]{1,0:T(8,128)(2,1)S(1)}, u32[]{:S(2)}, u32[]{:S(2)}) collective-permute-start(bf16[112,128]{1,0:T(8,128)(2,1)S(1)} %get-tuple-element.61), channel_id=1, source_target_pairs={{0,24},{1,25},{2,26},{3,27},{4,28},{5,29},{6,30},{7,31},{8,0},{9,1... | collective-permute-start | bytes 86024 | tf_op jit(solution)/shard_map/ppermute | solution.py:410
  28.9 1.7 %collective-permute-start.6 = (bf16[112,128]{1,0:T(8,128)(2,1)S(1)}, bf16[112,128]{1,0:T(8,128)(2,1)S(1)}, u32[]{:S(2)}, u32[]{:S(2)}) collective-permute-start(bf16[112,128]{1,0:T(8,128)(2,1)S(1)} %get-tuple-element.62), channel_id=1, source_target_pairs={{0,28},{1,29},{2,30},{3,31},{4,0},{5,1},{6,2},{7,3},{8,4},{9,5},{1... | collective-permute-start | bytes 86024 | tf_op jit(solution)/shard_map/ppermute | solution.py:410
  30.6 0.0 collective-permute-done.2.refs_3_
  30.6 0.1 collective-permute-start.15
  30.7 0.6 collective-permute-done.4.refs_5_
  31.3 1.5 %collective-permute-done.6.refs_7_ = bf16[112,128]{1,0:T(8,128)(2,1)S(1)} collective-permute-done((bf16[112,128]{1,0:T(8,128)(2,1)S(1)}, bf16[112,128]{1,0:T(8,128)(2,1)S(1)}, u32[]{:S(2)}, u32[]{:S(2)}) %collective-permute-start.6) | collective-permute-done | bytes 28704 | tf_op jit(solution)/shard_map/ppermute | solution.py:410
  32.8 1.6 %collective-permute-start.7 = (bf16[8,96,128]{2,1,0:T(8,128)(2,1)S(1)}, bf16[8,96,128]{2,1,0:T(8,128)(2,1)S(1)}, u32[]{:S(2)}, u32[]{:S(2)}) collective-permute-start(bf16[8,96,128]{2,1,0:T(8,128)(2,1)S(1)} %get-tuple-element.63.refs_0_), channel_id=1, source_target_pairs={{2,0},{3,1},{0,2},{1,3},{6,4},{7,5},{4,6},{5,7},{10,8},{11,9},{8,1... | collective-permute-start | bytes 589832 | tf_op jit(solution)/shard_map/ppermute | solution.py:400
  34.4 0.5 collective-permute-start.17
  34.9 1.3 %collective-permute-start.16 = (bf16[8,16,128]{2,1,0:T(8,128)(2,1)S(1)}, bf16[8,16,128]{2,1,0:T(8,128)(2,1)S(1)}, u32[]{:S(2)}, u32[]{:S(2)}) collective-permute-start(bf16[8,16,128]{2,1,0:T(8,128)(2,1)S(1)} %get-tuple-element.72.refs_0_), channel_id=1, source_target_pairs={{1,0},{0,1},{3,2},{2,3},{5,4},{4,5},{7,6},{6,7},{9,8},{8,9},{11,10... | collective-permute-start | bytes 98312 | tf_op jit(solution)/shard_map/ppermute | solution.py:400
  36.2 2.3 %collective-permute-done.18.refs_3_ = bf16[8,16,128]{2,1,0:T(8,128)(2,1)S(1)} collective-permute-done((bf16[8,16,128]{2,1,0:T(8,128)(2,1)S(1)}, bf16[8,16,128]{2,1,0:T(8,128)(2,1)S(1)}, u32[]{:S(2)}, u32[]{:S(2)}) %collective-permute-start.18) | collective-permute-done | bytes 32800 | tf_op jit(solution)/shard_map/ppermute | solution.py:400
  38.6 1.4 %collective-permute-done.17.refs_2_ = bf16[8,16,128]{2,1,0:T(8,128)(2,1)S(1)} collective-permute-done((bf16[8,16,128]{2,1,0:T(8,128)(2,1)S(1)}, bf16[8,16,128]{2,1,0:T(8,128)(2,1)S(1)}, u32[]{:S(2)}, u32[]{:S(2)}) %collective-permute-start.17) | collective-permute-done | bytes 32800 | tf_op jit(solution)/shard_map/ppermute | solution.py:400
  39.9 0.9 %shard_map.105 = (f32[1,48,128]{2,1,0:T(8,128)S(1)}, f32[1,48,128]{2,1,0:T(8,128)S(1)}, f32[8,128]{1,0:T(8,128)S(1)}) custom-call(s32[5]{0:T(128)S(1)} %stack.23.ids, bf16[8,16,128]{2,1,0:T(8,128)(2,1)S(1)} %get-tuple-element.72.refs_0_, bf16[8,16,128]{2,1,0:T(8,128)(2,1)S(1)} %collective-permute-done.16.refs_1_, ...), custom_call_target="tpu_custom_call" | custom-call | tf_op jit(solution)/shard_map/pallas_call | solution.py:369
  40.8 0.0 collective-permute-done.15.refs_3_
  40.9 3.2 %shard_map.106 = (f32[8,48,128]{2,1,0:T(8,128)S(1)}, f32[8,48,128]{2,1,0:T(8,128)S(1)}, f32[8,48,128]{2,1,0:T(8,128)S(1)}, f32[48,128]{1,0:T(8,128)S(1)}, bf16[8...) custom-call(s32[5]{0:T(128)S(1)} %stack.23.ids, bf16[8,96,128]{2,1,0:T(8,128)(2,1)S(1)} %get-tuple-element.63.refs_0_, ...), custom_call_target="tpu_custom_call" | custom-call | tf_op jit(solution)/shard_map/pallas_call | solution.py:369
  44.1 0.1 collective-permute-start.30
  44.1 1.5 %collective-permute-start.19 = (bf16[8,48,128]{2,1,0:T(8,128)(2,1)S(1)}, bf16[8,48,128]{2,1,0:T(8,128)(2,1)S(1)}, u32[]{:S(2)}, u32[]{:S(2)}) collective-permute-start(bf16[8,48,128]{2,1,0:T(8,128)(2,1)S(1)} %get-tuple-element.79), channel_id=1, source_target_pairs={{2,0},{3,1},{0,2},{1,3},{6,4},{7,5},{4,6},{5,7},{10,8},{11,9},{8,1... | collective-permute-start | bytes 294920 | tf_op jit(solution)/shard_map/ppermute | solution.py:400
  45.6 0.9 %shard_map.107 = (f32[8,128]{1,0:T(8,128)S(1)}, bf16[8,16,128]{2,1,0:T(8,128)(2,1)S(1)}, bf16[8,16,128]{2,1,0:T(8,128)(2,1)S(1)}, bf16[8,16,128]{2,1,0:T(8,128)(2,1)S(1)}) custom-call(s32[5]{0:T(128)S(1)} %stack.23.ids, f32[48,128]{1,0:T(8,128)S(1)} %get-tuple-element.76.sums_ref), custom_call_target="tpu_custom_call" | custom-call | tf_op jit(solution)/shard_map/pallas_call | solution.py:369
  46.6 0.2 collective-permute-start.20
  46.8 0.6 collective-permute-start.21
  47.4 1.1 %collective-permute-start.22 = (bf16[8,16,128]{2,1,0:T(8,128)(2,1)S(1)}, bf16[8,16,128]{2,1,0:T(8,128)(2,1)S(1)}, u32[]{:S(2)}, u32[]{:S(2)}) collective-permute-start(bf16[8,16,128]{2,1,0:T(8,128)(2,1)S(1)} %get-tuple-element.82), channel_id=1, source_target_pairs={{3,0},{2,1},{1,2},{0,3},{7,4},{6,5},{5,6},{4,7},{11,8},{10,9},{9,1... | collective-permute-start | bytes 98312 | tf_op jit(solution)/shard_map/ppermute | solution.py:400
  48.5 2.6 %collective-permute-done.21.refs_2_ = bf16[8,16,128]{2,1,0:T(8,128)(2,1)S(1)} collective-permute-done((bf16[8,16,128]{2,1,0:T(8,128)(2,1)S(1)}, bf16[8,16,128]{2,1,0:T(8,128)(2,1)S(1)}, u32[]{:S(2)}, u32[]{:S(2)}) %collective-permute-start.21) | collective-permute-done | bytes 32800 | tf_op jit(solution)/shard_map/ppermute | solution.py:400
  51.1 0.0 collective-permute-done.22.refs_3_
  51.1 0.1 shard_map.108
  51.1 4.4 %collective-permute-start.23 = (bf16[64,128]{1,0:T(8,128)(2,1)S(1)}, bf16[64,128]{1,0:T(8,128)(2,1)S(1)}, u32[]{:S(2)}, u32[]{:S(2)}) collective-permute-start(bf16[64,128]{1,0:T(8,128)(2,1)S(1)} %get-tuple-element.84), channel_id=1, source_target_pairs={{0,28},{1,29},{2,30},{3,31},{4,0},{5,1},{6,2},{7,3},{8,4},{9,5},{1... | collective-permute-start | bytes 49160 | tf_op jit(solution)/shard_map/ppermute | solution.py:410
  55.5 0.0 collective-permute-start.24
  55.6 3.0 %collective-permute-start.26 = (bf16[64,128]{1,0:T(8,128)(2,1)S(1)}, bf16[64,128]{1,0:T(8,128)(2,1)S(1)}, u32[]{:S(2)}, u32[]{:S(2)}) collective-permute-start(bf16[64,128]{1,0:T(8,128)(2,1)S(1)} %get-tuple-element.87), channel_id=1, source_target_pairs={{0,16},{1,17},{2,18},{3,19},{4,20},{5,21},{6,22},{7,23},{8,24},{9,... | collective-permute-start | bytes 49160 | tf_op jit(solution)/shard_map/ppermute | solution.py:410
  58.6 2.4 %collective-permute-start.31 = (bf16[96,128]{1,0:T(8,128)(2,1)S(1)}, bf16[96,128]{1,0:T(8,128)(2,1)S(1)}, u32[]{:S(2)}, u32[]{:S(2)}) collective-permute-start(bf16[96,128]{1,0:T(8,128)(2,1)S(1)} %get-tuple-element.95), channel_id=1, source_target_pairs={{0,28},{1,29},{2,30},{3,31},{4,0},{5,1},{6,2},{7,3},{8,4},{9,5},{1... | collective-permute-start | bytes 73736 | tf_op jit(solution)/shard_map/ppermute | solution.py:410
  61.0 1.2 %collective-permute-start.32 = (bf16[96,128]{1,0:T(8,128)(2,1)S(1)}, bf16[96,128]{1,0:T(8,128)(2,1)S(1)}, u32[]{:S(2)}, u32[]{:S(2)}) collective-permute-start(bf16[96,128]{1,0:T(8,128)(2,1)S(1)} %get-tuple-element.96), channel_id=1, source_target_pairs={{0,24},{1,25},{2,26},{3,27},{4,28},{5,29},{6,30},{7,31},{8,0},{9,1... | collective-permute-start | bytes 73736 | tf_op jit(solution)/shard_map/ppermute | solution.py:410
  62.2 0.9 %collective-permute-start.28 = (bf16[64,128]{1,0:T(8,128)(2,1)S(1)}, bf16[64,128]{1,0:T(8,128)(2,1)S(1)}, u32[]{:S(2)}, u32[]{:S(2)}) collective-permute-start(bf16[64,128]{1,0:T(8,128)(2,1)S(1)} %get-tuple-element.89), channel_id=1, source_target_pairs={{0,8},{1,9},{2,10},{3,11},{4,12},{5,13},{6,14},{7,15},{8,16},{9,17... | collective-permute-start | bytes 49160 | tf_op jit(solution)/shard_map/ppermute | solution.py:410
  63.1 2.0 %collective-permute-start.29 = (bf16[64,128]{1,0:T(8,128)(2,1)S(1)}, bf16[64,128]{1,0:T(8,128)(2,1)S(1)}, u32[]{:S(2)}, u32[]{:S(2)}) collective-permute-start(bf16[64,128]{1,0:T(8,128)(2,1)S(1)} %get-tuple-element.90), channel_id=1, source_target_pairs={{0,4},{1,5},{2,6},{3,7},{4,8},{5,9},{6,10},{7,11},{8,12},{9,13},{1... | collective-permute-start | bytes 49160 | tf_op jit(solution)/shard_map/ppermute | solution.py:410
  65.1 2.7 %collective-permute-done.27.refs_5_ = bf16[64,128]{1,0:T(8,128)(2,1)S(1)} collective-permute-done((bf16[64,128]{1,0:T(8,128)(2,1)S(1)}, bf16[64,128]{1,0:T(8,128)(2,1)S(1)}, u32[]{:S(2)}, u32[]{:S(2)}) %collective-permute-start.27) | collective-permute-done | bytes 16416 | tf_op jit(solution)/shard_map/ppermute | solution.py:410
  67.7 0.1 collective-permute-done.28.refs_6_
  67.8 3.6 %collective-permute-start.34 = (bf16[96,128]{1,0:T(8,128)(2,1)S(1)}, bf16[96,128]{1,0:T(8,128)(2,1)S(1)}, u32[]{:S(2)}, u32[]{:S(2)}) collective-permute-start(bf16[96,128]{1,0:T(8,128)(2,1)S(1)} %get-tuple-element.98), channel_id=1, source_target_pairs={{0,16},{1,17},{2,18},{3,19},{4,20},{5,21},{6,22},{7,23},{8,24},{9,... | collective-permute-start | bytes 73736 | tf_op jit(solution)/shard_map/ppermute | solution.py:410
  71.4 0.6 collective-permute-start.35
  72.0 1.5 %collective-permute-start.36 = (bf16[96,128]{1,0:T(8,128)(2,1)S(1)}, bf16[96,128]{1,0:T(8,128)(2,1)S(1)}, u32[]{:S(2)}, u32[]{:S(2)}) collective-permute-start(bf16[96,128]{1,0:T(8,128)(2,1)S(1)} %get-tuple-element.100), channel_id=1, source_target_pairs={{0,8},{1,9},{2,10},{3,11},{4,12},{5,13},{6,14},{7,15},{8,16},{9,17... | collective-permute-start | bytes 73736 | tf_op jit(solution)/shard_map/ppermute | solution.py:410
  73.5 0.4 collective-permute-done.34.refs_12_
  73.8 3.1 %collective-permute-done.35.refs_13_ = bf16[96,128]{1,0:T(8,128)(2,1)S(1)} collective-permute-done((bf16[96,128]{1,0:T(8,128)(2,1)S(1)}, bf16[96,128]{1,0:T(8,128)(2,1)S(1)}, u32[]{:S(2)}, u32[]{:S(2)}) %collective-permute-start.35) | collective-permute-done | bytes 24608 | tf_op jit(solution)/shard_map/ppermute | solution.py:410
  77.0 0.6 collective-permute-done.36.refs_14_
  77.6 2.4 %collective-permute-done.37.refs_15_ = bf16[96,128]{1,0:T(8,128)(2,1)S(1)} collective-permute-done((bf16[96,128]{1,0:T(8,128)(2,1)S(1)}, bf16[96,128]{1,0:T(8,128)(2,1)S(1)}, u32[]{:S(2)}, u32[]{:S(2)}) %collective-permute-start.37) | collective-permute-done | bytes 24608 | tf_op jit(solution)/shard_map/ppermute | solution.py:410
  80.0 1.3 %shard_map.110 = (bf16[48,1024]{1,0:T(8,128)(2,1)}, bf16[48,1024]{1,0:T(8,128)(2,1)}, bf16[48,1024]{1,0:T(8,128)(2,1)}, bf16[8,48]{1,0:T(8,128)(2,1)}) custom-call(s32[5]{0:T(128)S(1)} %stack.23.ids, bf16[64,128]{1,0:T(8,128)(2,1)S(1)} %get-tuple-element.83.refs_0_, bf16[64,128]{1,0:T(8,128)(2,1)S(1)} %collective-permute-done.23.refs_1_, ...), custom_call_target="tpu_custom_call" | custom-call | tf_op jit(solution)/shard_map/pallas_call | solution.py:369
  (36 shorter events, 0.2 us)
Async XLA Ops:
  0.7 0.7 copy-start.5
  0.7 0.7 copy-start.6
  0.7 0.9 %copy-start.2 = (bf16[48,1024]{1,0:T(8,128)(2,1)S(1)}, bf16[48,1024]{1,0:T(8,128)(2,1)}, u32[]{:S(2)}) copy-start(bf16[48,1024]{1,0:T(8,128)(2,1)} %refs_2_.1) | copy-start | bytes 294916
  0.8 0.9 %copy-start = (bf16[48,1024]{1,0:T(8,128)(2,1)S(1)}, bf16[48,1024]{1,0:T(8,128)(2,1)}, u32[]{:S(2)}) copy-start(bf16[48,1024]{1,0:T(8,128)(2,1)} %refs_0_.1) | copy-start | bytes 294916
  0.8 0.9 %copy-start.1 = (bf16[48,1024]{1,0:T(8,128)(2,1)S(1)}, bf16[48,1024]{1,0:T(8,128)(2,1)}, u32[]{:S(2)}) copy-start(bf16[48,1024]{1,0:T(8,128)(2,1)} %refs_1_.1) | copy-start | bytes 294916
  1.7 0.9 %copy-start.3 = (bf16[48,1024]{1,0:T(8,128)(2,1)S(1)}, bf16[48,1024]{1,0:T(8,128)(2,1)}, u32[]{:S(2)}) copy-start(bf16[48,1024]{1,0:T(8,128)(2,1)} %refs_3_.1) | copy-start | bytes 294916
  2.6 0.9 %copy-start.4 = (bf16[48,1024]{1,0:T(8,128)(2,1)S(1)}, bf16[48,1024]{1,0:T(8,128)(2,1)}, u32[]{:S(2)}) copy-start(bf16[48,1024]{1,0:T(8,128)(2,1)} %refs_4_.1) | copy-start | bytes 294916
  5.2 9.0 %collective-permute-start.8 = (bf16[96,128]{1,0:T(8,128)(2,1)S(1)}, bf16[96,128]{1,0:T(8,128)(2,1)S(1)}, u32[]{:S(2)}, u32[]{:S(2)}) collective-permute-start(bf16[96,128]{1,0:T(8,128)(2,1)S(1)} %get-tuple-element.65), channel_id=1, source_target_pairs={{0,4},{1,5},{2,6},{3,7},{4,8},{5,9},{6,10},{7,11},{8,12},{9,13},{1... | collective-permute-start | bytes 73736 | tf_op jit(solution)/shard_map/ppermute | solution.py:410
  8.2 7.5 %collective-permute-start.9 = (bf16[96,128]{1,0:T(8,128)(2,1)S(1)}, bf16[96,128]{1,0:T(8,128)(2,1)S(1)}, u32[]{:S(2)}, u32[]{:S(2)}) collective-permute-start(bf16[96,128]{1,0:T(8,128)(2,1)S(1)} %get-tuple-element.66), channel_id=1, source_target_pairs={{0,8},{1,9},{2,10},{3,11},{4,12},{5,13},{6,14},{7,15},{8,16},{9,17... | collective-permute-start | bytes 73736 | tf_op jit(solution)/shard_map/ppermute | solution.py:410
  9.8 9.1 %collective-permute-start.10 = (bf16[96,128]{1,0:T(8,128)(2,1)S(1)}, bf16[96,128]{1,0:T(8,128)(2,1)S(1)}, u32[]{:S(2)}, u32[]{:S(2)}) collective-permute-start(bf16[96,128]{1,0:T(8,128)(2,1)S(1)} %get-tuple-element.67), channel_id=1, source_target_pairs={{0,12},{1,13},{2,14},{3,15},{4,16},{5,17},{6,18},{7,19},{8,20},{9,... | collective-permute-start | bytes 73736 | tf_op jit(solution)/shard_map/ppermute | solution.py:410
  12.3 6.9 %collective-permute-start.11 = (bf16[96,128]{1,0:T(8,128)(2,1)S(1)}, bf16[96,128]{1,0:T(8,128)(2,1)S(1)}, u32[]{:S(2)}, u32[]{:S(2)}) collective-permute-start(bf16[96,128]{1,0:T(8,128)(2,1)S(1)} %get-tuple-element.68), channel_id=1, source_target_pairs={{0,16},{1,17},{2,18},{3,19},{4,20},{5,21},{6,22},{7,23},{8,24},{9,... | collective-permute-start | bytes 73736 | tf_op jit(solution)/shard_map/ppermute | solution.py:410
  13.6 13.0 %collective-permute-start = (bf16[112,128]{1,0:T(8,128)(2,1)S(1)}, bf16[112,128]{1,0:T(8,128)(2,1)S(1)}, u32[]{:S(2)}, u32[]{:S(2)}) collective-permute-start(bf16[112,128]{1,0:T(8,128)(2,1)S(1)} %get-tuple-element.56), channel_id=1, source_target_pairs={{0,4},{1,5},{2,6},{3,7},{4,8},{5,9},{6,10},{7,11},{8,12},{9,13},{1... | collective-permute-start | bytes 86024 | tf_op jit(solution)/shard_map/ppermute | solution.py:410
  14.2 14.8 %collective-permute-start.1 = (bf16[112,128]{1,0:T(8,128)(2,1)S(1)}, bf16[112,128]{1,0:T(8,128)(2,1)S(1)}, u32[]{:S(2)}, u32[]{:S(2)}) collective-permute-start(bf16[112,128]{1,0:T(8,128)(2,1)S(1)} %get-tuple-element.57), channel_id=1, source_target_pairs={{0,8},{1,9},{2,10},{3,11},{4,12},{5,13},{6,14},{7,15},{8,16},{9,17... | collective-permute-start | bytes 86024 | tf_op jit(solution)/shard_map/ppermute | solution.py:410
  15.7 5.4 %collective-permute-start.12 = (bf16[96,128]{1,0:T(8,128)(2,1)S(1)}, bf16[96,128]{1,0:T(8,128)(2,1)S(1)}, u32[]{:S(2)}, u32[]{:S(2)}) collective-permute-start(bf16[96,128]{1,0:T(8,128)(2,1)S(1)} %get-tuple-element.69), channel_id=1, source_target_pairs={{0,20},{1,21},{2,22},{3,23},{4,24},{5,25},{6,26},{7,27},{8,28},{9,... | collective-permute-start | bytes 73736 | tf_op jit(solution)/shard_map/ppermute | solution.py:410
  18.9 3.8 %collective-permute-start.13 = (bf16[96,128]{1,0:T(8,128)(2,1)S(1)}, bf16[96,128]{1,0:T(8,128)(2,1)S(1)}, u32[]{:S(2)}, u32[]{:S(2)}) collective-permute-start(bf16[96,128]{1,0:T(8,128)(2,1)S(1)} %get-tuple-element.70), channel_id=1, source_target_pairs={{0,24},{1,25},{2,26},{3,27},{4,28},{5,29},{6,30},{7,31},{8,0},{9,1... | collective-permute-start | bytes 73736 | tf_op jit(solution)/shard_map/ppermute | solution.py:410
  19.2 7.4 %collective-permute-start.14 = (bf16[96,128]{1,0:T(8,128)(2,1)S(1)}, bf16[96,128]{1,0:T(8,128)(2,1)S(1)}, u32[]{:S(2)}, u32[]{:S(2)}) collective-permute-start(bf16[96,128]{1,0:T(8,128)(2,1)S(1)} %get-tuple-element.71), channel_id=1, source_target_pairs={{0,28},{1,29},{2,30},{3,31},{4,0},{5,1},{6,2},{7,3},{8,4},{9,5},{1... | collective-permute-start | bytes 73736 | tf_op jit(solution)/shard_map/ppermute | solution.py:410
  21.1 9.4 %collective-permute-start.2 = (bf16[112,128]{1,0:T(8,128)(2,1)S(1)}, bf16[112,128]{1,0:T(8,128)(2,1)S(1)}, u32[]{:S(2)}, u32[]{:S(2)}) collective-permute-start(bf16[112,128]{1,0:T(8,128)(2,1)S(1)} %get-tuple-element.58), channel_id=1, source_target_pairs={{0,12},{1,13},{2,14},{3,15},{4,16},{5,17},{6,18},{7,19},{8,20},{9,... | collective-permute-start | bytes 86024 | tf_op jit(solution)/shard_map/ppermute | solution.py:410
  22.7 8.0 %collective-permute-start.3 = (bf16[112,128]{1,0:T(8,128)(2,1)S(1)}, bf16[112,128]{1,0:T(8,128)(2,1)S(1)}, u32[]{:S(2)}, u32[]{:S(2)}) collective-permute-start(bf16[112,128]{1,0:T(8,128)(2,1)S(1)} %get-tuple-element.59), channel_id=1, source_target_pairs={{0,16},{1,17},{2,18},{3,19},{4,20},{5,21},{6,22},{7,23},{8,24},{9,... | collective-permute-start | bytes 86024 | tf_op jit(solution)/shard_map/ppermute | solution.py:410
  26.5 4.8 %collective-permute-start.4 = (bf16[112,128]{1,0:T(8,128)(2,1)S(1)}, bf16[112,128]{1,0:T(8,128)(2,1)S(1)}, u32[]{:S(2)}, u32[]{:S(2)}) collective-permute-start(bf16[112,128]{1,0:T(8,128)(2,1)S(1)} %get-tuple-element.60), channel_id=1, source_target_pairs={{0,20},{1,21},{2,22},{3,23},{4,24},{5,25},{6,26},{7,27},{8,28},{9,... | collective-permute-start | bytes 86024 | tf_op jit(solution)/shard_map/ppermute | solution.py:410
  26.5 4.8 %collective-permute-start.5 = (bf16[112,128]{1,0:T(8,128)(2,1)S(1)}, bf16[112,128]{1,0:T(8,128)(2,1)S(1)}, u32[]{:S(2)}, u32[]{:S(2)}) collective-permute-start(bf16[112,128]{1,0:T(8,128)(2,1)S(1)} %get-tuple-element.61), channel_id=1, source_target_pairs={{0,24},{1,25},{2,26},{3,27},{4,28},{5,29},{6,30},{7,31},{8,0},{9,1... | collective-permute-start | bytes 86024 | tf_op jit(solution)/shard_map/ppermute | solution.py:410
  28.9 3.9 %collective-permute-start.6 = (bf16[112,128]{1,0:T(8,128)(2,1)S(1)}, bf16[112,128]{1,0:T(8,128)(2,1)S(1)}, u32[]{:S(2)}, u32[]{:S(2)}) collective-permute-start(bf16[112,128]{1,0:T(8,128)(2,1)S(1)} %get-tuple-element.62), channel_id=1, source_target_pairs={{0,28},{1,29},{2,30},{3,31},{4,0},{5,1},{6,2},{7,3},{8,4},{9,5},{1... | collective-permute-start | bytes 86024 | tf_op jit(solution)/shard_map/ppermute | solution.py:410
  30.6 10.2 %collective-permute-start.15 = (bf16[8,96,128]{2,1,0:T(8,128)(2,1)S(1)}, bf16[8,96,128]{2,1,0:T(8,128)(2,1)S(1)}, u32[]{:S(2)}, u32[]{:S(2)}) collective-permute-start(bf16[8,96,128]{2,1,0:T(8,128)(2,1)S(1)} %shard_map.104.refs_2_), channel_id=1, source_target_pairs={{1,0},{0,1},{3,2},{2,3},{5,4},{4,5},{7,6},{6,7},{9,8},{8,9},{11,10... | collective-permute-start | bytes 589832 | tf_op jit(solution)/shard_map/ppermute | solution.py:400
  32.8 8.0 %collective-permute-start.7 = (bf16[8,96,128]{2,1,0:T(8,128)(2,1)S(1)}, bf16[8,96,128]{2,1,0:T(8,128)(2,1)S(1)}, u32[]{:S(2)}, u32[]{:S(2)}) collective-permute-start(bf16[8,96,128]{2,1,0:T(8,128)(2,1)S(1)} %get-tuple-element.63.refs_0_), channel_id=1, source_target_pairs={{2,0},{3,1},{0,2},{1,3},{6,4},{7,5},{4,6},{5,7},{10,8},{11,9},{8,1... | collective-permute-start | bytes 589832 | tf_op jit(solution)/shard_map/ppermute | solution.py:400
  34.4 4.2 %collective-permute-start.18 = (bf16[8,16,128]{2,1,0:T(8,128)(2,1)S(1)}, bf16[8,16,128]{2,1,0:T(8,128)(2,1)S(1)}, u32[]{:S(2)}, u32[]{:S(2)}) collective-permute-start(bf16[8,16,128]{2,1,0:T(8,128)(2,1)S(1)} %get-tuple-element.72.refs_0_), channel_id=1, source_target_pairs={{3,0},{2,1},{1,2},{0,3},{7,4},{6,5},{5,6},{4,7},{11,8},{10,9},{9,1... | collective-permute-start | bytes 98312 | tf_op jit(solution)/shard_map/ppermute | solution.py:400
  34.4 5.6 %collective-permute-start.17 = (bf16[8,16,128]{2,1,0:T(8,128)(2,1)S(1)}, bf16[8,16,128]{2,1,0:T(8,128)(2,1)S(1)}, u32[]{:S(2)}, u32[]{:S(2)}) collective-permute-start(bf16[8,16,128]{2,1,0:T(8,128)(2,1)S(1)} %get-tuple-element.72.refs_0_), channel_id=1, source_target_pairs={{2,0},{3,1},{0,2},{1,3},{6,4},{7,5},{4,6},{5,7},{10,8},{11,9},{8,1... | collective-permute-start | bytes 98312 | tf_op jit(solution)/shard_map/ppermute | solution.py:400
  34.9 5.0 %collective-permute-start.16 = (bf16[8,16,128]{2,1,0:T(8,128)(2,1)S(1)}, bf16[8,16,128]{2,1,0:T(8,128)(2,1)S(1)}, u32[]{:S(2)}, u32[]{:S(2)}) collective-permute-start(bf16[8,16,128]{2,1,0:T(8,128)(2,1)S(1)} %get-tuple-element.72.refs_0_), channel_id=1, source_target_pairs={{1,0},{0,1},{3,2},{2,3},{5,4},{4,5},{7,6},{6,7},{9,8},{8,9},{11,10... | collective-permute-start | bytes 98312 | tf_op jit(solution)/shard_map/ppermute | solution.py:400
  44.1 14.5 %collective-permute-start.30 = (bf16[8,96,128]{2,1,0:T(8,128)(2,1)S(1)}, bf16[8,96,128]{2,1,0:T(8,128)(2,1)S(1)}, u32[]{:S(2)}, u32[]{:S(2)}) collective-permute-start(bf16[8,96,128]{2,1,0:T(8,128)(2,1)S(1)} %get-tuple-element.93), channel_id=1, source_target_pairs={{1,0},{0,1},{3,2},{2,3},{5,4},{4,5},{7,6},{6,7},{9,8},{8,9},{11,10... | collective-permute-start | bytes 589832 | tf_op jit(solution)/shard_map/ppermute | solution.py:400
  44.1 6.9 %collective-permute-start.19 = (bf16[8,48,128]{2,1,0:T(8,128)(2,1)S(1)}, bf16[8,48,128]{2,1,0:T(8,128)(2,1)S(1)}, u32[]{:S(2)}, u32[]{:S(2)}) collective-permute-start(bf16[8,48,128]{2,1,0:T(8,128)(2,1)S(1)} %get-tuple-element.79), channel_id=1, source_target_pairs={{2,0},{3,1},{0,2},{1,3},{6,4},{7,5},{4,6},{5,7},{10,8},{11,9},{8,1... | collective-permute-start | bytes 294920 | tf_op jit(solution)/shard_map/ppermute | solution.py:400
  46.6 1.9 %collective-permute-start.20 = (bf16[8,16,128]{2,1,0:T(8,128)(2,1)S(1)}, bf16[8,16,128]{2,1,0:T(8,128)(2,1)S(1)}, u32[]{:S(2)}, u32[]{:S(2)}) collective-permute-start(bf16[8,16,128]{2,1,0:T(8,128)(2,1)S(1)} %get-tuple-element.80), channel_id=1, source_target_pairs={{1,0},{0,1},{3,2},{2,3},{5,4},{4,5},{7,6},{6,7},{9,8},{8,9},{11,10... | collective-permute-start | bytes 98312 | tf_op jit(solution)/shard_map/ppermute | solution.py:400
  46.8 4.3 %collective-permute-start.21 = (bf16[8,16,128]{2,1,0:T(8,128)(2,1)S(1)}, bf16[8,16,128]{2,1,0:T(8,128)(2,1)S(1)}, u32[]{:S(2)}, u32[]{:S(2)}) collective-permute-start(bf16[8,16,128]{2,1,0:T(8,128)(2,1)S(1)} %get-tuple-element.81), channel_id=1, source_target_pairs={{2,0},{3,1},{0,2},{1,3},{6,4},{7,5},{4,6},{5,7},{10,8},{11,9},{8,1... | collective-permute-start | bytes 98312 | tf_op jit(solution)/shard_map/ppermute | solution.py:400
  47.4 3.7 %collective-permute-start.22 = (bf16[8,16,128]{2,1,0:T(8,128)(2,1)S(1)}, bf16[8,16,128]{2,1,0:T(8,128)(2,1)S(1)}, u32[]{:S(2)}, u32[]{:S(2)}) collective-permute-start(bf16[8,16,128]{2,1,0:T(8,128)(2,1)S(1)} %get-tuple-element.82), channel_id=1, source_target_pairs={{3,0},{2,1},{1,2},{0,3},{7,4},{6,5},{5,6},{4,7},{11,8},{10,9},{9,1... | collective-permute-start | bytes 98312 | tf_op jit(solution)/shard_map/ppermute | solution.py:400
  51.1 9.8 %collective-permute-start.23 = (bf16[64,128]{1,0:T(8,128)(2,1)S(1)}, bf16[64,128]{1,0:T(8,128)(2,1)S(1)}, u32[]{:S(2)}, u32[]{:S(2)}) collective-permute-start(bf16[64,128]{1,0:T(8,128)(2,1)S(1)} %get-tuple-element.84), channel_id=1, source_target_pairs={{0,28},{1,29},{2,30},{3,31},{4,0},{5,1},{6,2},{7,3},{8,4},{9,5},{1... | collective-permute-start | bytes 49160 | tf_op jit(solution)/shard_map/ppermute | solution.py:410
  55.5 6.6 %collective-permute-start.24 = (bf16[64,128]{1,0:T(8,128)(2,1)S(1)}, bf16[64,128]{1,0:T(8,128)(2,1)S(1)}, u32[]{:S(2)}, u32[]{:S(2)}) collective-permute-start(bf16[64,128]{1,0:T(8,128)(2,1)S(1)} %get-tuple-element.85), channel_id=1, source_target_pairs={{0,24},{1,25},{2,26},{3,27},{4,28},{5,29},{6,30},{7,31},{8,0},{9,1... | collective-permute-start | bytes 49160 | tf_op jit(solution)/shard_map/ppermute | solution.py:410
  55.6 6.6 %collective-permute-start.25 = (bf16[64,128]{1,0:T(8,128)(2,1)S(1)}, bf16[64,128]{1,0:T(8,128)(2,1)S(1)}, u32[]{:S(2)}, u32[]{:S(2)}) collective-permute-start(bf16[64,128]{1,0:T(8,128)(2,1)S(1)} %get-tuple-element.86), channel_id=1, source_target_pairs={{0,20},{1,21},{2,22},{3,23},{4,24},{5,25},{6,26},{7,27},{8,28},{9,... | collective-permute-start | bytes 49160 | tf_op jit(solution)/shard_map/ppermute | solution.py:410
  55.6 7.5 %collective-permute-start.26 = (bf16[64,128]{1,0:T(8,128)(2,1)S(1)}, bf16[64,128]{1,0:T(8,128)(2,1)S(1)}, u32[]{:S(2)}, u32[]{:S(2)}) collective-permute-start(bf16[64,128]{1,0:T(8,128)(2,1)S(1)} %get-tuple-element.87), channel_id=1, source_target_pairs={{0,16},{1,17},{2,18},{3,19},{4,20},{5,21},{6,22},{7,23},{8,24},{9,... | collective-permute-start | bytes 49160 | tf_op jit(solution)/shard_map/ppermute | solution.py:410
  58.6 13.4 %collective-permute-start.31 = (bf16[96,128]{1,0:T(8,128)(2,1)S(1)}, bf16[96,128]{1,0:T(8,128)(2,1)S(1)}, u32[]{:S(2)}, u32[]{:S(2)}) collective-permute-start(bf16[96,128]{1,0:T(8,128)(2,1)S(1)} %get-tuple-element.95), channel_id=1, source_target_pairs={{0,28},{1,29},{2,30},{3,31},{4,0},{5,1},{6,2},{7,3},{8,4},{9,5},{1... | collective-permute-start | bytes 73736 | tf_op jit(solution)/shard_map/ppermute | solution.py:410
  61.0 12.5 %collective-permute-start.32 = (bf16[96,128]{1,0:T(8,128)(2,1)S(1)}, bf16[96,128]{1,0:T(8,128)(2,1)S(1)}, u32[]{:S(2)}, u32[]{:S(2)}) collective-permute-start(bf16[96,128]{1,0:T(8,128)(2,1)S(1)} %get-tuple-element.96), channel_id=1, source_target_pairs={{0,24},{1,25},{2,26},{3,27},{4,28},{5,29},{6,30},{7,31},{8,0},{9,1... | collective-permute-start | bytes 73736 | tf_op jit(solution)/shard_map/ppermute | solution.py:410
  62.2 5.5 %collective-permute-start.27 = (bf16[64,128]{1,0:T(8,128)(2,1)S(1)}, bf16[64,128]{1,0:T(8,128)(2,1)S(1)}, u32[]{:S(2)}, u32[]{:S(2)}) collective-permute-start(bf16[64,128]{1,0:T(8,128)(2,1)S(1)} %get-tuple-element.88), channel_id=1, source_target_pairs={{0,12},{1,13},{2,14},{3,15},{4,16},{5,17},{6,18},{7,19},{8,20},{9,... | collective-permute-start | bytes 49160 | tf_op jit(solution)/shard_map/ppermute | solution.py:410
  62.2 5.6 %collective-permute-start.28 = (bf16[64,128]{1,0:T(8,128)(2,1)S(1)}, bf16[64,128]{1,0:T(8,128)(2,1)S(1)}, u32[]{:S(2)}, u32[]{:S(2)}) collective-permute-start(bf16[64,128]{1,0:T(8,128)(2,1)S(1)} %get-tuple-element.89), channel_id=1, source_target_pairs={{0,8},{1,9},{2,10},{3,11},{4,12},{5,13},{6,14},{7,15},{8,16},{9,17... | collective-permute-start | bytes 49160 | tf_op jit(solution)/shard_map/ppermute | solution.py:410
  63.1 8.3 %collective-permute-start.29 = (bf16[64,128]{1,0:T(8,128)(2,1)S(1)}, bf16[64,128]{1,0:T(8,128)(2,1)S(1)}, u32[]{:S(2)}, u32[]{:S(2)}) collective-permute-start(bf16[64,128]{1,0:T(8,128)(2,1)S(1)} %get-tuple-element.90), channel_id=1, source_target_pairs={{0,4},{1,5},{2,6},{3,7},{4,8},{5,9},{6,10},{7,11},{8,12},{9,13},{1... | collective-permute-start | bytes 49160 | tf_op jit(solution)/shard_map/ppermute | solution.py:410
  67.7 5.8 %collective-permute-start.33 = (bf16[96,128]{1,0:T(8,128)(2,1)S(1)}, bf16[96,128]{1,0:T(8,128)(2,1)S(1)}, u32[]{:S(2)}, u32[]{:S(2)}) collective-permute-start(bf16[96,128]{1,0:T(8,128)(2,1)S(1)} %get-tuple-element.97), channel_id=1, source_target_pairs={{0,20},{1,21},{2,22},{3,23},{4,24},{5,25},{6,26},{7,27},{8,28},{9,... | collective-permute-start | bytes 73736 | tf_op jit(solution)/shard_map/ppermute | solution.py:410
  67.8 6.1 %collective-permute-start.34 = (bf16[96,128]{1,0:T(8,128)(2,1)S(1)}, bf16[96,128]{1,0:T(8,128)(2,1)S(1)}, u32[]{:S(2)}, u32[]{:S(2)}) collective-permute-start(bf16[96,128]{1,0:T(8,128)(2,1)S(1)} %get-tuple-element.98), channel_id=1, source_target_pairs={{0,16},{1,17},{2,18},{3,19},{4,20},{5,21},{6,22},{7,23},{8,24},{9,... | collective-permute-start | bytes 73736 | tf_op jit(solution)/shard_map/ppermute | solution.py:410
  71.4 5.6 %collective-permute-start.35 = (bf16[96,128]{1,0:T(8,128)(2,1)S(1)}, bf16[96,128]{1,0:T(8,128)(2,1)S(1)}, u32[]{:S(2)}, u32[]{:S(2)}) collective-permute-start(bf16[96,128]{1,0:T(8,128)(2,1)S(1)} %get-tuple-element.99), channel_id=1, source_target_pairs={{0,12},{1,13},{2,14},{3,15},{4,16},{5,17},{6,18},{7,19},{8,20},{9,... | collective-permute-start | bytes 73736 | tf_op jit(solution)/shard_map/ppermute | solution.py:410
  72.0 5.6 %collective-permute-start.36 = (bf16[96,128]{1,0:T(8,128)(2,1)S(1)}, bf16[96,128]{1,0:T(8,128)(2,1)S(1)}, u32[]{:S(2)}, u32[]{:S(2)}) collective-permute-start(bf16[96,128]{1,0:T(8,128)(2,1)S(1)} %get-tuple-element.100), channel_id=1, source_target_pairs={{0,8},{1,9},{2,10},{3,11},{4,12},{5,13},{6,14},{7,15},{8,16},{9,17... | collective-permute-start | bytes 73736 | tf_op jit(solution)/shard_map/ppermute | solution.py:410
  73.5 6.5 %collective-permute-start.37 = (bf16[96,128]{1,0:T(8,128)(2,1)S(1)}, bf16[96,128]{1,0:T(8,128)(2,1)S(1)}, u32[]{:S(2)}, u32[]{:S(2)}) collective-permute-start(bf16[96,128]{1,0:T(8,128)(2,1)S(1)} %get-tuple-element.101), channel_id=1, source_target_pairs={{0,4},{1,5},{2,6},{3,7},{4,8},{5,9},{6,10},{7,11},{8,12},{9,13},{1... | collective-permute-start | bytes 73736 | tf_op jit(solution)/shard_map/ppermute | solution.py:410

commit v2 on v1

v2 whole, which is shorter than its diff:
```python
import functools
import math

import jax
import jax.numpy as jnp
from jax import lax
from jax.experimental import pallas as pl
from jax.experimental.pallas import tpu as pltpu
from jax.sharding import PartitionSpec as P

BF16 = jnp.bfloat16
F32 = jnp.float32
LANES = 128
STAT = 16
EXACT = lax.Precision.HIGHEST
VMEM = pl.BlockSpec(memory_space=pltpu.VMEM)
SMEM = pl.BlockSpec(memory_space=pltpu.SMEM)
HBM = pl.BlockSpec(memory_space=pltpu.HBM)
PACK_LIMIT = 64


def iota(shape, dim):
    return lax.broadcasted_iota(jnp.int32, shape, dim)


def dot_exact(a, b):
    return jnp.dot(a, b, precision=EXACT, preferred_element_type=F32)


def split3(x):
    hi = x.astype(BF16).astype(F32)
    rest = x - hi
    mid = rest.astype(BF16).astype(F32)
    low = (rest - mid).astype(BF16).astype(F32)
    return hi, mid, low


def stack_rows(rows):
    at = iota((STAT, LANES), 0)
    block = jnp.zeros((STAT, LANES), F32)
    for j, row in enumerate(rows):
        block = jnp.where(at == j, jnp.broadcast_to(row, (STAT, LANES)), block)
    return block


def pad_rows(x):
    missing = LANES - x.shape[0]
    if missing:
        x = jnp.concatenate([x, jnp.zeros((missing, x.shape[1]), x.dtype)], axis=0)
    return x


def wrap(x, n):
    return jnp.where(x >= n, x - n, x)


KIND, HALF, MEMBER, BASE = range(4)


def block_positions(ids, shape, dim, heads, stride, first, sources):
    index = iota(shape, dim)
    pos = jnp.full(shape, -1, jnp.int32)
    for at, src in enumerate(sources):
        begin = first + at * heads
        here = (index >= begin) & (index < begin + heads)
        pos = jnp.where(here, ids[BASE + src] + (index - begin) * stride, pos)
    return pos


def pack_kernel(*refs):
    sources, out_ref, refs = (refs[:7], refs[7], refs[8:])
    heads, rows = sources[5].shape
    *held, gate_wide, lse_wide, sems = refs
    copies = [pltpu.make_async_copy(src, dst, sems.at[i]) for i, (src, dst) in enumerate(zip(sources, held))]
    for i in (5, 6, 3, 4, 0, 1, 2):
        copies[i].start()
    q_ref, k_ref, v_ref, g_ref, o_ref, gate_ref, lse_ref = held
    copies[5].wait()
    copies[6].wait()
    gate_wide[...] = jnp.zeros_like(gate_wide)
    lse_wide[...] = jnp.zeros_like(lse_wide)
    gate_wide[:, 0:rows] = gate_ref[...].astype(F32)
    lse_wide[:, 0:rows] = lse_ref[...]
    copies[3].wait()
    copies[4].wait()
    lane = iota((rows, LANES), 1)
    delta = jnp.zeros((rows, LANES), F32)
    for h in range(heads):
        cols = pl.ds(h * LANES, LANES)
        grad = g_ref[:, cols]
        row_sum = jnp.sum(grad.astype(F32) * o_ref[:, cols].astype(F32), axis=1, keepdims=True)
        delta = jnp.where(lane == h, row_sum, delta)
        out_ref[h, rows : 2 * rows, :] = grad
    parts = [gate_wide[...], *split3(lse_wide[...]), *split3(pad_rows(delta).T[:heads])]
    for h in range(heads):
        block = stack_rows([part[h : h + 1] for part in parts])
        out_ref[h, 2 * rows : 2 * rows + STAT, :] = block.astype(BF16)
    for i, ref, first in ((0, q_ref, 0), (1, k_ref, 2 * rows + STAT), (2, v_ref, 3 * rows + STAT)):
        copies[i].wait()
        for h in range(heads):
            out_ref[h, first : first + rows, :] = ref[:, pl.ds(h * LANES, LANES)]


def attention_kernel(plan, ids, own_ref, *refs):
    rows, heads, members, scale = plan
    peers, cross, corner, refs = (
        refs[: members - 1],
        refs[members - 1],
        refs[members : 2 * members - 1],
        refs[2 * members - 1 :],
    )
    outs, scratch = (refs[: 6 + 2 * (members - 1)], refs[6 + 2 * (members - 1) :])
    for kind in (0, 1):

        @pl.when(ids[KIND] == kind)
        def _(kind=kind):
            attention_body(plan, kind, ids, own_ref, peers, cross, corner, outs, scratch)


def attention_body(plan, kind, ids, own_ref, peers, cross, corner, outs, scratch):
    rows, heads, members, scale = plan
    dq_own, dk_own, dv_own, gate_own, keep_own, to_cross = outs[:6]
    to_peer, to_corner = (outs[6 : 5 + members], outs[5 + members :])
    full_1, full_2, some_1, some_2, full_acc, some_acc, value_acc = scratch
    wanted = ids[HALF] == kind
    count = 2 * members
    stat_at = 2 * rows
    peer_stat, cross_stat = ((0, stat_at) if kind == 0 else (stat_at, 0))

    def stat_block(src):
        if src == 0:
            block = own_ref[:, stat_at : stat_at + STAT, :]
        elif src < members:
            block = peers[src - 1][:, peer_stat : peer_stat + STAT, :]
        elif src == members:
            block = cross[:, cross_stat : cross_stat + STAT, :]
        else:
            block = corner[src - members - 1][...]
        return block.astype(F32)

    stats = [stat_block(src) for src in range(count)]

    def row_of(src, j):
        return jnp.concatenate([stats[src][k, j : j + 1, :] for k in range(heads)], axis=0)

    gates = [row_of(src, 0) for src in range(count)]
    in_row = iota((heads, LANES), 1) < rows
    logs = []
    for src, x in enumerate(gates):
        log_gate = jnp.minimum(x, 0.0) - jnp.log1p(jnp.exp(-jnp.abs(x)))
        held = in_row if src < members else in_row & wanted
        logs.append(jnp.where(held, log_gate, 0.0))
    logs = jnp.concatenate(logs, axis=0)
    blocks = count * heads
    square = (LANES, LANES)
    upto = (iota(square, 0) <= iota(square, 1)).astype(F32)
    row_pos = block_positions(ids, (blocks, blocks), 0, heads, members, 0, range(count))
    lane_pos = block_positions(ids, (blocks, blocks), 1, heads, members, 0, range(count))
    before = jnp.sum(dot_exact((lane_pos < row_pos).astype(F32), logs), axis=1, keepdims=True)
    curve = dot_exact(logs, upto) + before

    def curve_of(src):
        return curve[src * heads : (src + 1) * heads]

    all_members, pair = (list(range(members)), [0, members])
    q_sources, k_sources = ((pair, all_members) if kind == 0 else (all_members, pair))
    zero = jnp.zeros((heads, LANES), F32)
    score_cols, delta_cols = [], []
    for m in range(-(-max(members, 2) // 2)):
        q_rows, d_rows, k_rows = [], [], []
        for s in (2 * m, 2 * m + 1):
            if s < len(q_sources):
                src = q_sources[s]
                lse = row_of(src, 1) + row_of(src, 2) + row_of(src, 3)
                q_rows += [*split3((curve_of(src) - lse) / scale), zero]
                d_rows += [-row_of(src, 4), -row_of(src, 5), -row_of(src, 6), zero]
            else:
                q_rows += [zero] * 4
                d_rows += [zero] * 4
            if s < len(k_sources):
                k_rows += [*split3(-curve_of(k_sources[s]) / scale), zero]
            else:
                k_rows += [zero] * 4
        score_cols.append(jnp.concatenate(q_rows + k_rows, axis=0).T[:rows])
        delta_cols.append(pad_rows(jnp.concatenate(d_rows, axis=0)).T[:rows])

    lane = iota((rows, LANES), 1)
    half = 8 * heads
    upper = (lane >= half).astype(F32)
    lower = (lane < half).astype(F32)
    ones = jnp.ones((rows, LANES), BF16)

    def slot(s, k, start):
        inner = lane - start - (s % 2) * 4 * heads
        return (inner >= 0) & (inner < 4 * heads) & (lane % heads == k)

    def full_at(k, s):
        begin = (k * members + wrap(ids[MEMBER] + s, members)) * rows
        return pl.ds(pl.multiple_of(begin, math.gcd(rows, LANES)), rows)

    def some_at(k, s):
        return pl.ds((s * heads + k) * rows, rows)

    def pieces(src, query_side):
        if src == 0:
            return own_ref, 0 if query_side else stat_at + STAT
        return (cross if src == members else peers[src - 1]), 0 if query_side else STAT

    (q_1, q_2, q_at), (k_1, k_2, k_at) = (full_1, full_2, full_at), (some_1, some_2, some_at)
    if kind == 0:
        (q_1, q_2, q_at), (k_1, k_2, k_at) = (k_1, k_2, k_at), (q_1, q_2, q_at)
    for k in range(heads):
        for s, src in enumerate(q_sources):
            array, first = pieces(src, True)
            mine = slot(s, k, 0)
            q_1[q_at(k, s), 0:LANES] = array[k, first : first + rows, :]
            q_1[q_at(k, s), LANES:] = jnp.where(mine, score_cols[s // 2], upper).astype(BF16)
            q_2[q_at(k, s), 0:LANES] = array[k, first + rows : first + 2 * rows, :]
            q_2[q_at(k, s), LANES:] = jnp.where(mine, delta_cols[s // 2], 0.0).astype(BF16)
        for s, src in enumerate(k_sources):
            array, first = pieces(src, False)
            mine = slot(s, k, half)
            k_1[k_at(k, s), 0:LANES] = array[k, first : first + rows, :]
            k_1[k_at(k, s), LANES:] = jnp.where(mine, score_cols[s // 2], lower).astype(BF16)
            k_2[k_at(k, s), 0:LANES] = array[k, first + rows : first + 2 * rows, :]
            k_2[k_at(k, s), LANES:] = ones

    factor = scale * math.log2(math.e)
    nt = (((1,), (1,)), ((), ()))
    tn = (((0,), (0,)), ((), ()))
    own_rows, slot_rows = (heads * rows, members * rows)
    full_rows = heads * slot_rows

    def some_pos(begin, size):
        index = iota((1, size), 1) + begin
        pos = index + ids[MEMBER] * rows
        for k in range(1, heads):
            pos = jnp.where(index >= k * rows, pos + (slot_rows - rows), pos)
        return pos

    def tile(full, some, causal):
        f_at, s_at = (pl.ds(*full), pl.ds(*some))
        f_1, f_2, s_1, s_2 = (full_1[f_at, :], full_2[f_at, :], some_1[s_at, :], some_2[s_at, :])
        scores = lax.dot_general(f_1, s_1, nt, preferred_element_type=F32)
        shifted = lax.dot_general(f_2, s_2, nt, preferred_element_type=F32)
        probs = jnp.exp2(scores * factor)
        if causal:
            f_pos = iota((full[1], some[1]), 0) + full[0]
            s_pos = some_pos(*some)
            probs = jnp.where(f_pos <= s_pos if kind == 0 else f_pos >= s_pos, probs, 0.0)
        grads = (probs * shifted).astype(BF16)
        probs = probs.astype(BF16)
        to_full = jnp.dot(grads, s_1, preferred_element_type=F32)
        to_some = lax.dot_general(grads, f_1, tn, preferred_element_type=F32)
        if kind == 0:
            value = jnp.dot(probs, s_2[:, 0:LANES], preferred_element_type=F32)
        else:
            value = lax.dot_general(probs, f_2[:, 0:LANES], tn, preferred_element_type=F32)
        return to_full, to_some, value

    if members == 2:
        quarter = own_rows // 2
        written = set()

        def store(acc, begin, value):
            for first in range(0, value.shape[0], quarter):
                at = pl.ds(begin + first, quarter)
                part = value[first : first + quarter]
                key = (id(acc), begin + first)
                acc[at, :] = acc[at, :] + part if key in written else part
                written.add(key)

        def add(full, some, causal):
            to_full, to_some, value = tile(full, some, causal)
            store(full_acc, full[0], to_full)
            store(some_acc, some[0], to_some)
            store(value_acc, full[0] if kind == 0 else some[0], value)

        top, bottom = ((0, full_rows // 2), (full_rows // 2, full_rows // 2))
        if kind == 0:
            add(top, (0, own_rows), True)
            add(bottom, (quarter, quarter), True)
        else:
            add(bottom, (0, own_rows), True)
            add(top, (0, quarter), True)

        @pl.when(wanted)
        def _():
            add(top, (own_rows, own_rows), False)
            add(bottom, (own_rows, own_rows), False)

        @pl.when(jnp.logical_not(wanted))
        def _():
            at = pl.ds(own_rows, own_rows)
            some_acc[at, :] = jnp.zeros((own_rows, 2 * LANES), F32)
            if kind == 1:
                value_acc[at, :] = jnp.zeros((own_rows, LANES), F32)

    else:
        full_acc[...] = jnp.zeros_like(full_acc)
        some_acc[...] = jnp.zeros_like(some_acc)
        value_acc[...] = jnp.zeros_like(value_acc)

        def add(full, some, causal):
            to_full, to_some, value = tile(full, some, causal)
            full_acc[pl.ds(*full), :] += to_full
            some_acc[pl.ds(*some), :] += to_some
            value_acc[pl.ds(*(full if kind == 0 else some)), :] += value

        @pl.loop(0, heads)
        def _(k):
            full = (pl.multiple_of(k * slot_rows, math.gcd(slot_rows, LANES)), slot_rows)
            add(full, (0, own_rows), True)

            @pl.when(wanted)
            def _():
                add(full, (own_rows, own_rows), False)

    shape = (blocks, LANES)
    target_pos = block_positions(ids, shape, 0, heads, members, 0, range(count))
    onward = (iota(square, 0) >= iota(square, 1)).astype(F32)
    (q_acc, k_acc) = (some_acc, full_acc) if kind == 0 else (full_acc, some_acc)
    later, inner = (jnp.zeros(shape, F32), jnp.zeros(shape, F32))
    for m in range(-(-max(members, 2) // 8)):
        some_q, some_k = (q_sources[8 * m : 8 * m + 8], k_sources[8 * m : 8 * m + 8])
        sums = jnp.zeros((rows, LANES), F32)
        for k in range(heads):
            for s in range(len(some_q)):
                part = q_acc[q_at(k, 8 * m + s), LANES:]
                sums = jnp.where(lane == s * heads + k, part, sums)
            for s in range(len(some_k)):
                part = k_acc[k_at(k, 8 * m + s), LANES:]
                sums = jnp.where(lane == half + s * heads + k, -part, sums)
        turned = pad_rows(sums).T
        slot_pos = jnp.maximum(
            block_positions(ids, shape, 1, heads, members, 0, some_q),
            block_positions(ids, shape, 1, heads, members, half, some_k),
        )
        later += dot_exact((slot_pos > target_pos).astype(F32), turned)
        inner += dot_exact((slot_pos == target_pos).astype(F32), turned)
    suffix = jnp.sum(later, axis=1, keepdims=True) + dot_exact(inner, onward)

    def suffix_block(src, k):
        at = slice(src * heads + k, src * heads + k + 1)
        return stack_rows(split3(suffix[at])).astype(BF16)

    gate_own[...] = suffix[0:heads]
    keep_own[...] = 1.0 / (1.0 + jnp.exp(gates[0]))

    def query_grad(k, s):
        return q_acc[q_at(k, s), 0:LANES]

    def key_grad(k, s):
        return k_acc[k_at(k, s), 0:LANES]

    def value_grad(k, s):
        return value_acc[k_at(k, s), :]

    blank = jnp.zeros((rows, LANES), BF16)
    for k in range(heads):
        dq_own[k] = query_grad(k, 0)
        dk_own[k] = key_grad(k, 0)
        dv_own[k] = value_grad(k, 0)
        sends = [(to_cross, 1, members, kind == 1)]
        sends += [(to_peer[s - 1], s, s, kind == 0) for s in range(1, members)]
        for ref, s, src, keys in sends:
            ref[k, 0:rows, :] = (key_grad(k, s) if keys else query_grad(k, s)).astype(BF16)
            ref[k, rows : 2 * rows, :] = value_grad(k, s).astype(BF16) if keys else blank
            ref[k, 2 * rows :, :] = suffix_block(src, k)
        for s in range(1, members):
            to_corner[s - 1][k] = suffix_block(members + s, k)


def combine_kernel(plan, ids, dq_ref, dk_ref, dv_ref, gate_ref, keep_ref, cross, *refs):
    rows, heads, members, scale = plan
    peers, corner, out_ref = (refs[: members - 1], refs[members - 1 : -1], refs[-1])
    for kind in (0, 1):

        @pl.when(ids[KIND] == kind)
        def _(kind=kind):
            key_from, query_from = ((peers, [cross]) if kind == 0 else ([cross], peers))
            for k in range(heads):
                dq, dk, dv = (dq_ref[k], dk_ref[k], dv_ref[k])
                extra = jnp.zeros((STAT, LANES), F32)
                for ref in query_from:
                    dq += ref[k, 0:rows, :].astype(F32)
                for ref in key_from:
                    dk += ref[k, 0:rows, :].astype(F32)
                    dv += ref[k, rows : 2 * rows, :].astype(F32)
                for ref in (cross, *peers):
                    extra += ref[k, 2 * rows :, :].astype(F32)
                for ref in corner:
                    extra += ref[k].astype(F32)
                out_ref[k, 0:rows, :] = (scale * dq).astype(BF16)
                out_ref[k, rows : 2 * rows, :] = (scale * dk).astype(BF16)
                out_ref[k, 2 * rows : 3 * rows, :] = dv.astype(BF16)
                total = gate_ref[k : k + 1, :] + jnp.sum(extra, axis=0, keepdims=True)
                gate = total * keep_ref[k : k + 1, :]
                out_ref[k, 3 * rows :, :] = jnp.broadcast_to(gate, (STAT, LANES)).astype(BF16)


def unpack_kernel(in_ref, dq_ref, dk_ref, dv_ref, gate_ref):
    rows = dq_ref.shape[0]
    heads = in_ref.shape[0]
    gates = []
    for h in range(heads):
        cols = pl.ds(h * LANES, LANES)
        dq_ref[:, cols] = in_ref[h, 0:rows, :]
        dk_ref[:, cols] = in_ref[h, rows : 2 * rows, :]
        dv_ref[:, cols] = in_ref[h, 2 * rows : 3 * rows, :]
        gates.append(in_ref[h, 3 * rows :, :].astype(F32)[0:1])
    gate_ref[...] = jnp.concatenate(gates, axis=0)[:, 0:rows].astype(BF16)


def struct(shape, dtype=BF16):
    return jax.ShapeDtypeStruct(shape, dtype)


def call(kernel, out_shape, inputs, scratch=(), smem=0, space=VMEM, limit=40):
    return pl.pallas_call(
        kernel,
        out_shape=out_shape,
        in_specs=[SMEM] * smem + [space] * (len(inputs) - smem),
        out_specs=jax.tree.map(lambda _: VMEM, out_shape),
        scratch_shapes=list(scratch),
        compiler_params=pltpu.CompilerParams(vmem_limit_bytes=limit * 1024 * 1024),
    )(*inputs)


def per_device(queries, key_inputs, value_inputs, out_grad, attn_output, gate_logits, lse):
    ctx, group = (lax.axis_size("ctx"), lax.axis_size("head"))
    rows, heads = gate_logits.shape
    width = queries.shape[1]
    scale = (width // heads) ** -0.5
    half = ctx * group // 2
    members = half // heads
    both = ("ctx", "head")

    def device(side, slot, member):
        return side * half + slot * members + member

    def shift(array, across, along, chosen):
        pairs = [
            (device(side ^ across, slot, (member + along) % members), device(side, slot, member))
            for side in (0, 1)
            for slot in range(heads)
            for member in range(members)
            if chosen(side, int(slot >= heads // 2))
        ]
        return lax.ppermute(array, both, pairs)

    def everyone(side, kind):
        return True

    def working(side, kind):
        return side == kind

    def waiting(side, kind):
        return side != kind

    regions = [
        [device(side, slot, member) for slot in range(heads)] for side in (0, 1) for member in range(members)
    ]

    def exchange(array):
        return lax.all_to_all(
            array, both, split_axis=0, concat_axis=0, axis_index_groups=regions, tiled=True
        )

    here = lax.axis_index("ctx") * group + lax.axis_index("head")
    side, place = (here // half, here % half)
    slot, member = (place // members, place % members)
    kind = jnp.where(slot >= heads // 2, 1, 0)
    ids = [kind, side, member]
    for other in (0, 1):
        ids += [((side + other) % 2) * half + (member + s) % members for s in range(members)]
    ids = jnp.stack(ids).astype(jnp.int32)

    packed = call(
        pack_kernel,
        struct((heads, 4 * rows + STAT, LANES)),
        (queries, key_inputs, value_inputs, out_grad, attn_output, gate_logits.T, lse.T),
        scratch=[pltpu.VMEM((rows, width), BF16)] * 5
        + [pltpu.VMEM((heads, rows), BF16), pltpu.VMEM((heads, rows), F32)]
        + [pltpu.VMEM((heads, LANES), F32)] * 2
        + [pltpu.SemaphoreType.DMA((7,))],
        space=HBM,
        limit=PACK_LIMIT,
    )
    own = exchange(packed)
    length = 2 * rows + STAT

    def part(keys):
        return lax.dynamic_slice_in_dim(own, jnp.where(keys, 2 * rows, 0), length, axis=1)

    cross_send, peer_send = (part(kind == 1), part(kind == 0))
    stat_send = own[:, 2 * rows : length]
    cross = shift(cross_send, 1, 0, working)
    peers = [shift(peer_send, 0, s, everyone) for s in range(1, members)]
    corner = [shift(stat_send, 1, s, working) for s in range(1, members)]

    plan = (rows, heads, members, scale)
    own_rows, full_rows = (heads * rows, heads * members * rows)
    piece = struct((heads, rows, LANES), F32)
    small = struct((heads, LANES), F32)
    sent = struct((heads, length, LANES))
    dq, dk, dv, gate, keep, to_cross, *others = call(
        functools.partial(attention_kernel, plan),
        [piece, piece, piece, small, small, sent]
        + [sent] * (members - 1)
        + [struct((heads, STAT, LANES))] * (members - 1),
        (ids, own, *peers, cross, *corner),
        scratch=[
            pltpu.VMEM((full_rows, 2 * LANES), BF16),
            pltpu.VMEM((full_rows, 2 * LANES), BF16),
            pltpu.VMEM((2 * own_rows, 2 * LANES), BF16),
            pltpu.VMEM((2 * own_rows, 2 * LANES), BF16),
            pltpu.VMEM((full_rows, 2 * LANES), F32),
            pltpu.VMEM((2 * own_rows, 2 * LANES), F32),
            pltpu.VMEM((max(full_rows, 2 * own_rows), LANES), F32),
        ],
        smem=1,
    )
    to_peer, to_corner = (others[: members - 1], others[members - 1 :])
    cross = shift(to_cross, 1, 0, waiting)
    peers = [shift(to_peer[s - 1], 0, members - s, everyone) for s in range(1, members)]
    corner = [shift(to_corner[s - 1], 1, members - s, waiting) for s in range(1, members)]
    summed = call(
        functools.partial(combine_kernel, plan),
        struct((heads, 3 * rows + STAT, LANES)),
        (ids, dq, dk, dv, gate, keep, cross, *peers, *corner),
        smem=1,
    )
    final = exchange(summed)
    full = struct(queries.shape)
    dq, dk, dv, gate_grad = call(unpack_kernel, [full, full, full, struct((heads, rows))], (final,))
    return dq, dk, dv, gate_grad.T


def solution(mesh):
    split = P(("ctx", "head"), None)
    return jax.shard_map(
        per_device,
        mesh=mesh,
        in_specs=(split,) * 7,
        out_specs=(split,) * 4,
        check_vma=False,
    )
```

time: 81.5 us -> 52.9 us (0.65)
  starting transfers between devices: 51.8 us -> 11.7 us
  blocking collectives: 0 us -> 13.3 us
  local copies, waits for them, and re-layouts: 2.6 us -> 0.12 us
  waiting for transfers between devices: 17.8 us -> 19.1 us
    ppermute x28 -> x0, starting transfers between devices: 44.8 us -> none  [turn(): moved.append(lax.ppermute(chunks[k], both, pairs))]
    all_to_all x0 -> x1, blocking collectives: none -> 13.3 us  [exchange(): lax.all_to_all(array, both, split_axis=0, concat_axis=0, axis_index_group...]
    ppermute x28 -> x0, waiting for transfers between devices: 11.5 us -> none  [turn(): moved.append(lax.ppermute(chunks[k], both, pairs))]
    all_to_all x0 -> x1, waiting for transfers between devices: none -> 8.15 us  [exchange(): lax.all_to_all(array, both, split_axis=0, concat_axis=0, axis_index_group...]
    all_to_all x0 -> x1, starting transfers between devices: none -> 6.2 us  [exchange(): lax.all_to_all(array, both, split_axis=0, concat_axis=0, axis_index_group...]
    ppermute x10 -> x6, waiting for transfers between devices: 6.28 us -> 10.9 us  [shift(): return lax.ppermute(array, both, pairs)]
    unnamed x14 -> x0, local copies, waits for them, and re-layouts: 2.51 us -> none
    ppermute x10 -> x6, starting transfers between devices: 7.03 us -> 5.48 us  [shift(): return lax.ppermute(array, both, pairs)]
  transfers between devices with their start and end apart: 38 -> 7, of which waited for: 12 -> 4; matrix products, arithmetic and copies ran while one was open for 0% -> 0% of each run, Pallas kernels for 2% -> 0%
where the time goes in v2:
time: 52.9 us; the launch traced here: 52.6 us
  waiting for transfers between devices  19.1 us (36%)
  blocking collectives  13.3 us (25%)
  starting transfers between devices  11.7 us (22%)
  Pallas kernels  7.6 us (14%)
  between operations  0.79 us (1%)
    all_to_all x1, blocking collectives, exchange(): lax.all_to_all(array, both, split_axis=0, concat_axis=0, axis_index_group...  13.3 us
    ppermute x6, waiting for transfers between devices, shift(): return lax.ppermute(array, both, pairs)  10.9 us
    all_to_all x1, waiting for transfers between devices, exchange(): lax.all_to_all(array, both, split_axis=0, concat_axis=0, axis_index_group...  8.15 us
    pallas_call x4, Pallas kernels, call(): pl.pallas_call(kernel, out_shape=out_shape, in_specs=[SMEM] * smem + [spa...  7.6 us
    all_to_all x1, starting transfers between devices, exchange(): lax.all_to_all(array, both, split_axis=0, concat_axis=0, axis_index_group...  6.2 us
    ppermute x6, starting transfers between devices, shift(): return lax.ppermute(array, both, pairs)  5.48 us
  transfers between devices with their start and end apart: 7, of which 4 were waited for; matrix products, arithmetic and copies ran while one was open for 0% of the time, Pallas kernels for 0%

profile of v2, /device:TPU:0, one launch (start us, length us, event | category | flops | bytes accessed | tf_op | source)
XLA Modules:
  0.0 52.6 jit_solution(12254552978988691599)
XLA Ops:
  0.6 2.0 %shard_map.102 = bf16[8,208,128]{2,1,0:T(8,128)(2,1)} custom-call(bf16[48,1024]{1,0:T(8,128)(2,1)} %refs_0_.1, bf16[48,1024]{1,0:T(8,128)(2,1)} %refs_1_.1, bf16[48,1024]{1,0:T(8,128)(2,1)} %refs_2_.1, bf16[48,1024]{1,0:T(8,128)(2,1)} %refs_3_.1, bf16[48,1024]{1,0:T(8,128)(2,1)} %refs_4_.1, bf16[8,48]{1,0:T(8,128)(2,1)} %bitcast.11, f32[8,48]{1,0:T(8,128)} %bitcast.10), custom_call_target="tpu_custom_call" | custom-call | tf_op jit(solution)/shard_map/pallas_call | solution.py:420
  2.7 6.2 %all-to-all-start = ((bf16[8,208,128]{2,1,0:T(8,128)(2,1)}), bf16[8,208,128]{2,1,0:T(8,128)(2,1)S(1)}, u32[]{:S(2)}, u32[]{:S(2)}) async-start(bf16[8,208,128]{2,1,0:T(8,128)(2,1)} %shard_map.102), calls=%async_computation | async-start | bytes 851968 | tf_op jit(solution)/shard_map/all_to_all | solution.py:466
  8.9 8.1 %all-to-all-done.own_ref = bf16[8,208,128]{2,1,0:T(8,128)(2,1)S(1)} async-done(((bf16[8,208,128]{2,1,0:T(8,128)(2,1)}), bf16[8,208,128]{2,1,0:T(8,128)(2,1)S(1)}, u32[]{:S(2)}, u32[]{:S(2)}) %all-to-all-start) | async-done | bytes 426016 | tf_op jit(solution)/shard_map/all_to_all | solution.py:466
  17.1 1.3 %collective-permute-start.1 = (bf16[8,112,128]{2,1,0:T(8,128)(2,1)S(1)}, bf16[8,112,128]{2,1,0:T(8,128)(2,1)S(1)}, u32[]{:S(2)}, u32[]{:S(2)}) collective-permute-start(bf16[8,112,128]{2,1,0:T(8,128)(2,1)S(1)} %get-tuple-element.28), channel_id=1, source_target_pairs={{16,0},{17,1},{18,2},{19,3},{20,4},{21,5},{22,6},{23,7},{8,24},{9,... | collective-permute-start | bytes 688136 | tf_op jit(solution)/shard_map/ppermute | solution.py:450
  18.4 0.1 collective-permute-start
  18.4 1.3 %collective-permute-start.2 = (bf16[8,16,128]{2,1,0:T(8,128)(2,1)S(1)}, bf16[8,16,128]{2,1,0:T(8,128)(2,1)S(1)}, u32[]{:S(2)}, u32[]{:S(2)}) collective-permute-start(bf16[8,16,128]{2,1,0:T(8,128)(2,1)S(1)} %slice.4), channel_id=1, source_target_pairs={{17,0},{16,1},{19,2},{18,3},{21,4},{20,5},{23,6},{22,7},{9,24},{8,... | collective-permute-start | bytes 98312 | tf_op jit(solution)/shard_map/ppermute | solution.py:450
  19.8 0.1 stack.31.ids
  19.9 5.4 %collective-permute-done.2.refs_2_ = bf16[8,16,128]{2,1,0:T(8,128)(2,1)S(1)} collective-permute-done((bf16[8,16,128]{2,1,0:T(8,128)(2,1)S(1)}, bf16[8,16,128]{2,1,0:T(8,128)(2,1)S(1)}, u32[]{:S(2)}, u32[]{:S(2)}) %collective-permute-start.2) | collective-permute-done | bytes 32800 | tf_op jit(solution)/shard_map/ppermute | solution.py:450
  25.3 0.9 %collective-permute-done.1.refs_1_ = bf16[8,112,128]{2,1,0:T(8,128)(2,1)S(1)} collective-permute-done((bf16[8,112,128]{2,1,0:T(8,128)(2,1)S(1)}, bf16[8,112,128]{2,1,0:T(8,128)(2,1)S(1)}, u32[]{:S(2)}, u32[]{:S(2)}) %collective-permute-start.1) | collective-permute-done | bytes 229408 | tf_op jit(solution)/shard_map/ppermute | solution.py:450
  26.2 0.0 collective-permute-done.refs_0_
  26.2 4.1 %shard_map.103 = (f32[8,48,128]{2,1,0:T(8,128)S(1)}, f32[8,48,128]{2,1,0:T(8,128)S(1)}, f32[8,48,128]{2,1,0:T(8,128)S(1)}, f32[8,128]{1,0:T(8,128)S(1)}, f32[8,1...) custom-call(s32[7]{0:T(128)S(1)} %stack.31.ids, ...), custom_call_target="tpu_custom_call" | custom-call | tf_op jit(solution)/shard_map/pallas_call | solution.py:420
  30.4 1.3 %collective-permute-start.3 = (bf16[8,112,128]{2,1,0:T(8,128)(2,1)S(1)}, bf16[8,112,128]{2,1,0:T(8,128)(2,1)S(1)}, u32[]{:S(2)}, u32[]{:S(2)}) collective-permute-start(bf16[8,112,128]{2,1,0:T(8,128)(2,1)S(1)} %get-tuple-element.21), channel_id=1, source_target_pairs={{24,8},{25,9},{26,10},{27,11},{28,12},{29,13},{30,14},{31,15},{0,1... | collective-permute-start | bytes 688136 | tf_op jit(solution)/shard_map/ppermute | solution.py:450
  31.7 0.2 collective-permute-start.4
  31.9 1.3 %collective-permute-start.5 = (bf16[8,16,128]{2,1,0:T(8,128)(2,1)S(1)}, bf16[8,16,128]{2,1,0:T(8,128)(2,1)S(1)}, u32[]{:S(2)}, u32[]{:S(2)}) collective-permute-start(bf16[8,16,128]{2,1,0:T(8,128)(2,1)S(1)} %get-tuple-element.23), channel_id=1, source_target_pairs={{25,8},{24,9},{27,10},{26,11},{29,12},{28,13},{31,14},{30,15},{1,1... | collective-permute-start | bytes 98312 | tf_op jit(solution)/shard_map/ppermute | solution.py:450
  33.2 4.6 %collective-permute-done.5.refs_1_ = bf16[8,16,128]{2,1,0:T(8,128)(2,1)S(1)} collective-permute-done((bf16[8,16,128]{2,1,0:T(8,128)(2,1)S(1)}, bf16[8,16,128]{2,1,0:T(8,128)(2,1)S(1)}, u32[]{:S(2)}, u32[]{:S(2)}) %collective-permute-start.5) | collective-permute-done | bytes 32800 | tf_op jit(solution)/shard_map/ppermute | solution.py:450
  37.8 0.0 collective-permute-done.3.cross
  37.8 0.0 collective-permute-done.4.refs_0_
  37.8 0.7 %shard_map.104 = bf16[8,160,128]{2,1,0:T(8,128)(2,1)S(1)} custom-call(s32[7]{0:T(128)S(1)} %stack.31.ids, f32[8,48,128]{2,1,0:T(8,128)S(1)} %get-tuple-element.16.dq_ref, f32[8,48,128]{2,1,0:T(8,128)S(1)} %get-tuple-element.17.dk_ref, f32[8,48,128]{2,1,0:T(8,128)S(1)} %get-tuple-element.18.dv_ref, f32[8,128]{1,0:T(8,128)S(1)} %get-tuple-element.19.gate_ref, ...), custom_call_target="tpu_custom_call" | custom-call | tf_op jit(solution)/shard_map/pallas_call | solution.py:420
  38.5 13.3 %all_to_all.10.in_ref = bf16[8,160,128]{2,1,0:T(8,128)(2,1)S(1)} all-to-all(bf16[8,160,128]{2,1,0:T(8,128)(2,1)S(1)} %shard_map.104), channel_id=1, replica_groups={{0,2,4,6,8,10,12,14},{1,3,5,7,9,11,13,15},{16,18,20,22,24,26,28,30},{17..., dimensions={0} | all-to-all | bytes 655360 | tf_op jit(solution)/shard_map/all_to_all | solution.py:466
  51.8 0.8 %shard_map.105 = (bf16[48,1024]{1,0:T(8,128)(2,1)}, bf16[48,1024]{1,0:T(8,128)(2,1)}, bf16[48,1024]{1,0:T(8,128)(2,1)}, bf16[8,48]{1,0:T(8,128)(2,1)}) custom-call(bf16[8,160,128]{2,1,0:T(8,128)(2,1)S(1)} %all_to_all.10.in_ref), custom_call_target="tpu_custom_call" | custom-call | tf_op jit(solution)/shard_map/pallas_call | solution.py:420
  (2 shorter events, 0.0 us)
Async XLA Ops:
  2.7 14.3 %all-to-all-start = ((bf16[8,208,128]{2,1,0:T(8,128)(2,1)}), bf16[8,208,128]{2,1,0:T(8,128)(2,1)S(1)}, u32[]{:S(2)}, u32[]{:S(2)}) async-start(bf16[8,208,128]{2,1,0:T(8,128)(2,1)} %shard_map.102), calls=%async_computation | async-start | bytes 851968 | tf_op jit(solution)/shard_map/all_to_all | solution.py:466
  17.1 9.2 %collective-permute-start.1 = (bf16[8,112,128]{2,1,0:T(8,128)(2,1)S(1)}, bf16[8,112,128]{2,1,0:T(8,128)(2,1)S(1)}, u32[]{:S(2)}, u32[]{:S(2)}) collective-permute-start(bf16[8,112,128]{2,1,0:T(8,128)(2,1)S(1)} %get-tuple-element.28), channel_id=1, source_target_pairs={{16,0},{17,1},{18,2},{19,3},{20,4},{21,5},{22,6},{23,7},{8,24},{9,... | collective-permute-start | bytes 688136 | tf_op jit(solution)/shard_map/ppermute | solution.py:450
  18.4 7.9 %collective-permute-start = (bf16[8,112,128]{2,1,0:T(8,128)(2,1)S(1)}, bf16[8,112,128]{2,1,0:T(8,128)(2,1)S(1)}, u32[]{:S(2)}, u32[]{:S(2)}) collective-permute-start(bf16[8,112,128]{2,1,0:T(8,128)(2,1)S(1)} %get-tuple-element.29), channel_id=1, source_target_pairs={{1,0},{0,1},{3,2},{2,3},{5,4},{4,5},{7,6},{6,7},{9,8},{8,9},{11,10... | collective-permute-start | bytes 688136 | tf_op jit(solution)/shard_map/ppermute | solution.py:450
  18.4 6.9 %collective-permute-start.2 = (bf16[8,16,128]{2,1,0:T(8,128)(2,1)S(1)}, bf16[8,16,128]{2,1,0:T(8,128)(2,1)S(1)}, u32[]{:S(2)}, u32[]{:S(2)}) collective-permute-start(bf16[8,16,128]{2,1,0:T(8,128)(2,1)S(1)} %slice.4), channel_id=1, source_target_pairs={{17,0},{16,1},{19,2},{18,3},{21,4},{20,5},{23,6},{22,7},{9,24},{8,... | collective-permute-start | bytes 98312 | tf_op jit(solution)/shard_map/ppermute | solution.py:450
  30.4 7.5 %collective-permute-start.3 = (bf16[8,112,128]{2,1,0:T(8,128)(2,1)S(1)}, bf16[8,112,128]{2,1,0:T(8,128)(2,1)S(1)}, u32[]{:S(2)}, u32[]{:S(2)}) collective-permute-start(bf16[8,112,128]{2,1,0:T(8,128)(2,1)S(1)} %get-tuple-element.21), channel_id=1, source_target_pairs={{24,8},{25,9},{26,10},{27,11},{28,12},{29,13},{30,14},{31,15},{0,1... | collective-permute-start | bytes 688136 | tf_op jit(solution)/shard_map/ppermute | solution.py:450
  31.7 6.2 %collective-permute-start.4 = (bf16[8,112,128]{2,1,0:T(8,128)(2,1)S(1)}, bf16[8,112,128]{2,1,0:T(8,128)(2,1)S(1)}, u32[]{:S(2)}, u32[]{:S(2)}) collective-permute-start(bf16[8,112,128]{2,1,0:T(8,128)(2,1)S(1)} %get-tuple-element.22), channel_id=1, source_target_pairs={{1,0},{0,1},{3,2},{2,3},{5,4},{4,5},{7,6},{6,7},{9,8},{8,9},{11,10... | collective-permute-start | bytes 688136 | tf_op jit(solution)/shard_map/ppermute | solution.py:450
  31.9 5.9 %collective-permute-start.5 = (bf16[8,16,128]{2,1,0:T(8,128)(2,1)S(1)}, bf16[8,16,128]{2,1,0:T(8,128)(2,1)S(1)}, u32[]{:S(2)}, u32[]{:S(2)}) collective-permute-start(bf16[8,16,128]{2,1,0:T(8,128)(2,1)S(1)} %get-tuple-element.23), channel_id=1, source_target_pairs={{25,8},{24,9},{27,10},{26,11},{29,12},{28,13},{31,14},{30,15},{1,1... | collective-permute-start | bytes 98312 | tf_op jit(solution)/shard_map/ppermute | solution.py:450

commit v3 on v2

v3 whole, which is shorter than its diff:
```python
import functools
import math

import jax
import jax.numpy as jnp
from jax import lax
from jax.experimental import pallas as pl
from jax.experimental.pallas import tpu as pltpu
from jax.sharding import PartitionSpec as P

BF16 = jnp.bfloat16
F32 = jnp.float32
LANES = 128
STAT = 16
EXACT = lax.Precision.HIGHEST
VMEM = pl.BlockSpec(memory_space=pltpu.VMEM)
HBM = pl.BlockSpec(memory_space=pltpu.HBM)
PACK_LIMIT = 64


def iota(shape, dim):
    return lax.broadcasted_iota(jnp.int32, shape, dim)


def dot_exact(a, b):
    return jnp.dot(a, b, precision=EXACT, preferred_element_type=F32)


def split3(x):
    hi = x.astype(BF16).astype(F32)
    rest = x - hi
    mid = rest.astype(BF16).astype(F32)
    low = (rest - mid).astype(BF16).astype(F32)
    return hi, mid, low


def stack_rows(rows):
    at = iota((STAT, LANES), 0)
    block = jnp.zeros((STAT, LANES), F32)
    for j, row in enumerate(rows):
        block = jnp.where(at == j, jnp.broadcast_to(row, (STAT, LANES)), block)
    return block


def pad_rows(x):
    missing = LANES - x.shape[0]
    if missing:
        x = jnp.concatenate([x, jnp.zeros((missing, x.shape[1]), x.dtype)], axis=0)
    return x


def wrap(x, n):
    return jnp.where(x >= n, x - n, x)


KIND, HALF, MEMBER, BASE = range(4)


def place_of(heads, members):
    here = lax.axis_index("ctx") * lax.axis_size("head") + lax.axis_index("head")
    half = heads * members
    side = (here >= half).astype(jnp.int32)
    place = here - side * half
    member = lax.rem(place, members)
    kind = (place >= half // 2).astype(jnp.int32)
    bases = [
        jnp.where(side == other, 0, half) + wrap(member + s, members) for other in (0, 1) for s in range(members)
    ]
    return [kind, side, member, *bases]


def block_positions(bases, shape, dim, heads, stride, first, sources):
    index = iota(shape, dim)
    pos = jnp.full(shape, -1, jnp.int32)
    for at, src in enumerate(sources):
        begin = first + at * heads
        here = (index >= begin) & (index < begin + heads)
        pos = jnp.where(here, bases[src] + (index - begin) * stride, pos)
    return pos


def pack_kernel(*refs):
    sources, out_ref, refs = (refs[:7], refs[7], refs[8:])
    heads, rows = sources[5].shape
    *held, gate_wide, lse_wide, sems = refs
    copies = [pltpu.make_async_copy(src, dst, sems.at[i]) for i, (src, dst) in enumerate(zip(sources, held))]
    for i in (5, 6, 3, 4, 0, 1, 2):
        copies[i].start()
    q_ref, k_ref, v_ref, g_ref, o_ref, gate_ref, lse_ref = held
    copies[5].wait()
    copies[6].wait()
    gate_wide[...] = jnp.zeros_like(gate_wide)
    lse_wide[...] = jnp.zeros_like(lse_wide)
    gate_wide[:, 0:rows] = gate_ref[...].astype(F32)
    lse_wide[:, 0:rows] = lse_ref[...]
    copies[3].wait()
    copies[4].wait()
    lane = iota((rows, LANES), 1)
    delta = jnp.zeros((rows, LANES), F32)
    for h in range(heads):
        cols = pl.ds(h * LANES, LANES)
        grad = g_ref[:, cols]
        row_sum = jnp.sum(grad.astype(F32) * o_ref[:, cols].astype(F32), axis=1, keepdims=True)
        delta = jnp.where(lane == h, row_sum, delta)
        out_ref[h, rows : 2 * rows, :] = grad
    parts = [gate_wide[...], *split3(lse_wide[...]), *split3(pad_rows(delta).T[:heads])]
    for h in range(heads):
        block = stack_rows([part[h : h + 1] for part in parts])
        out_ref[h, 2 * rows : 2 * rows + STAT, :] = block.astype(BF16)
    for i, ref, first in ((0, q_ref, 0), (1, k_ref, 2 * rows + STAT), (2, v_ref, 3 * rows + STAT)):
        copies[i].wait()
        for h in range(heads):
            out_ref[h, first : first + rows, :] = ref[:, pl.ds(h * LANES, LANES)]


def stat_row(block, j):
    return jnp.concatenate([block[k, j : j + 1, :].astype(F32) for k in range(block.shape[0])], axis=0)


def curves(gates, rows, members, bases):
    heads = gates[0].shape[0]
    in_row = iota((heads, LANES), 1) < rows
    logs = [
        jnp.where(in_row, jnp.minimum(x, 0.0) - jnp.log1p(jnp.exp(-jnp.abs(x))), 0.0) for x in gates
    ]
    logs = jnp.concatenate(logs, axis=0)
    square = (LANES, LANES)
    upto = (iota(square, 0) <= iota(square, 1)).astype(F32)
    shape = (members * heads, members * heads)
    row_pos = block_positions(bases, shape, 0, heads, members, 0, range(members))
    lane_pos = block_positions(bases, shape, 1, heads, members, 0, range(members))
    before = jnp.sum(dot_exact((lane_pos < row_pos).astype(F32), logs), axis=1, keepdims=True)
    curve = dot_exact(logs, upto) + before
    return [curve[s * heads : (s + 1) * heads] for s in range(members)], jnp.sum(logs)


def extra_columns(rows, scale, queries, keys):
    heads = (queries or keys)[0][0].shape[0]
    zero = jnp.zeros((heads, LANES), F32)
    score_cols, delta_cols = [], []
    for m in range(-(-max(len(queries), len(keys)) // 2)):
        q_rows, d_rows, k_rows = [], [], []
        for s in (2 * m, 2 * m + 1):
            if s < len(queries):
                curve, block = queries[s]
                lse = stat_row(block, 1) + stat_row(block, 2) + stat_row(block, 3)
                q_rows += [*split3((curve - lse) / scale), zero]
                d_rows += [-stat_row(block, 4), -stat_row(block, 5), -stat_row(block, 6), zero]
            else:
                q_rows += [zero] * 4
                d_rows += [zero] * 4
            k_rows += [*split3(-keys[s][0] / scale), zero] if s < len(keys) else [zero] * 4
        score_cols.append(jnp.concatenate(q_rows + k_rows, axis=0).T[:rows])
        if queries:
            delta_cols.append(pad_rows(jnp.concatenate(d_rows, axis=0)).T[:rows])
    return score_cols, delta_cols


def lay_out(rows, heads, columns, sides):
    score_cols, delta_cols = columns
    lane = iota((rows, LANES), 1)
    half = 8 * heads
    upper = (lane >= half).astype(F32)
    lower = (lane < half).astype(F32)
    ones = jnp.ones((rows, LANES), BF16)
    for query, sources, place, first, second in sides:
        for k in range(heads):
            for s, (array, begin) in enumerate(sources):
                at = place(k, s)
                inner = lane - (s % 2) * 4 * heads - (0 if query else half)
                mine = (inner >= 0) & (inner < 4 * heads) & (lane % heads == k)
                score = jnp.where(mine, score_cols[s // 2], upper if query else lower)
                first[at, 0:LANES] = array[k, begin : begin + rows, :]
                first[at, LANES:] = score.astype(BF16)
                second[at, 0:LANES] = array[k, begin + rows : begin + 2 * rows, :]
                if query:
                    second[at, LANES:] = jnp.where(mine, delta_cols[s // 2], 0.0).astype(BF16)
                else:
                    second[at, LANES:] = ones


def tile(scale, key, value, query, grad, allowed):
    nt = (((1,), (1,)), ((), ()))
    tn = (((0,), (0,)), ((), ()))
    scores = lax.dot_general(key, query, nt, preferred_element_type=F32)
    shifted = lax.dot_general(value, grad, nt, preferred_element_type=F32)
    probs = jnp.exp2(scores * (scale * math.log2(math.e)))
    if allowed is not None:
        probs = jnp.where(allowed, probs, 0.0)
    grads = (probs * shifted).astype(BF16)
    dk = jnp.dot(grads, query, preferred_element_type=F32)
    dq = lax.dot_general(grads, key, tn, preferred_element_type=F32)
    dv = jnp.dot(probs.astype(BF16), grad[:, 0:LANES], preferred_element_type=F32)
    return dk, dq, dv


class Sums:
    def __init__(self, ref, step, start=None):
        self.ref, self.step, self.start, self.seen = ref, step, start, set()

    def add(self, begin, value):
        for first in range(0, value.shape[0], self.step):
            at = pl.ds(begin + first, self.step)
            part = value[first : first + self.step]
            if begin + first in self.seen:
                part = self.ref[at, :] + part
            elif self.start is not None:
                part = self.start[at, :] + part
            self.ref[at, :] = part
            self.seen.add(begin + first)


def full_place(place, rows, members):
    def at(k, s):
        begin = (k * members + wrap(place[MEMBER] + s, members)) * rows
        return pl.ds(pl.multiple_of(begin, math.gcd(rows, LANES)), rows)

    return at


def some_place(rows):
    return lambda k, s: pl.ds(k * rows, rows)


def own_kernel(plan, own_ref, *refs):
    rows, heads, members, scale = plan
    peers, outs, scratch = (refs[: members - 1], refs[members - 1 : members + 5], refs[members + 5 :])
    place = place_of(heads, members)
    for kind in (0, 1):

        @pl.when(place[KIND] == kind)
        def _(kind=kind):
            own_body(plan, kind, place, own_ref, peers, outs, scratch)


def own_body(plan, kind, place, own_ref, peers, outs, scratch):
    rows, heads, members, scale = plan
    full_1, full_2, full_acc, some_acc, value_acc, total_ref = outs
    some_1, some_2 = scratch
    stat_at = 2 * rows
    peer_stat = 0 if kind == 0 else stat_at
    blocks = [own_ref[:, stat_at : stat_at + STAT, :].astype(F32)]
    blocks += [ref[:, peer_stat : peer_stat + STAT, :].astype(F32) for ref in peers]
    curve, total = curves([stat_row(block, 0) for block in blocks], rows, members, place[BASE:])
    total_ref[...] = jnp.full(total_ref.shape, total, F32)
    every = list(zip(curve, blocks))
    full_at, some_at = (full_place(place, rows, members), some_place(rows))
    keys_at = stat_at + STAT
    if kind == 0:
        columns = extra_columns(rows, scale, every[:1], every)
        query_sources = [(own_ref, 0)]
        key_sources = [(own_ref, keys_at)] + [(ref, STAT) for ref in peers]
        (k_1, k_2, k_acc, k_at), (q_1, q_2, q_acc, q_at) = (
            (full_1, full_2, full_acc, full_at),
            (some_1, some_2, some_acc, some_at),
        )
    else:
        columns = extra_columns(rows, scale, every, every[:1])
        query_sources = [(own_ref, 0)] + [(ref, 0) for ref in peers]
        key_sources = [(own_ref, keys_at)]
        (q_1, q_2, q_acc, q_at), (k_1, k_2, k_acc, k_at) = (
            (full_1, full_2, full_acc, full_at),
            (some_1, some_2, some_acc, some_at),
        )
    sides = [(True, query_sources, q_at, q_1, q_2), (False, key_sources, k_at, k_1, k_2)]
    lay_out(rows, heads, columns, sides)
    own_rows, slot_rows = (heads * rows, members * rows)

    def full_pos(shape, dim, begin):
        return iota(shape, dim) + begin

    def some_pos(shape, dim, begin):
        index = iota(shape, dim) + begin
        pos = index + place[MEMBER] * rows
        for k in range(1, heads):
            pos = jnp.where(index >= k * rows, pos + (slot_rows - rows), pos)
        return pos

    def product(keys, queries, causal):
        allowed = None
        if causal:
            k_pos, q_pos = ((full_pos, some_pos) if kind == 0 else (some_pos, full_pos))
            allowed = k_pos((keys[1], 1), 0, keys[0]) <= q_pos((1, queries[1]), 1, queries[0])
        k_rows, q_rows = (pl.ds(*keys), pl.ds(*queries))
        return tile(scale, k_1[k_rows, :], k_2[k_rows, :], q_1[q_rows, :], q_2[q_rows, :], allowed)

    if members == 2:
        part = own_rows // 2
        sums = [Sums(k_acc, part), Sums(q_acc, part), Sums(value_acc, part)]

        def add(keys, queries, causal):
            dk, dq, dv = product(keys, queries, causal)
            sums[0].add(keys[0], dk)
            sums[1].add(queries[0], dq)
            sums[2].add(keys[0], dv)

        if kind == 0:
            for i in range(4):
                add((i * part, part), (0, own_rows) if i < 2 else (part, part), True)
        else:
            add((0, part), (0, own_rows), True)
            add((0, part), (own_rows, own_rows), False)
            add((part, part), (own_rows, own_rows), True)
    else:
        full_acc[...] = jnp.zeros_like(full_acc)
        some_acc[...] = jnp.zeros_like(some_acc)
        value_acc[...] = jnp.zeros_like(value_acc)

        @pl.loop(0, heads)
        def _(k):
            full = (pl.multiple_of(k * slot_rows, math.gcd(slot_rows, LANES)), slot_rows)
            keys, queries = ((full, (0, own_rows)) if kind == 0 else ((0, own_rows), full))
            dk, dq, dv = product(keys, queries, True)
            k_acc[pl.ds(*keys), :] += dk
            q_acc[pl.ds(*queries), :] += dq
            value_acc[pl.ds(*keys), :] += dv


def square_kernel(plan, *refs):
    rows, heads, members, scale = plan
    chunks = -(-members // 8)
    cut = 7 + members - 1
    ins, outs, scratch = (
        refs[:cut],
        refs[cut : cut + 4 + members - 1 + chunks],
        refs[cut + 4 + members - 1 + chunks :],
    )
    place = place_of(heads, members)
    for kind in (0, 1):

        @pl.when(place[KIND] == kind)
        def _(kind=kind):
            square_body(plan, kind, place, ins, outs, scratch)


def square_body(plan, kind, place, ins, outs, scratch):
    rows, heads, members, scale = plan
    full_1, full_2, full_in, some_in, value_in, total_ref, cross, *corner = ins
    dq_own, dk_own, dv_own, to_cross = outs[:4]
    to_peer, sums_refs = (outs[4 : 3 + members], outs[3 + members :])
    cross_1, cross_2, full_acc, cross_acc, value_acc = scratch
    own_rows = heads * rows
    full_rows = own_rows * members
    full_at, some_at = (full_place(place, rows, members), some_place(rows))
    wanted = place[HALF] == kind

    @pl.when(wanted)
    def _():
        stat_at = 2 * rows if kind == 0 else 0
        block = cross[:, stat_at : stat_at + STAT, :].astype(F32)
        gates = [stat_row(block, 0)] + [ref[...].astype(F32) for ref in corner]
        curve, total = curves(gates, rows, members, place[BASE + members :])
        if kind == 0:
            columns = extra_columns(rows, scale, [(curve[0] + total_ref[...], block)], [])
            side = (True, [(cross, 0)], some_at, cross_1, cross_2)
        else:
            columns = extra_columns(rows, scale, [], [(curve[0] - total, block)])
            side = (False, [(cross, STAT)], some_at, cross_1, cross_2)
        lay_out(rows, heads, columns, [side])
        if members == 2:
            part = own_rows // 2
            full_sums = Sums(full_acc, part, full_in)
            cross_sums = Sums(cross_acc, part)
            if kind == 0:
                value_sums = Sums(value_acc, part, value_in)
                for i in range(4):
                    at = pl.ds(i * part, part)
                    dk, dq, dv = tile(
                        scale, full_1[at, :], full_2[at, :], cross_1[...], cross_2[...], None
                    )
                    full_sums.add(i * part, dk)
                    cross_sums.add(0, dq)
                    value_sums.add(i * part, dv)
            else:
                value_acc[0:own_rows, :] = value_in[0:own_rows, :]
                value_sums = Sums(value_acc, part)
                for i in (0, 1):
                    for j in (0, 1):
                        k_rows, q_rows = (pl.ds(i * part, part), pl.ds(j * own_rows, own_rows))
                        dk, dq, dv = tile(
                            scale,
                            cross_1[k_rows, :],
                            cross_2[k_rows, :],
                            full_1[q_rows, :],
                            full_2[q_rows, :],
                            None,
                        )
                        cross_sums.add(i * part, dk)
                        full_sums.add(j * own_rows, dq)
                        value_sums.add(own_rows + i * part, dv)
        else:
            full_acc[...] = full_in[...]
            value_acc[...] = value_in[...]
            cross_acc[...] = jnp.zeros_like(cross_acc)
            if kind == 1:
                value_acc[pl.ds(own_rows, own_rows), :] = jnp.zeros((own_rows, LANES), F32)
            slot_rows = members * rows

            @pl.loop(0, heads)
            def _(k):
                at = pl.ds(pl.multiple_of(k * slot_rows, math.gcd(slot_rows, LANES)), slot_rows)
                if kind == 0:
                    dk, dq, dv = tile(
                        scale, full_1[at, :], full_2[at, :], cross_1[...], cross_2[...], None
                    )
                    full_acc[at, :] += dk
                    cross_acc[...] += dq
                    value_acc[at, :] += dv
                else:
                    dk, dq, dv = tile(
                        scale, cross_1[...], cross_2[...], full_1[at, :], full_2[at, :], None
                    )
                    cross_acc[...] += dk
                    full_acc[at, :] += dq
                    value_acc[pl.ds(own_rows, own_rows), :] += dv

    @pl.when(jnp.logical_not(wanted))
    def _():
        full_acc[...] = full_in[...]
        cross_acc[...] = jnp.zeros_like(cross_acc)
        value_acc[...] = value_in[...]
        if kind == 1:
            value_acc[pl.ds(own_rows, own_rows), :] = jnp.zeros((own_rows, LANES), F32)

    def some_ref(s):
        return some_in if s == 0 else cross_acc

    def full_grad(k, s, lanes):
        return full_acc[full_at(k, s), lanes]

    def some_grad(k, s, lanes):
        return some_ref(s)[some_at(k, s), lanes]

    (query_grad, key_grad) = (some_grad, full_grad) if kind == 0 else (full_grad, some_grad)
    query_count, key_count = ((2, members) if kind == 0 else (members, 2))
    low, high = (slice(0, LANES), slice(LANES, 2 * LANES))

    def value_grad(k, s):
        if kind == 0:
            return value_acc[full_at(k, s), :]
        return value_acc[pl.ds((s * heads + k) * rows, rows), :]

    lane = iota((rows, LANES), 1)
    half = 8 * heads
    for m, sums_ref in enumerate(sums_refs):
        sums = jnp.zeros((rows, LANES), F32)
        for k in range(heads):
            for s in range(8 * m, min(8 * m + 8, query_count)):
                at = (s - 8 * m) * heads + k
                sums = jnp.where(lane == at, query_grad(k, s, high), sums)
            for s in range(8 * m, min(8 * m + 8, key_count)):
                at = half + (s - 8 * m) * heads + k
                sums = jnp.where(lane == at, -key_grad(k, s, high), sums)
        sums_ref[...] = sums
    blank = jnp.zeros((rows, LANES), BF16)
    for k in range(heads):
        dq_own[k] = query_grad(k, 0, low)
        dk_own[k] = key_grad(k, 0, low)
        dv_own[k] = value_grad(k, 0)
        sends = [(to_cross, 1, kind == 1)]
        sends += [(to_peer[s - 1], s, kind == 0) for s in range(1, members)]
        for ref, s, keys in sends:
            ref[k, 0:rows, :] = (key_grad(k, s, low) if keys else query_grad(k, s, low)).astype(BF16)
            ref[k, rows : 2 * rows, :] = value_grad(k, s).astype(BF16) if keys else blank


def suffix_kernel(plan, *refs):
    rows, heads, members, scale = plan
    chunks = -(-members // 8)
    sums_refs, outs = (refs[:chunks], refs[chunks:])
    place = place_of(heads, members)
    bases = place[BASE:]
    first_kind = place[KIND] == 0
    count = 2 * members
    half = 8 * heads
    square = (LANES, LANES)
    shape = (count * heads, LANES)
    target_pos = block_positions(bases, shape, 0, heads, members, 0, range(count))
    onward = (iota(square, 0) >= iota(square, 1)).astype(F32)
    later, inner = (jnp.zeros(shape, F32), jnp.zeros(shape, F32))
    pair = [0, members]
    for m, sums_ref in enumerate(sums_refs):
        turned = pad_rows(sums_ref[...]).T
        some = pair if m == 0 else []
        full = range(8 * m, min(8 * m + 8, members))
        slot_pos = [
            jnp.maximum(
                block_positions(bases, (8, LANES), 1, heads, members, 0, queries),
                block_positions(bases, (8, LANES), 1, heads, members, half, keys),
            )[0:1]
            for queries, keys in ((some, full), (full, some))
        ]
        slot_pos = jnp.where(first_kind, slot_pos[0], slot_pos[1])
        later += dot_exact((slot_pos > target_pos).astype(F32), turned)
        inner += dot_exact((slot_pos == target_pos).astype(F32), turned)
    suffix = jnp.sum(later, axis=1, keepdims=True) + dot_exact(inner, onward)
    for src, ref in enumerate(outs):
        ref[...] = suffix[src * heads : (src + 1) * heads]


def combine_kernel(plan, dq_ref, dk_ref, dv_ref, cross, *refs):
    rows, heads, members, scale = plan
    peers, gate_refs, out_ref = (refs[: members - 1], refs[members - 1 : -1], refs[-1])
    first_kind = place_of(heads, members)[KIND] == 0
    gates = gate_refs[0][...]
    for ref in gate_refs[1:]:
        gates += ref[...]
    gates = split3(gates)
    for k in range(heads):
        far = cross[k].astype(F32)
        near = peers[0][k].astype(F32)
        for ref in peers[1:]:
            near += ref[k].astype(F32)
        to_keys = jnp.where(first_kind, near, far)
        to_queries = jnp.where(first_kind, far[0:rows], near[0:rows])
        out_ref[k, 0:rows, :] = (scale * (dq_ref[k] + to_queries)).astype(BF16)
        out_ref[k, rows : 2 * rows, :] = (scale * (dk_ref[k] + to_keys[0:rows])).astype(BF16)
        out_ref[k, 2 * rows : 3 * rows, :] = (dv_ref[k] + to_keys[rows:]).astype(BF16)
        out_ref[k, 3 * rows :, :] = stack_rows([part[k : k + 1] for part in gates]).astype(BF16)


def unpack_kernel(in_ref, keep_ref, dq_ref, dk_ref, dv_ref, gate_ref):
    rows = dq_ref.shape[0]
    heads = in_ref.shape[0]
    gates = []
    for h in range(heads):
        cols = pl.ds(h * LANES, LANES)
        dq_ref[:, cols] = in_ref[h, 0:rows, :]
        dk_ref[:, cols] = in_ref[h, rows : 2 * rows, :]
        dv_ref[:, cols] = in_ref[h, 2 * rows : 3 * rows, :]
        gates.append(jnp.sum(in_ref[h, 3 * rows :, :].astype(F32), axis=0, keepdims=True))
    gate_ref[...] = (jnp.concatenate(gates, axis=0)[:, 0:rows] * keep_ref[...]).astype(BF16)


def struct(shape, dtype=BF16):
    return jax.ShapeDtypeStruct(shape, dtype)


def call(kernel, out_shape, inputs, scratch=(), space=VMEM, limit=40):
    return pl.pallas_call(
        kernel,
        out_shape=out_shape,
        in_specs=[space] * len(inputs),
        out_specs=jax.tree.map(lambda _: VMEM, out_shape),
        scratch_shapes=list(scratch),
        compiler_params=pltpu.CompilerParams(vmem_limit_bytes=int(limit * 1024 * 1024)),
    )(*inputs)


def per_device(queries, key_inputs, value_inputs, out_grad, attn_output, gate_logits, lse):
    ctx, group = (lax.axis_size("ctx"), lax.axis_size("head"))
    rows, heads = gate_logits.shape
    width = queries.shape[1]
    scale = (width // heads) ** -0.5
    half = ctx * group // 2
    members = half // heads
    both = ("ctx", "head")

    def device(side, slot, member):
        return side * half + slot * members + member

    def shift(array, across, along, chosen):
        pairs = [
            (device(side ^ across, slot, (member + along) % members), device(side, slot, member))
            for side in (0, 1)
            for slot in range(heads)
            for member in range(members)
            if chosen(side, int(slot >= heads // 2))
        ]
        return lax.ppermute(array, both, pairs)

    def everyone(side, kind):
        return True

    def working(side, kind):
        return side == kind

    def waiting(side, kind):
        return side != kind

    regions = [
        [device(side, slot, member) for slot in range(heads)] for side in (0, 1) for member in range(members)
    ]

    def exchange(array):
        return lax.all_to_all(
            array, both, split_axis=0, concat_axis=0, axis_index_groups=regions, tiled=True
        )

    kind = place_of(heads, members)[KIND]

    packed = call(
        pack_kernel,
        struct((heads, 4 * rows + STAT, LANES)),
        (queries, key_inputs, value_inputs, out_grad, attn_output, gate_logits.T, lse.T),
        scratch=[pltpu.VMEM((rows, width), BF16)] * 5
        + [pltpu.VMEM((heads, rows), BF16), pltpu.VMEM((heads, rows), F32)]
        + [pltpu.VMEM((heads, LANES), F32)] * 2
        + [pltpu.SemaphoreType.DMA((7,))],
        space=HBM,
        limit=PACK_LIMIT,
    )
    own = exchange(packed)
    length = 2 * rows + STAT

    def part(keys):
        return lax.dynamic_slice_in_dim(own, jnp.where(keys, 2 * rows, 0), length, axis=1)

    cross_send, peer_send = (part(kind == 1), part(kind == 0))
    gate_send = own[:, 2 * rows]
    cross = shift(cross_send, 1, 0, working)
    peers = [shift(peer_send, 0, s, everyone) for s in range(1, members)]
    corner = [shift(gate_send, 1, s, working) for s in range(1, members)]

    plan = (rows, heads, members, scale)
    own_rows, full_rows = (heads * rows, heads * members * rows)
    value_rows = max(full_rows, 2 * own_rows)
    wide = 2 * LANES
    small = struct((heads, LANES), F32)
    state = call(
        functools.partial(own_kernel, plan),
        [
            struct((full_rows, wide)),
            struct((full_rows, wide)),
            struct((full_rows, wide), F32),
            struct((own_rows, wide), F32),
            struct((value_rows, LANES), F32),
            small,
        ],
        (own, *peers),
        scratch=[pltpu.VMEM((own_rows, wide), BF16)] * 2,
    )
    piece = struct((heads, rows, LANES), F32)
    sent = struct((heads, 2 * rows, LANES))
    chunks = -(-members // 8)
    dq, dk, dv, to_cross, *others = call(
        functools.partial(square_kernel, plan),
        [piece, piece, piece, sent] + [sent] * (members - 1) + [struct((rows, LANES), F32)] * chunks,
        (*state, cross, *corner),
        scratch=[pltpu.VMEM((own_rows, wide), BF16)] * 2
        + [
            pltpu.VMEM((full_rows, wide), F32),
            pltpu.VMEM((own_rows, wide), F32),
            pltpu.VMEM((value_rows, LANES), F32),
        ],
    )
    to_peer, sums = (others[: members - 1], others[members - 1 :])
    cross = shift(to_cross, 1, 0, waiting)
    peers = [shift(to_peer[s - 1], 0, members - s, everyone) for s in range(1, members)]
    gates = call(functools.partial(suffix_kernel, plan), [small] * (2 * members), tuple(sums))
    gates = (
        [gates[0]]
        + [shift(gates[s], 0, members - s, everyone) for s in range(1, members)]
        + [shift(gates[members + s], 1, (members - s) % members, waiting) for s in range(members)]
    )
    summed = call(
        functools.partial(combine_kernel, plan),
        struct((heads, 3 * rows + STAT, LANES)),
        (dq, dk, dv, cross, *peers, *gates),
    )
    final = exchange(summed)
    keep = jax.nn.sigmoid(-gate_logits.T.astype(F32))
    full = struct(queries.shape)
    dq, dk, dv, gate_grad = call(unpack_kernel, [full, full, full, struct((heads, rows))], (final, keep))
    return dq, dk, dv, gate_grad.T


def solution(mesh):
    split = P(("ctx", "head"), None)
    return jax.shard_map(
        per_device,
        mesh=mesh,
        in_specs=(split,) * 7,
        out_specs=(split,) * 4,
        check_vma=False,
    )
```

time: 52.9 us -> 51.5 us (0.974)
  blocking collectives: 13.3 us -> 0 us
  starting transfers between devices: 11.7 us -> 19 us
  waiting for transfers between devices: 19.1 us -> 23.3 us
    all_to_all x1 -> x0, blocking collectives: 13.3 us -> none  [exchange(): lax.all_to_all(array, both, split_axis=0, concat_axis=0, axis_index_group...]
    all_to_all x1 -> x2, waiting for transfers between devices: 8.15 us -> 15.6 us  [exchange(): lax.all_to_all(array, both, split_axis=0, concat_axis=0, axis_index_group...]
    all_to_all x1 -> x2, starting transfers between devices: 6.2 us -> 11.9 us  [exchange(): lax.all_to_all(array, both, split_axis=0, concat_axis=0, axis_index_group...]
    ppermute x6 -> x8, waiting for transfers between devices: 10.9 us -> 7.65 us  [shift(): return lax.ppermute(array, both, pairs)]
    ppermute x6 -> x8, starting transfers between devices: 5.48 us -> 7.15 us  [shift(): return lax.ppermute(array, both, pairs)]
    pallas_call x4 -> x6, Pallas kernels: 7.6 us -> 7.97 us  [call(): pl.pallas_call(kernel, out_shape=out_shape, in_specs=[space] * len(inputs...]
  transfers between devices with their start and end apart: 7 -> 10, of which waited for: 4 -> 5; matrix products, arithmetic and copies ran while one was open for 0% -> 0% of each run, Pallas kernels for 0% -> 4%
where the time goes in v3:
time: 51.5 us; the launch traced here: 51.1 us
  waiting for transfers between devices  23.3 us (45%)
  starting transfers between devices  19 us (37%)
  Pallas kernels  7.97 us (15%)
  between operations  0.75 us (1%)
    all_to_all x2, waiting for transfers between devices, exchange(): lax.all_to_all(array, both, split_axis=0, concat_axis=0, axis_index_group...  15.6 us
    all_to_all x2, starting transfers between devices, exchange(): lax.all_to_all(array, both, split_axis=0, concat_axis=0, axis_index_group...  11.9 us
    pallas_call x6, Pallas kernels, call(): pl.pallas_call(kernel, out_shape=out_shape, in_specs=[space] * len(inputs...  7.97 us
    ppermute x8, waiting for transfers between devices, shift(): return lax.ppermute(array, both, pairs)  7.65 us
    ppermute x8, starting transfers between devices, shift(): return lax.ppermute(array, both, pairs)  7.15 us
  transfers between devices with their start and end apart: 10, of which 5 were waited for; matrix products, arithmetic and copies ran while one was open for 0% of the time, Pallas kernels for 4%

profile of v3, /device:TPU:0, one launch (start us, length us, event | category | flops | bytes accessed | tf_op | source)
XLA Modules:
  0.0 51.1 jit_solution(9461166954615407174)
XLA Ops:
  0.6 2.0 %shard_map.102 = bf16[8,208,128]{2,1,0:T(8,128)(2,1)} custom-call(bf16[48,1024]{1,0:T(8,128)(2,1)} %refs_0_.1, bf16[48,1024]{1,0:T(8,128)(2,1)} %refs_1_.1, bf16[48,1024]{1,0:T(8,128)(2,1)} %refs_2_.1, bf16[48,1024]{1,0:T(8,128)(2,1)} %refs_3_.1, bf16[48,1024]{1,0:T(8,128)(2,1)} %refs_4_.1, bf16[8,48]{1,0:T(8,128)(2,1)} %bitcast.7, f32[8,48]{1,0:T(8,128)} %bitcast.8), custom_call_target="tpu_custom_call" | custom-call | tf_op jit(solution)/shard_map/pallas_call | solution.py:540
  2.7 6.2 %all-to-all-start = ((bf16[8,208,128]{2,1,0:T(8,128)(2,1)}), bf16[8,208,128]{2,1,0:T(8,128)(2,1)S(1)}, u32[]{:S(2)}, u32[]{:S(2)}) async-start(bf16[8,208,128]{2,1,0:T(8,128)(2,1)} %shard_map.102), calls=%async_computation | async-start | bytes 851968 | tf_op jit(solution)/shard_map/all_to_all | solution.py:586
  8.9 8.1 %all-to-all-done.own_ref = bf16[8,208,128]{2,1,0:T(8,128)(2,1)S(1)} async-done(((bf16[8,208,128]{2,1,0:T(8,128)(2,1)}), bf16[8,208,128]{2,1,0:T(8,128)(2,1)S(1)}, u32[]{:S(2)}, u32[]{:S(2)}) %all-to-all-start) | async-done | bytes 426016 | tf_op jit(solution)/shard_map/all_to_all | solution.py:586
  17.1 0.1 collective-permute-start
  17.1 1.3 %collective-permute-start.1 = (bf16[8,112,128]{2,1,0:T(8,128)(2,1)S(1)}, bf16[8,112,128]{2,1,0:T(8,128)(2,1)S(1)}, u32[]{:S(2)}, u32[]{:S(2)}) collective-permute-start(bf16[8,112,128]{2,1,0:T(8,128)(2,1)S(1)} %get-tuple-element.44), channel_id=1, source_target_pairs={{16,0},{17,1},{18,2},{19,3},{20,4},{21,5},{22,6},{23,7},{8,24},{9,... | collective-permute-start | bytes 688136 | tf_op jit(solution)/shard_map/ppermute | solution.py:570
  18.5 1.3 %collective-permute-start.2 = (bf16[8,128]{1,0:T(8,128)(2,1)S(1)}, bf16[8,128]{1,0:T(8,128)(2,1)S(1)}, u32[]{:S(2)}, u32[]{:S(2)}) collective-permute-start(bf16[8,128]{1,0:T(8,128)(2,1)S(1)} %bitcast.9), channel_id=1, source_target_pairs={{17,0},{16,1},{19,2},{18,3},{21,4},{20,5},{23,6},{22,7},{9,24},{8,... | collective-permute-start | bytes 6152 | tf_op jit(solution)/shard_map/ppermute | solution.py:570
  19.8 0.0 collective-permute-done.refs_0_
  19.8 1.9 %shard_map.103 = (bf16[768,256]{1,0:T(8,128)(2,1)S(1)}, bf16[768,256]{1,0:T(8,128)(2,1)S(1)}, f32[768,256]{1,0:T(8,128)S(1)}, f32[384,256]{1,0:T(8,128)S(1)}, f3...) custom-call(bf16[8,208,128]{2,1,0:T(8,128)(2,1)S(1)} %all-to-all-done.own_ref, ...), custom_call_target="tpu_custom_call" | custom-call | tf_op jit(solution)/shard_map/pallas_call | solution.py:540
  21.6 5.9 %collective-permute-done.2.refs_7_ = bf16[8,128]{1,0:T(8,128)(2,1)S(1)} collective-permute-done((bf16[8,128]{1,0:T(8,128)(2,1)S(1)}, bf16[8,128]{1,0:T(8,128)(2,1)S(1)}, u32[]{:S(2)}, u32[]{:S(2)}) %collective-permute-start.2) | collective-permute-done | bytes 2080 | tf_op jit(solution)/shard_map/ppermute | solution.py:570
  27.6 0.4 collective-permute-done.1.refs_6_
  28.0 2.1 %shard_map.104 = (f32[8,48,128]{2,1,0:T(8,128)S(1)}, f32[8,48,128]{2,1,0:T(8,128)S(1)}, f32[8,48,128]{2,1,0:T(8,128)S(1)}, bf16[8,96,128]{2,1,0:T(8,128)(2,1)S(1...) custom-call(bf16[768,256]{1,0:T(8,128)(2,1)S(1)} %get-tuple-element.24.refs_0_, ...), custom_call_target="tpu_custom_call" | custom-call | tf_op jit(solution)/shard_map/pallas_call | solution.py:540
  30.1 1.3 %collective-permute-start.3 = (bf16[8,96,128]{2,1,0:T(8,128)(2,1)S(1)}, bf16[8,96,128]{2,1,0:T(8,128)(2,1)S(1)}, u32[]{:S(2)}, u32[]{:S(2)}) collective-permute-start(bf16[8,96,128]{2,1,0:T(8,128)(2,1)S(1)} %get-tuple-element.33), channel_id=1, source_target_pairs={{24,8},{25,9},{26,10},{27,11},{28,12},{29,13},{30,14},{31,15},{0,1... | collective-permute-start | bytes 589832 | tf_op jit(solution)/shard_map/ppermute | solution.py:570
  31.4 0.2 collective-permute-start.4
  31.6 0.3 shard_map.105
  31.9 0.4 collective-permute-start.5
  32.3 1.3 %collective-permute-start.6 = (f32[8,128]{1,0:T(8,128)S(1)}, f32[8,128]{1,0:T(8,128)S(1)}, u32[]{:S(2)}, u32[]{:S(2)}) collective-permute-start(f32[8,128]{1,0:T(8,128)S(1)} %get-tuple-element.38), channel_id=1, source_target_pairs={{24,8},{25,9},{26,10},{27,11},{28,12},{29,13},{30,14},{31,15},{0,1... | collective-permute-start | bytes 12296 | tf_op jit(solution)/shard_map/ppermute | solution.py:570
  33.6 1.3 %collective-permute-start.7 = (f32[8,128]{1,0:T(8,128)S(1)}, f32[8,128]{1,0:T(8,128)S(1)}, u32[]{:S(2)}, u32[]{:S(2)}) collective-permute-start(f32[8,128]{1,0:T(8,128)S(1)} %get-tuple-element.39), channel_id=1, source_target_pairs={{25,8},{24,9},{27,10},{26,11},{29,12},{28,13},{31,14},{30,15},{1,1... | collective-permute-start | bytes 12296 | tf_op jit(solution)/shard_map/ppermute | solution.py:570
  34.9 0.0 collective-permute-done.5.refs_2_
  34.9 1.3 %collective-permute-done.6.refs_3_ = f32[8,128]{1,0:T(8,128)S(1)} collective-permute-done((f32[8,128]{1,0:T(8,128)S(1)}, f32[8,128]{1,0:T(8,128)S(1)}, u32[]{:S(2)}, u32[]{:S(2)}) %collective-permute-start.6) | collective-permute-done | bytes 4128 | tf_op jit(solution)/shard_map/ppermute | solution.py:570
  36.2 0.0 collective-permute-done.7.refs_4_
  36.3 0.0 collective-permute-done.3.cross
  36.3 0.0 collective-permute-done.4.refs_0_
  36.3 0.8 %shard_map.106 = bf16[8,160,128]{2,1,0:T(8,128)(2,1)} custom-call(f32[8,48,128]{2,1,0:T(8,128)S(1)} %get-tuple-element.30.dq_ref, f32[8,48,128]{2,1,0:T(8,128)S(1)} %get-tuple-element.31.dk_ref, f32[8,48,128]{2,1,0:T(8,128)S(1)} %get-tuple-element.32.dv_ref, bf16[8,96,128]{2,1,0:T(8,128)(2,1)S(1)} %collective-permute-done.3.cross, ...), custom_call_target="tpu_custom_call" | custom-call | tf_op jit(solution)/shard_map/pallas_call | solution.py:540
  37.1 0.0 copy-start
  37.1 5.7 %all-to-all-start.1 = ((bf16[8,160,128]{2,1,0:T(8,128)(2,1)}), bf16[8,160,128]{2,1,0:T(8,128)(2,1)S(1)}, u32[]{:S(2)}, u32[]{:S(2)}) async-start(bf16[8,160,128]{2,1,0:T(8,128)(2,1)} %shard_map.106), calls=%async_computation.1 | async-start | bytes 655360 | tf_op jit(solution)/shard_map/all_to_all | solution.py:586
  42.8 0.0 copy-done
  42.8 7.5 %all-to-all-done.1.in_ref = bf16[8,160,128]{2,1,0:T(8,128)(2,1)S(1)} async-done(((bf16[8,160,128]{2,1,0:T(8,128)(2,1)}), bf16[8,160,128]{2,1,0:T(8,128)(2,1)S(1)}, u32[]{:S(2)}, u32[]{:S(2)}) %all-to-all-start.1) | async-done | bytes 327712 | tf_op jit(solution)/shard_map/all_to_all | solution.py:586
  50.3 0.8 %shard_map.107 = (bf16[48,1024]{1,0:T(8,128)(2,1)}, bf16[48,1024]{1,0:T(8,128)(2,1)}, bf16[48,1024]{1,0:T(8,128)(2,1)}, bf16[8,48]{1,0:T(8,128)(2,1)}) custom-call(bf16[8,160,128]{2,1,0:T(8,128)(2,1)S(1)} %all-to-all-done.1.in_ref, f32[8,48]{1,0:T(8,128)S(1)} %add_divide_fusion.keep_ref), custom_call_target="tpu_custom_call" | custom-call | tf_op jit(solution)/shard_map/pallas_call | solution.py:540
  (4 shorter events, 0.1 us)
Async XLA Ops:
  2.7 14.3 %all-to-all-start = ((bf16[8,208,128]{2,1,0:T(8,128)(2,1)}), bf16[8,208,128]{2,1,0:T(8,128)(2,1)S(1)}, u32[]{:S(2)}, u32[]{:S(2)}) async-start(bf16[8,208,128]{2,1,0:T(8,128)(2,1)} %shard_map.102), calls=%async_computation | async-start | bytes 851968 | tf_op jit(solution)/shard_map/all_to_all | solution.py:586
  17.1 2.7 %collective-permute-start = (bf16[8,112,128]{2,1,0:T(8,128)(2,1)S(1)}, bf16[8,112,128]{2,1,0:T(8,128)(2,1)S(1)}, u32[]{:S(2)}, u32[]{:S(2)}) collective-permute-start(bf16[8,112,128]{2,1,0:T(8,128)(2,1)S(1)} %get-tuple-element.45), channel_id=1, source_target_pairs={{1,0},{0,1},{3,2},{2,3},{5,4},{4,5},{7,6},{6,7},{9,8},{8,9},{11,10... | collective-permute-start | bytes 688136 | tf_op jit(solution)/shard_map/ppermute | solution.py:570
  17.1 10.8 %collective-permute-start.1 = (bf16[8,112,128]{2,1,0:T(8,128)(2,1)S(1)}, bf16[8,112,128]{2,1,0:T(8,128)(2,1)S(1)}, u32[]{:S(2)}, u32[]{:S(2)}) collective-permute-start(bf16[8,112,128]{2,1,0:T(8,128)(2,1)S(1)} %get-tuple-element.44), channel_id=1, source_target_pairs={{16,0},{17,1},{18,2},{19,3},{20,4},{21,5},{22,6},{23,7},{8,24},{9,... | collective-permute-start | bytes 688136 | tf_op jit(solution)/shard_map/ppermute | solution.py:570
  18.5 9.1 %collective-permute-start.2 = (bf16[8,128]{1,0:T(8,128)(2,1)S(1)}, bf16[8,128]{1,0:T(8,128)(2,1)S(1)}, u32[]{:S(2)}, u32[]{:S(2)}) collective-permute-start(bf16[8,128]{1,0:T(8,128)(2,1)S(1)} %bitcast.9), channel_id=1, source_target_pairs={{17,0},{16,1},{19,2},{18,3},{21,4},{20,5},{23,6},{22,7},{9,24},{8,... | collective-permute-start | bytes 6152 | tf_op jit(solution)/shard_map/ppermute | solution.py:570
  30.1 6.2 %collective-permute-start.3 = (bf16[8,96,128]{2,1,0:T(8,128)(2,1)S(1)}, bf16[8,96,128]{2,1,0:T(8,128)(2,1)S(1)}, u32[]{:S(2)}, u32[]{:S(2)}) collective-permute-start(bf16[8,96,128]{2,1,0:T(8,128)(2,1)S(1)} %get-tuple-element.33), channel_id=1, source_target_pairs={{24,8},{25,9},{26,10},{27,11},{28,12},{29,13},{30,14},{31,15},{0,1... | collective-permute-start | bytes 589832 | tf_op jit(solution)/shard_map/ppermute | solution.py:570
  31.4 4.9 %collective-permute-start.4 = (bf16[8,96,128]{2,1,0:T(8,128)(2,1)S(1)}, bf16[8,96,128]{2,1,0:T(8,128)(2,1)S(1)}, u32[]{:S(2)}, u32[]{:S(2)}) collective-permute-start(bf16[8,96,128]{2,1,0:T(8,128)(2,1)S(1)} %get-tuple-element.34), channel_id=1, source_target_pairs={{1,0},{0,1},{3,2},{2,3},{5,4},{4,5},{7,6},{6,7},{9,8},{8,9},{11,10... | collective-permute-start | bytes 589832 | tf_op jit(solution)/shard_map/ppermute | solution.py:570
  31.9 3.0 %collective-permute-start.5 = (f32[8,128]{1,0:T(8,128)S(1)}, f32[8,128]{1,0:T(8,128)S(1)}, u32[]{:S(2)}, u32[]{:S(2)}) collective-permute-start(f32[8,128]{1,0:T(8,128)S(1)} %get-tuple-element.37), channel_id=1, source_target_pairs={{1,0},{0,1},{3,2},{2,3},{5,4},{4,5},{7,6},{6,7},{9,8},{8,9},{11,10... | collective-permute-start | bytes 12296 | tf_op jit(solution)/shard_map/ppermute | solution.py:570
  32.3 3.9 %collective-permute-start.6 = (f32[8,128]{1,0:T(8,128)S(1)}, f32[8,128]{1,0:T(8,128)S(1)}, u32[]{:S(2)}, u32[]{:S(2)}) collective-permute-start(f32[8,128]{1,0:T(8,128)S(1)} %get-tuple-element.38), channel_id=1, source_target_pairs={{24,8},{25,9},{26,10},{27,11},{28,12},{29,13},{30,14},{31,15},{0,1... | collective-permute-start | bytes 12296 | tf_op jit(solution)/shard_map/ppermute | solution.py:570
  33.6 2.6 %collective-permute-start.7 = (f32[8,128]{1,0:T(8,128)S(1)}, f32[8,128]{1,0:T(8,128)S(1)}, u32[]{:S(2)}, u32[]{:S(2)}) collective-permute-start(f32[8,128]{1,0:T(8,128)S(1)} %get-tuple-element.39), channel_id=1, source_target_pairs={{25,8},{24,9},{27,10},{26,11},{29,12},{28,13},{31,14},{30,15},{1,1... | collective-permute-start | bytes 12296 | tf_op jit(solution)/shard_map/ppermute | solution.py:570
  37.1 5.7 %copy-start = (bf16[48,8]{0,1:T(8,128)(2,1)S(1)}, bf16[48,8]{0,1:T(8,128)(2,1)}, u32[]{:S(2)}) copy-start(bf16[48,8]{0,1:T(8,128)(2,1)} %param.12) | copy-start | bytes 2308
  37.1 13.2 %all-to-all-start.1 = ((bf16[8,160,128]{2,1,0:T(8,128)(2,1)}), bf16[8,160,128]{2,1,0:T(8,128)(2,1)S(1)}, u32[]{:S(2)}, u32[]{:S(2)}) async-start(bf16[8,160,128]{2,1,0:T(8,128)(2,1)} %shard_map.106), calls=%async_computation.1 | async-start | bytes 655360 | tf_op jit(solution)/shard_map/all_to_all | solution.py:586

commit v4 on v3

--- a/solution.py
+++ b/solution.py
@@ -224,24 +224,26 @@
 
 def own_kernel(plan, own_ref, *refs):
     rows, heads, members, scale = plan
-    peers, outs, scratch = (refs[: members - 1], refs[members - 1 : members + 5], refs[members + 5 :])
+    others = members - 1
+    peers, stats, refs = (refs[:others], refs[others : 2 * others], refs[2 * others :])
     place = place_of(heads, members)
     for kind in (0, 1):
 
         @pl.when(place[KIND] == kind)
         def _(kind=kind):
-            own_body(plan, kind, place, own_ref, peers, outs, scratch)
-
-
-def own_body(plan, kind, place, own_ref, peers, outs, scratch):
+            own_body(plan, kind, place, own_ref, peers, stats, refs[:7], refs[7:])
+
+
+def own_body(plan, kind, place, own_ref, peers, stats, outs, scratch):
     rows, heads, members, scale = plan
-    full_1, full_2, full_acc, some_acc, value_acc, total_ref = outs
+    full_1, full_2, full_acc, some_acc, value_acc, total_ref, keep_ref = outs
     some_1, some_2 = scratch
     stat_at = 2 * rows
-    peer_stat = 0 if kind == 0 else stat_at
     blocks = [own_ref[:, stat_at : stat_at + STAT, :].astype(F32)]
-    blocks += [ref[:, peer_stat : peer_stat + STAT, :].astype(F32) for ref in peers]
-    curve, total = curves([stat_row(block, 0) for block in blocks], rows, members, place[BASE:])
+    blocks += [ref[...].astype(F32) for ref in stats]
+    gates = [stat_row(block, 0) for block in blocks]
+    curve, total = curves(gates, rows, members, place[BASE:])
+    keep_ref[...] = 1.0 / (1.0 + jnp.exp(gates[0]))
     total_ref[...] = jnp.full(total_ref.shape, total, F32)
     every = list(zip(curve, blocks))
     full_at, some_at = (full_place(place, rows, members), some_place(rows))
@@ -249,7 +251,7 @@
     if kind == 0:
         columns = extra_columns(rows, scale, every[:1], every)
         query_sources = [(own_ref, 0)]
-        key_sources = [(own_ref, keys_at)] + [(ref, STAT) for ref in peers]
+        key_sources = [(own_ref, keys_at)] + [(ref, 0) for ref in peers]
         (k_1, k_2, k_acc, k_at), (q_1, q_2, q_acc, q_at) = (
             (full_1, full_2, full_acc, full_at),
             (some_1, some_2, some_acc, some_at),
@@ -498,14 +500,14 @@
         ref[...] = suffix[src * heads : (src + 1) * heads]
 
 
-def combine_kernel(plan, dq_ref, dk_ref, dv_ref, cross, *refs):
+def combine_kernel(plan, keep_ref, dq_ref, dk_ref, dv_ref, cross, *refs):
     rows, heads, members, scale = plan
     peers, gate_refs, out_ref = (refs[: members - 1], refs[members - 1 : -1], refs[-1])
     first_kind = place_of(heads, members)[KIND] == 0
     gates = gate_refs[0][...]
     for ref in gate_refs[1:]:
         gates += ref[...]
-    gates = split3(gates)
+    gates *= keep_ref[...]
     for k in range(heads):
         far = cross[k].astype(F32)
         near = peers[0][k].astype(F32)
@@ -516,10 +518,10 @@
         out_ref[k, 0:rows, :] = (scale * (dq_ref[k] + to_queries)).astype(BF16)
         out_ref[k, rows : 2 * rows, :] = (scale * (dk_ref[k] + to_keys[0:rows])).astype(BF16)
         out_ref[k, 2 * rows : 3 * rows, :] = (dv_ref[k] + to_keys[rows:]).astype(BF16)
-        out_ref[k, 3 * rows :, :] = stack_rows([part[k : k + 1] for part in gates]).astype(BF16)
-
-
-def unpack_kernel(in_ref, keep_ref, dq_ref, dk_ref, dv_ref, gate_ref):
+        out_ref[k, 3 * rows :, :] = jnp.broadcast_to(gates[k : k + 1], (STAT, LANES)).astype(BF16)
+
+
+def unpack_kernel(in_ref, dq_ref, dk_ref, dv_ref, gate_ref):
     rows = dq_ref.shape[0]
     heads = in_ref.shape[0]
     gates = []
@@ -528,21 +530,22 @@
         dq_ref[:, cols] = in_ref[h, 0:rows, :]
         dk_ref[:, cols] = in_ref[h, rows : 2 * rows, :]
         dv_ref[:, cols] = in_ref[h, 2 * rows : 3 * rows, :]
-        gates.append(jnp.sum(in_ref[h, 3 * rows :, :].astype(F32), axis=0, keepdims=True))
-    gate_ref[...] = (jnp.concatenate(gates, axis=0)[:, 0:rows] * keep_ref[...]).astype(BF16)
+        gates.append(in_ref[h, 3 * rows :, :].astype(F32)[0:1])
+    gate_ref[...] = jnp.concatenate(gates, axis=0)[:, 0:rows].astype(BF16)
 
 
 def struct(shape, dtype=BF16):
     return jax.ShapeDtypeStruct(shape, dtype)
 
 
-def call(kernel, out_shape, inputs, scratch=(), space=VMEM, limit=40):
+def call(kernel, out_shape, inputs, scratch=(), space=VMEM, limit=40, flops=None):
     return pl.pallas_call(
         kernel,
         out_shape=out_shape,
         in_specs=[space] * len(inputs),
         out_specs=jax.tree.map(lambda _: VMEM, out_shape),
         scratch_shapes=list(scratch),
+        cost_estimate=None if flops is None else pl.CostEstimate(flops=flops, bytes_accessed=0, transcendentals=0),
         compiler_params=pltpu.CompilerParams(vmem_limit_bytes=int(limit * 1024 * 1024)),
     )(*inputs)
 
@@ -603,13 +606,13 @@
     own = exchange(packed)
     length = 2 * rows + STAT
 
-    def part(keys):
-        return lax.dynamic_slice_in_dim(own, jnp.where(keys, 2 * rows, 0), length, axis=1)
-
-    cross_send, peer_send = (part(kind == 1), part(kind == 0))
+    cross_send = lax.dynamic_slice_in_dim(own, jnp.where(kind == 1, 2 * rows, 0), length, axis=1)
+    peer_send = lax.dynamic_slice_in_dim(own, jnp.where(kind == 0, length, 0), 2 * rows, axis=1)
+    stat_send = own[:, 2 * rows : length]
     gate_send = own[:, 2 * rows]
     cross = shift(cross_send, 1, 0, working)
     peers = [shift(peer_send, 0, s, everyone) for s in range(1, members)]
+    peer_stats = [shift(stat_send, 0, s, everyone) for s in range(1, members)]
     corner = [shift(gate_send, 1, s, working) for s in range(1, members)]
 
     plan = (rows, heads, members, scale)
@@ -617,7 +620,7 @@
     value_rows = max(full_rows, 2 * own_rows)
     wide = 2 * LANES
     small = struct((heads, LANES), F32)
-    state = call(
+    *state, keep = call(
         functools.partial(own_kernel, plan),
         [
             struct((full_rows, wide)),
@@ -626,8 +629,9 @@
             struct((own_rows, wide), F32),
             struct((value_rows, LANES), F32),
             small,
+            small,
         ],
-        (own, *peers),
+        (own, *peers, *peer_stats),
         scratch=[pltpu.VMEM((own_rows, wide), BF16)] * 2,
     )
     piece = struct((heads, rows, LANES), F32)
@@ -656,12 +660,11 @@
     summed = call(
         functools.partial(combine_kernel, plan),
         struct((heads, 3 * rows + STAT, LANES)),
-        (dq, dk, dv, cross, *peers, *gates),
+        (keep, dq, dk, dv, cross, *peers, *gates),
     )
     final = exchange(summed)
-    keep = jax.nn.sigmoid(-gate_logits.T.astype(F32))
     full = struct(queries.shape)
-    dq, dk, dv, gate_grad = call(unpack_kernel, [full, full, full, struct((heads, rows))], (final, keep))
+    dq, dk, dv, gate_grad = call(unpack_kernel, [full, full, full, struct((heads, rows))], (final,))
     return dq, dk, dv, gate_grad.T
 
 

time: 51.5 us -> 49.1 us (0.953)
  blocking collectives: 0 us -> 13.6 us
  waiting for transfers between devices: 23.3 us -> 13.2 us
  starting transfers between devices: 19 us -> 13.8 us
  Pallas kernels: 7.97 us -> 7.3 us
    all_to_all x0 -> x1, blocking collectives: none -> 13.6 us  [exchange(): lax.all_to_all(array, both, split_axis=0, concat_axis=0, axis_index_group...]
    all_to_all x2 -> x1, waiting for transfers between devices: 15.6 us -> 8.15 us  [exchange(): lax.all_to_all(array, both, split_axis=0, concat_axis=0, axis_index_group...]
    all_to_all x2 -> x1, starting transfers between devices: 11.9 us -> 6.2 us  [exchange(): lax.all_to_all(array, both, split_axis=0, concat_axis=0, axis_index_group...]
    ppermute x8 -> x9, waiting for transfers between devices: 7.65 us -> 5.08 us  [shift(): return lax.ppermute(array, both, pairs)]
    pallas_call x6, Pallas kernels: 7.97 us -> 7.3 us  [call(): pl.pallas_call(kernel, out_shape=out_shape, in_specs=[space] * len(inputs...]
    ppermute x8 -> x9, starting transfers between devices: 7.15 us -> 7.63 us  [shift(): return lax.ppermute(array, both, pairs)]
  transfers between devices with their start and end apart: 10 -> 10, of which waited for: 5 -> 4; matrix products, arithmetic and copies ran while one was open for 0% -> 0% of each run, Pallas kernels for 4% -> 4%
where the time goes in v4:
time: 49.1 us; the launch traced here: 48.8 us
  starting transfers between devices  13.8 us (28%)
  blocking collectives  13.6 us (28%)
  waiting for transfers between devices  13.2 us (27%)
  Pallas kernels  7.3 us (15%)
  between operations  0.76 us (2%)
    all_to_all x1, blocking collectives, exchange(): lax.all_to_all(array, both, split_axis=0, concat_axis=0, axis_index_group...  13.6 us
    all_to_all x1, waiting for transfers between devices, exchange(): lax.all_to_all(array, both, split_axis=0, concat_axis=0, axis_index_group...  8.15 us
    ppermute x9, starting transfers between devices, shift(): return lax.ppermute(array, both, pairs)  7.63 us
    pallas_call x6, Pallas kernels, call(): pl.pallas_call(kernel, out_shape=out_shape, in_specs=[space] * len(inputs...  7.3 us
    all_to_all x1, starting transfers between devices, exchange(): lax.all_to_all(array, both, split_axis=0, concat_axis=0, axis_index_group...  6.2 us
    ppermute x9, waiting for transfers between devices, shift(): return lax.ppermute(array, both, pairs)  5.08 us
  transfers between devices with their start and end apart: 10, of which 4 were waited for; matrix products, arithmetic and copies ran while one was open for 0% of the time, Pallas kernels for 4%

profile of v4, /device:TPU:0, one launch (start us, length us, event | category | flops | bytes accessed | tf_op | source)
XLA Modules:
  0.0 48.8 jit_solution(8262011275331508713)
XLA Ops:
  0.6 2.1 %shard_map.102 = bf16[8,208,128]{2,1,0:T(8,128)(2,1)} custom-call(bf16[48,1024]{1,0:T(8,128)(2,1)} %refs_0_.1, bf16[48,1024]{1,0:T(8,128)(2,1)} %refs_1_.1, bf16[48,1024]{1,0:T(8,128)(2,1)} %refs_2_.1, bf16[48,1024]{1,0:T(8,128)(2,1)} %refs_3_.1, bf16[48,1024]{1,0:T(8,128)(2,1)} %refs_4_.1, bf16[8,48]{1,0:T(8,128)(2,1)} %bitcast.7, f32[8,48]{1,0:T(8,128)} %bitcast.6), custom_call_target="tpu_custom_call" | custom-call | tf_op jit(solution)/shard_map/pallas_call | solution.py:542
  2.7 6.2 %all-to-all-start = ((bf16[8,208,128]{2,1,0:T(8,128)(2,1)}), bf16[8,208,128]{2,1,0:T(8,128)(2,1)S(1)}, u32[]{:S(2)}, u32[]{:S(2)}) async-start(bf16[8,208,128]{2,1,0:T(8,128)(2,1)} %shard_map.102), calls=%async_computation | async-start | bytes 851968 | tf_op jit(solution)/shard_map/all_to_all | solution.py:589
  8.9 8.1 %all-to-all-done.own_ref = bf16[8,208,128]{2,1,0:T(8,128)(2,1)S(1)} async-done(((bf16[8,208,128]{2,1,0:T(8,128)(2,1)}), bf16[8,208,128]{2,1,0:T(8,128)(2,1)S(1)}, u32[]{:S(2)}, u32[]{:S(2)}) %all-to-all-start) | async-done | bytes 426016 | tf_op jit(solution)/shard_map/all_to_all | solution.py:589
  17.1 1.3 %collective-permute-start.2 = (bf16[8,112,128]{2,1,0:T(8,128)(2,1)S(1)}, bf16[8,112,128]{2,1,0:T(8,128)(2,1)S(1)}, u32[]{:S(2)}, u32[]{:S(2)}) collective-permute-start(bf16[8,112,128]{2,1,0:T(8,128)(2,1)S(1)} %constant_dynamic-slice_fusion), channel_id=1, source_target_pairs={{16,0},{17,1},{18,2},{19,3},{20,4},{21,5},{22,6},{23,7},{8,24},{9,... | collective-permute-start | bytes 688136 | tf_op jit(solution)/shard_map/ppermute | solution.py:573
  18.4 0.1 collective-permute-start
  18.5 0.5 %collective-permute-start.1 = (bf16[8,16,128]{2,1,0:T(8,128)(2,1)S(1)}, bf16[8,16,128]{2,1,0:T(8,128)(2,1)S(1)}, u32[]{:S(2)}, u32[]{:S(2)}) collective-permute-start(bf16[8,16,128]{2,1,0:T(8,128)(2,1)S(1)} %slice.8), channel_id=1, source_target_pairs={{1,0},{0,1},{3,2},{2,3},{5,4},{4,5},{7,6},{6,7},{9,8},{8,9},{11,10... | collective-permute-start | bytes 98312 | tf_op jit(solution)/shard_map/ppermute | solution.py:573
  19.0 1.3 %collective-permute-start.3 = (bf16[8,128]{1,0:T(8,128)(2,1)S(1)}, bf16[8,128]{1,0:T(8,128)(2,1)S(1)}, u32[]{:S(2)}, u32[]{:S(2)}) collective-permute-start(bf16[8,128]{1,0:T(8,128)(2,1)S(1)} %bitcast.8), channel_id=1, source_target_pairs={{17,0},{16,1},{19,2},{18,3},{21,4},{20,5},{23,6},{22,7},{9,24},{8,... | collective-permute-start | bytes 6152 | tf_op jit(solution)/shard_map/ppermute | solution.py:573
  20.3 0.0 collective-permute-done.1.refs_1_
  20.3 0.0 collective-permute-done.refs_0_
  20.3 1.9 %shard_map.103 = (bf16[768,256]{1,0:T(8,128)(2,1)S(1)}, bf16[768,256]{1,0:T(8,128)(2,1)S(1)}, f32[768,256]{1,0:T(8,128)S(1)}, f32[384,256]{1,0:T(8,128)S(1)}, f3...) custom-call(bf16[8,208,128]{2,1,0:T(8,128)(2,1)S(1)} %all-to-all-done.own_ref, ...), custom_call_target="tpu_custom_call" | custom-call | tf_op jit(solution)/shard_map/pallas_call | solution.py:542
  22.2 2.7 %collective-permute-done.3.refs_7_ = bf16[8,128]{1,0:T(8,128)(2,1)S(1)} collective-permute-done((bf16[8,128]{1,0:T(8,128)(2,1)S(1)}, bf16[8,128]{1,0:T(8,128)(2,1)S(1)}, u32[]{:S(2)}, u32[]{:S(2)}) %collective-permute-start.3) | collective-permute-done | bytes 2080 | tf_op jit(solution)/shard_map/ppermute | solution.py:573
  24.8 1.0 %collective-permute-done.2.refs_6_ = bf16[8,112,128]{2,1,0:T(8,128)(2,1)S(1)} collective-permute-done((bf16[8,112,128]{2,1,0:T(8,128)(2,1)S(1)}, bf16[8,112,128]{2,1,0:T(8,128)(2,1)S(1)}, u32[]{:S(2)}, u32[]{:S(2)}) %collective-permute-start.2) | collective-permute-done | bytes 229408 | tf_op jit(solution)/shard_map/ppermute | solution.py:573
  25.9 2.2 %shard_map.104 = (f32[8,48,128]{2,1,0:T(8,128)S(1)}, f32[8,48,128]{2,1,0:T(8,128)S(1)}, f32[8,48,128]{2,1,0:T(8,128)S(1)}, bf16[8,96,128]{2,1,0:T(8,128)(2,1)S(1...) custom-call(bf16[768,256]{1,0:T(8,128)(2,1)S(1)} %get-tuple-element.26.refs_0_, ...), custom_call_target="tpu_custom_call" | custom-call | tf_op jit(solution)/shard_map/pallas_call | solution.py:542
  28.1 1.3 %collective-permute-start.4 = (bf16[8,96,128]{2,1,0:T(8,128)(2,1)S(1)}, bf16[8,96,128]{2,1,0:T(8,128)(2,1)S(1)}, u32[]{:S(2)}, u32[]{:S(2)}) collective-permute-start(bf16[8,96,128]{2,1,0:T(8,128)(2,1)S(1)} %get-tuple-element.35), channel_id=1, source_target_pairs={{24,8},{25,9},{26,10},{27,11},{28,12},{29,13},{30,14},{31,15},{0,1... | collective-permute-start | bytes 589832 | tf_op jit(solution)/shard_map/ppermute | solution.py:573
  29.4 0.2 collective-permute-start.5
  29.6 0.3 shard_map.105
  29.9 0.4 collective-permute-start.6
  30.3 1.3 %collective-permute-start.7 = (f32[8,128]{1,0:T(8,128)S(1)}, f32[8,128]{1,0:T(8,128)S(1)}, u32[]{:S(2)}, u32[]{:S(2)}) collective-permute-start(f32[8,128]{1,0:T(8,128)S(1)} %get-tuple-element.40), channel_id=1, source_target_pairs={{24,8},{25,9},{26,10},{27,11},{28,12},{29,13},{30,14},{31,15},{0,1... | collective-permute-start | bytes 12296 | tf_op jit(solution)/shard_map/ppermute | solution.py:573
  31.6 1.3 %collective-permute-start.8 = (f32[8,128]{1,0:T(8,128)S(1)}, f32[8,128]{1,0:T(8,128)S(1)}, u32[]{:S(2)}, u32[]{:S(2)}) collective-permute-start(f32[8,128]{1,0:T(8,128)S(1)} %get-tuple-element.41), channel_id=1, source_target_pairs={{25,8},{24,9},{27,10},{26,11},{29,12},{28,13},{31,14},{30,15},{1,1... | collective-permute-start | bytes 12296 | tf_op jit(solution)/shard_map/ppermute | solution.py:573
  32.9 0.0 collective-permute-done.6.refs_2_
  32.9 1.3 %collective-permute-done.7.refs_3_ = f32[8,128]{1,0:T(8,128)S(1)} collective-permute-done((f32[8,128]{1,0:T(8,128)S(1)}, f32[8,128]{1,0:T(8,128)S(1)}, u32[]{:S(2)}, u32[]{:S(2)}) %collective-permute-start.7) | collective-permute-done | bytes 4128 | tf_op jit(solution)/shard_map/ppermute | solution.py:573
  34.2 0.0 collective-permute-done.8.refs_4_
  34.3 0.0 collective-permute-done.4.cross
  34.3 0.0 collective-permute-done.5.refs_0_
  34.3 0.1 shard_map.106
  34.4 13.6 %all_to_all.10.in_ref = bf16[8,160,128]{2,1,0:T(8,128)(2,1)S(1)} all-to-all(bf16[8,160,128]{2,1,0:T(8,128)(2,1)S(1)} %shard_map.106), channel_id=1, replica_groups={{0,2,4,6,8,10,12,14},{1,3,5,7,9,11,13,15},{16,18,20,22,24,26,28,30},{17..., dimensions={0} | all-to-all | bytes 655360 | tf_op jit(solution)/shard_map/all_to_all | solution.py:589
  48.0 0.8 %shard_map.107 = (bf16[48,1024]{1,0:T(8,128)(2,1)}, bf16[48,1024]{1,0:T(8,128)(2,1)}, bf16[48,1024]{1,0:T(8,128)(2,1)}, bf16[8,48]{1,0:T(8,128)(2,1)}) custom-call(bf16[8,160,128]{2,1,0:T(8,128)(2,1)S(1)} %all_to_all.10.in_ref), custom_call_target="tpu_custom_call" | custom-call | tf_op jit(solution)/shard_map/pallas_call | solution.py:542
  (5 shorter events, 0.1 us)
Async XLA Ops:
  2.7 14.3 %all-to-all-start = ((bf16[8,208,128]{2,1,0:T(8,128)(2,1)}), bf16[8,208,128]{2,1,0:T(8,128)(2,1)S(1)}, u32[]{:S(2)}, u32[]{:S(2)}) async-start(bf16[8,208,128]{2,1,0:T(8,128)(2,1)} %shard_map.102), calls=%async_computation | async-start | bytes 851968 | tf_op jit(solution)/shard_map/all_to_all | solution.py:589
  17.1 8.8 %collective-permute-start.2 = (bf16[8,112,128]{2,1,0:T(8,128)(2,1)S(1)}, bf16[8,112,128]{2,1,0:T(8,128)(2,1)S(1)}, u32[]{:S(2)}, u32[]{:S(2)}) collective-permute-start(bf16[8,112,128]{2,1,0:T(8,128)(2,1)S(1)} %constant_dynamic-slice_fusion), channel_id=1, source_target_pairs={{16,0},{17,1},{18,2},{19,3},{20,4},{21,5},{22,6},{23,7},{8,24},{9,... | collective-permute-start | bytes 688136 | tf_op jit(solution)/shard_map/ppermute | solution.py:573
  18.4 1.9 %collective-permute-start = (bf16[8,96,128]{2,1,0:T(8,128)(2,1)S(1)}, bf16[8,96,128]{2,1,0:T(8,128)(2,1)S(1)}, u32[]{:S(2)}, u32[]{:S(2)}) collective-permute-start(bf16[8,96,128]{2,1,0:T(8,128)(2,1)S(1)} %constant_dynamic-slice_fusion.1), channel_id=1, source_target_pairs={{1,0},{0,1},{3,2},{2,3},{5,4},{4,5},{7,6},{6,7},{9,8},{8,9},{11,10... | collective-permute-start | bytes 589832 | tf_op jit(solution)/shard_map/ppermute | solution.py:573
  18.5 1.8 %collective-permute-start.1 = (bf16[8,16,128]{2,1,0:T(8,128)(2,1)S(1)}, bf16[8,16,128]{2,1,0:T(8,128)(2,1)S(1)}, u32[]{:S(2)}, u32[]{:S(2)}) collective-permute-start(bf16[8,16,128]{2,1,0:T(8,128)(2,1)S(1)} %slice.8), channel_id=1, source_target_pairs={{1,0},{0,1},{3,2},{2,3},{5,4},{4,5},{7,6},{6,7},{9,8},{8,9},{11,10... | collective-permute-start | bytes 98312 | tf_op jit(solution)/shard_map/ppermute | solution.py:573
  19.0 5.9 %collective-permute-start.3 = (bf16[8,128]{1,0:T(8,128)(2,1)S(1)}, bf16[8,128]{1,0:T(8,128)(2,1)S(1)}, u32[]{:S(2)}, u32[]{:S(2)}) collective-permute-start(bf16[8,128]{1,0:T(8,128)(2,1)S(1)} %bitcast.8), channel_id=1, source_target_pairs={{17,0},{16,1},{19,2},{18,3},{21,4},{20,5},{23,6},{22,7},{9,24},{8,... | collective-permute-start | bytes 6152 | tf_op jit(solution)/shard_map/ppermute | solution.py:573
  28.1 6.2 %collective-permute-start.4 = (bf16[8,96,128]{2,1,0:T(8,128)(2,1)S(1)}, bf16[8,96,128]{2,1,0:T(8,128)(2,1)S(1)}, u32[]{:S(2)}, u32[]{:S(2)}) collective-permute-start(bf16[8,96,128]{2,1,0:T(8,128)(2,1)S(1)} %get-tuple-element.35), channel_id=1, source_target_pairs={{24,8},{25,9},{26,10},{27,11},{28,12},{29,13},{30,14},{31,15},{0,1... | collective-permute-start | bytes 589832 | tf_op jit(solution)/shard_map/ppermute | solution.py:573
  29.4 4.9 %collective-permute-start.5 = (bf16[8,96,128]{2,1,0:T(8,128)(2,1)S(1)}, bf16[8,96,128]{2,1,0:T(8,128)(2,1)S(1)}, u32[]{:S(2)}, u32[]{:S(2)}) collective-permute-start(bf16[8,96,128]{2,1,0:T(8,128)(2,1)S(1)} %get-tuple-element.36), channel_id=1, source_target_pairs={{1,0},{0,1},{3,2},{2,3},{5,4},{4,5},{7,6},{6,7},{9,8},{8,9},{11,10... | collective-permute-start | bytes 589832 | tf_op jit(solution)/shard_map/ppermute | solution.py:573
  29.9 3.0 %collective-permute-start.6 = (f32[8,128]{1,0:T(8,128)S(1)}, f32[8,128]{1,0:T(8,128)S(1)}, u32[]{:S(2)}, u32[]{:S(2)}) collective-permute-start(f32[8,128]{1,0:T(8,128)S(1)} %get-tuple-element.39), channel_id=1, source_target_pairs={{1,0},{0,1},{3,2},{2,3},{5,4},{4,5},{7,6},{6,7},{9,8},{8,9},{11,10... | collective-permute-start | bytes 12296 | tf_op jit(solution)/shard_map/ppermute | solution.py:573
  30.3 3.9 %collective-permute-start.7 = (f32[8,128]{1,0:T(8,128)S(1)}, f32[8,128]{1,0:T(8,128)S(1)}, u32[]{:S(2)}, u32[]{:S(2)}) collective-permute-start(f32[8,128]{1,0:T(8,128)S(1)} %get-tuple-element.40), channel_id=1, source_target_pairs={{24,8},{25,9},{26,10},{27,11},{28,12},{29,13},{30,14},{31,15},{0,1... | collective-permute-start | bytes 12296 | tf_op jit(solution)/shard_map/ppermute | solution.py:573
  31.6 2.7 %collective-permute-start.8 = (f32[8,128]{1,0:T(8,128)S(1)}, f32[8,128]{1,0:T(8,128)S(1)}, u32[]{:S(2)}, u32[]{:S(2)}) collective-permute-start(f32[8,128]{1,0:T(8,128)S(1)} %get-tuple-element.41), channel_id=1, source_target_pairs={{25,8},{24,9},{27,10},{26,11},{29,12},{28,13},{31,14},{30,15},{1,1... | collective-permute-start | bytes 12296 | tf_op jit(solution)/shard_map/ppermute | solution.py:573
